TPU v7x, 32 devices: a whole 2x2x4 slice. The times are simulated.
32 devices in a mesh: blk: 8 (over z, x), head: 4 (over y, core).
Axes of the slice: x: 2, y: 2, z: 4, core: 2. Of those that a mesh axis runs over, the one named last changes fastest.
Arguments:
- tokens: bfloat16 [6144, 2048], P(('blk', 'head')), may hold values from -6 to 6
- attn_gain: bfloat16 [2048], P('blk'), may hold values from 0.25 to 1.75
- query_weight: bfloat16 [2048, 2048], P('blk', 'head'), may hold values from -0.125 to 0.125
- key_matrix: bfloat16 [2048, 1024], P('blk', 'head'), may hold values from -0.125 to 0.125
- value_matrix: bfloat16 [2048, 1024], P('blk', 'head'), may hold values from -0.125 to 0.125
- out_weight: bfloat16 [2048, 2048], P('head', 'blk'), may hold values from -3 to 3
- mlp_gain: bfloat16 [2048], P('blk'), may hold values from 0.25 to 1.75
- gate_weight: bfloat16 [2048, 8192], P('blk', 'head'), may hold values from -0.125 to 0.125
- up_weight: bfloat16 [2048, 8192], P('blk', 'head'), may hold values from -0.125 to 0.125
- down_weight: bfloat16 [8192, 2048], P('head', 'blk'), may hold values from -0.0625 to 0.0625
- segment_ids: int32 [6144], replicated, may hold values from 0 to 7, as said below
- positions: int32 [6144], replicated, may hold values from 0 to 8190, as said below
- cotangent: bfloat16 [6144, 2048], P(('blk', 'head')), may hold values from -6 to 6
Outputs:
- layer_out: bfloat16 [6144, 2048], P(('blk', 'head'))
- tokens_grad: float32 [6144, 2048], P(('blk', 'head'))
- attn_gain_grad: float32 [2048], P('blk')
- query_grad: float32 [2048, 2048], P('blk', 'head')
- key_grad: float32 [2048, 1024], P('blk', 'head')
- value_grad: float32 [2048, 1024], P('blk', 'head')
- out_grad: float32 [2048, 2048], P('head', 'blk')
- mlp_gain_grad: float32 [2048], P('blk')
- gate_grad: float32 [2048, 8192], P('blk', 'head')
- up_grad: float32 [2048, 8192], P('blk', 'head')
- down_grad: float32 [8192, 2048], P('head', 'blk')
Inputs may be any that keep to these rules, and one draw needn't show every extreme that they name: `segment_ids`: document number of each token of the stream, never falling along it; a document holds 1 to 4096 tokens and one holds exactly 4096; the first document is numbered 0 and the last one carries the largest number. Within a document the positions rise by one from token to token; the first token of the stream has position 0.
All inputs are finite; a program needn't handle non-finite values.
Results may differ from a plain program's by a relative error of at most 0.02.
Values may be sent and summed in bfloat16 or wider, within the bound.
No kernel may reach another device: no remote copies, remote signals or barrier semaphores. Data moves between devices by JAX's collectives and lax.ppermute only.
A program may use at most 320 MiB of HBM per device.

v0:
```python
import math

import jax
import jax.numpy as jnp
from jax import lax
from jax.sharding import PartitionSpec as P

QUERY_HEADS_ALL = 8
KEY_VALUE_HEADS = 4
HEAD_WIDTH = 256
SEQ = 4096


EPSILON = 1e-06
THETA_BASE = 1000042.0
MASKED = -1e30


def passed_along(block, axis, distance):
    devices = range(lax.axis_size(axis))
    route = [(i - distance, i) for i in devices if i - distance in devices]
    return lax.ppermute(block, axis, route)


def norm_rows(values, gain_vec):
    inverse = lax.rsqrt(jnp.mean(values * values, axis=-1, keepdims=True) + EPSILON)
    return (values * inverse * gain_vec, inverse)


def norm_back(values, gain_vec, inverse, upstream):
    weighted = upstream * gain_vec
    inner_mean = jnp.mean(weighted * values, axis=-1, keepdims=True)
    grad_values = inverse * weighted - values * (inverse * inverse * inverse) * inner_mean
    grad_gain = jnp.sum(upstream * values * inverse, axis=0)
    return (grad_values, grad_gain)


def apply_rotary(values, token_pos, direction):
    half_size = values.shape[-1] // 2
    frequency = THETA_BASE ** (-2.0 * jnp.arange(half_size, dtype=jnp.float32) / values.shape[-1])
    angles = token_pos.astype(jnp.float32)[:, None] * frequency[None, :]
    cosine = jnp.cos(angles)[:, None, :]
    sine_part = jnp.sin(angles)[:, None, :] * direction
    first_half = values[..., :half_size]
    second_half = values[..., half_size:]
    return jnp.concatenate(
        [
            first_half * cosine - second_half * sine_part,
            second_half * cosine + first_half * sine_part,
        ],
        axis=-1,
    )


def simple_product(matrix_a, matrix_b):
    return jnp.dot(matrix_a, matrix_b, preferred_element_type=jnp.float32)


def outer_sum(matrix_a, matrix_b):
    return lax.dot_general(
        matrix_a, matrix_b, (((0,), (0,)), ((), ())), preferred_element_type=jnp.float32
    )


def times_rows(matrix_a, matrix_b):
    return lax.dot_general(
        matrix_a, matrix_b, (((1,), (1,)), ((), ())), preferred_element_type=jnp.float32
    )


def gather_rows(matrix):
    return lax.all_gather(matrix, "head", axis=0, tiled=True)


def rows_sum(term_fn, row_count):
    return lax.psum_scatter(
        term_fn(jnp.int32(0), row_count * lax.axis_size("head")).astype(jnp.bfloat16),
        "head",
        scatter_dimension=0,
        tiled=True,
    ).astype(jnp.float32)


def block_mask(segment_ids, group_seg, block_index, offset, group_rows):
    key_block = block_index - offset
    key_seg = lax.dynamic_slice_in_dim(
        segment_ids, jnp.maximum(key_block, 0) * group_rows, group_rows, 0
    )
    allowed = (group_seg[:, None] == key_seg[None, :]) & (key_block >= 0)
    if offset == 0:
        local_index = jnp.arange(group_rows, dtype=jnp.int32)
        allowed = allowed & (local_index[None, :] <= local_index[:, None])
    return allowed


def split_pair(packed, key_value_heads, head_width):
    width = key_value_heads * head_width
    key_part = packed[:, :width].reshape(packed.shape[0], key_value_heads, head_width)
    value_part = packed[:, width:].reshape(packed.shape[0], key_value_heads, head_width)
    return (key_part, value_part)


def block_scores(grouped, key_part, allowed):
    score_scale = 1.0 / math.sqrt(grouped.shape[-1])
    raw_scores = (
        jnp.einsum("qgrd,kgd->grqk", grouped, key_part, preferred_element_type=jnp.float32)
        * score_scale
    )
    return jnp.where(allowed[None, None], raw_scores, MASKED)


def tally(operands):
    run_max, run_total, grouped, key_part, allowed = operands
    scores = block_scores(grouped, key_part, allowed)
    new_max = jnp.maximum(run_max, jnp.max(scores, axis=-1))
    new_total = run_total * jnp.exp(run_max - new_max) + jnp.sum(
        jnp.exp(scores - new_max[..., None]), axis=-1
    )
    return (new_max, new_total)


def accumulate(operands):
    out_sum, log_total, grouped, key_part, value_part, allowed = operands
    scores = block_scores(grouped, key_part, allowed)
    prob_low = jnp.exp(scores - log_total[..., None]).astype(jnp.bfloat16)
    return out_sum + jnp.einsum(
        "grqk,kgd->qgrd", prob_low, value_part, preferred_element_type=jnp.float32
    )


def gradients_block(operands):
    query_grad_sum, grouped, key_part, value_part, allowed, log_total, attn_grad, row_delta = (
        operands
    )
    score_scale = 1.0 / math.sqrt(grouped.shape[-1])
    scores = block_scores(grouped, key_part, allowed)
    softmax_out = jnp.exp(scores - log_total[..., None])
    prob_grad = jnp.einsum(
        "qgrd,kgd->grqk", attn_grad, value_part, preferred_element_type=jnp.float32
    )
    score_grad = (softmax_out * (prob_grad - row_delta[..., None])).astype(jnp.bfloat16)
    query_grad_sum = (
        query_grad_sum
        + jnp.einsum("grqk,kgd->qgrd", score_grad, key_part, preferred_element_type=jnp.float32)
        * score_scale
    )
    key_grad = (
        jnp.einsum("grqk,qgrd->kgd", score_grad, grouped, preferred_element_type=jnp.float32)
        * score_scale
    )
    value_grad = jnp.einsum(
        "grqk,qgrd->kgd",
        softmax_out.astype(jnp.bfloat16),
        attn_grad,
        preferred_element_type=jnp.float32,
    )
    key_rows = key_part.shape[0]
    pair_grad = jnp.concatenate(
        [key_grad.reshape(key_rows, -1), value_grad.reshape(key_rows, -1)], axis=-1
    )
    return (query_grad_sum, pair_grad)


def local(
    tokens,
    attn_gain,
    query_weight,
    key_matrix,
    value_matrix,
    out_weight,
    mlp_gain,
    gate_weight,
    up_weight,
    down_weight,
    segment_ids,
    positions,
    cotangent,
):
    count_of_heads = lax.axis_size("head")
    block_index = lax.axis_index("blk")
    head_index = lax.axis_index("head")
    rows_of_tokens = tokens.shape[0]
    group_rows = rows_of_tokens * count_of_heads
    cycle_steps = (SEQ + group_rows - 2) // group_rows
    head_width = HEAD_WIDTH
    query_heads = QUERY_HEADS_ALL // count_of_heads
    key_value_heads = KEY_VALUE_HEADS // count_of_heads
    group_size = query_heads // key_value_heads
    pairwise_width = key_value_heads * head_width
    own_start = (block_index * count_of_heads + head_index) * rows_of_tokens
    group_start = block_index * group_rows
    own_pos = lax.dynamic_slice_in_dim(positions, own_start, rows_of_tokens, 0)
    group_pos = lax.dynamic_slice_in_dim(positions, group_start, group_rows, 0)
    group_seg = lax.dynamic_slice_in_dim(segment_ids, group_start, group_rows, 0)
    gathered = (
        lax.all_gather(attn_gain, "blk", axis=0, tiled=True),
        lax.all_gather(query_weight, "blk", axis=0, tiled=True),
        lax.all_gather(key_matrix, "blk", axis=0, tiled=True),
        lax.all_gather(value_matrix, "blk", axis=0, tiled=True),
        lax.all_gather(out_weight, "blk", axis=1, tiled=True),
        lax.all_gather(mlp_gain, "blk", axis=0, tiled=True),
        lax.all_gather(gate_weight, "blk", axis=0, tiled=True),
        lax.all_gather(up_weight, "blk", axis=0, tiled=True),
        lax.all_gather(down_weight, "blk", axis=1, tiled=True),
    )
    gain_one = gathered[0].astype(jnp.float32)
    query_shard = gathered[1]
    key_shard = gathered[2]
    value_shard = gathered[3]
    out_shard = gathered[4]
    gain_two = gathered[5].astype(jnp.float32)
    gate_shard = gathered[6]
    up_shard = gathered[7]
    down_shard = gathered[8]
    source = tokens.astype(jnp.float32)
    normed_full, inverse_one = norm_rows(source, gain_one)
    normalized_input = normed_full.astype(jnp.bfloat16)
    query_full, key_complete, value_full, out_full = (
        lax.all_gather(query_shard, "head", axis=1, tiled=True),
        lax.all_gather(key_shard, "head", axis=1, tiled=True),
        lax.all_gather(value_shard, "head", axis=1, tiled=True),
        lax.all_gather(out_shard, "head", axis=0, tiled=True),
    )
    query_linear = simple_product(normalized_input, query_full).reshape(
        rows_of_tokens, QUERY_HEADS_ALL, head_width
    )
    key_linear = simple_product(normalized_input, key_complete).reshape(
        rows_of_tokens, KEY_VALUE_HEADS, head_width
    )
    value_linear = simple_product(normalized_input, value_full).astype(jnp.bfloat16)
    query_rot = (
        apply_rotary(query_linear, own_pos, 1.0)
        .astype(jnp.bfloat16)
        .reshape(rows_of_tokens, count_of_heads, query_heads * head_width)
    )
    key_rot = apply_rotary(key_linear, own_pos, 1.0).astype(jnp.bfloat16)
    pair_tok = jnp.concatenate(
        [key_rot, value_linear.reshape(rows_of_tokens, count_of_heads, pairwise_width)], axis=-1
    )
    query_grp, pair_grp = (
        lax.all_to_all(query_rot, "head", split_axis=1, concat_axis=0, tiled=True),
        lax.all_to_all(pair_tok, "head", split_axis=1, concat_axis=0, tiled=True),
    )
    query_rows = query_grp.reshape(group_rows, query_heads * head_width)
    pair_now = pair_grp.reshape(group_rows, 2 * pairwise_width)
    kept_pairs = [pair_now]
    for offset in range(cycle_steps):
        pair_now = passed_along(pair_now, "blk", 1)
        kept_pairs.append(pair_now)
    block_masks = [
        block_mask(segment_ids, group_seg, block_index, offset, group_rows)
        for offset in range(cycle_steps + 1)
    ]
    grouped = query_rows.reshape(group_rows, key_value_heads, group_size, head_width)
    run_max = jnp.full((key_value_heads, group_size, group_rows), MASKED, jnp.float32)
    run_total = jnp.zeros((key_value_heads, group_size, group_rows), jnp.float32)
    for offset in range(cycle_steps + 1):
        key_part, value_part = split_pair(kept_pairs[offset], key_value_heads, head_width)
        run_max, run_total = tally((run_max, run_total, grouped, key_part, block_masks[offset]))
    log_total = run_max + jnp.log(run_total)
    out_sum = jnp.zeros((group_rows, key_value_heads, group_size, head_width), jnp.float32)
    for offset in range(cycle_steps + 1):
        key_part, value_part = split_pair(kept_pairs[offset], key_value_heads, head_width)
        out_sum = accumulate(
            (out_sum, log_total, grouped, key_part, value_part, block_masks[offset])
        )
    attn_low = out_sum.reshape(group_rows, query_heads * head_width).astype(jnp.bfloat16)
    attn_tok = lax.all_to_all(
        attn_low.reshape(group_rows, 1, query_heads * head_width),
        "head",
        split_axis=0,
        concat_axis=1,
        tiled=True,
    ).reshape(rows_of_tokens, QUERY_HEADS_ALL * head_width)
    branch = simple_product(attn_tok, out_full)
    residual = source + branch
    normed_two_full, inverse_two = norm_rows(residual, gain_two)
    normed_two = normed_two_full.astype(jnp.bfloat16)
    normed_two_all = gather_rows(normed_two)
    gate_lin = simple_product(normed_two_all, gate_shard)
    up_lin = simple_product(normed_two_all, up_shard)
    sigmoid_gate = jax.nn.sigmoid(gate_lin)
    silu_gate = gate_lin * sigmoid_gate
    hidden = (silu_gate * up_lin).astype(jnp.bfloat16)

    def down_rows(row_start, row_count):
        return simple_product(hidden, down_shard)

    layer_out = (residual + rows_sum(down_rows, rows_of_tokens)).astype(jnp.bfloat16)
    cotangent_all = gather_rows(cotangent)
    hidden_grad = times_rows(cotangent_all, down_shard)
    down_grad = outer_sum(hidden, cotangent_all)
    gate_act_grad = (
        hidden_grad * up_lin * sigmoid_gate * (1.0 + gate_lin * (1.0 - sigmoid_gate))
    ).astype(jnp.bfloat16)
    up_act_grad = (hidden_grad * silu_gate).astype(jnp.bfloat16)
    gate_grad = outer_sum(normed_two_all, gate_act_grad)
    up_grad = outer_sum(normed_two_all, up_act_grad)

    def mlp_back_rows(row_start, row_count):
        return times_rows(gate_act_grad, gate_shard) + times_rows(up_act_grad, up_shard)

    normed_two_grad = rows_sum(mlp_back_rows, rows_of_tokens)
    residual_norm_grad, gain_two_grad = norm_back(residual, gain_two, inverse_two, normed_two_grad)
    residual_grad = cotangent.astype(jnp.float32) + residual_norm_grad
    branch_grad = residual_grad.astype(jnp.bfloat16)
    out_grad = outer_sum(attn_tok, branch_grad)
    attn_grad_tok = (
        times_rows(branch_grad, out_full)
        .astype(jnp.bfloat16)
        .reshape(rows_of_tokens, count_of_heads, query_heads * head_width)
    )
    attn_grad = lax.all_to_all(
        attn_grad_tok, "head", split_axis=1, concat_axis=0, tiled=True
    ).reshape(group_rows, query_heads * head_width)
    attn_grad_grp = attn_grad.reshape(group_rows, key_value_heads, group_size, head_width)
    row_delta = jnp.einsum("qgrd,qgrd->grq", attn_grad_grp.astype(jnp.float32), out_sum)
    query_grad_sum = jnp.zeros((group_rows, key_value_heads, group_size, head_width), jnp.float32)
    carried = None
    for offset in reversed(range(cycle_steps + 1)):
        key_part, value_part = split_pair(kept_pairs[offset], key_value_heads, head_width)
        query_grad_sum, pair_grad = gradients_block(
            (
                query_grad_sum,
                grouped,
                key_part,
                value_part,
                block_masks[offset],
                log_total,
                attn_grad_grp,
                row_delta,
            )
        )
        if offset == cycle_steps:
            carried = pair_grad
        else:
            carried = (
                passed_along(carried.astype(jnp.bfloat16), "blk", -1).astype(carried.dtype)
                + pair_grad
            )
    query_lin_grad = (
        apply_rotary(query_grad_sum.reshape(group_rows, query_heads, head_width), group_pos, -1.0)
        .astype(jnp.bfloat16)
        .reshape(group_rows, query_heads * head_width)
    )
    key_lin_grad = (
        apply_rotary(
            carried[:, :pairwise_width].reshape(group_rows, key_value_heads, head_width),
            group_pos,
            -1.0,
        )
        .astype(jnp.bfloat16)
        .reshape(group_rows, pairwise_width)
    )
    value_lin_grad = carried[:, pairwise_width:].astype(jnp.bfloat16)
    send_query = query_lin_grad.reshape(group_rows, 1, query_heads * head_width)
    send_pair = jnp.concatenate([key_lin_grad, value_lin_grad], axis=-1).reshape(
        group_rows, 1, 2 * pairwise_width
    )
    query_back, pairwise_backward = (
        lax.all_to_all(send_query, "head", split_axis=0, concat_axis=1, tiled=True),
        lax.all_to_all(send_pair, "head", split_axis=0, concat_axis=1, tiled=True),
    )
    query_tok_grad = query_back.reshape(rows_of_tokens, QUERY_HEADS_ALL * head_width)
    key_token_gradient = pairwise_backward[:, :, :pairwise_width].reshape(
        rows_of_tokens, KEY_VALUE_HEADS * head_width
    )
    value_token_gradient = pairwise_backward[:, :, pairwise_width:].reshape(
        rows_of_tokens, KEY_VALUE_HEADS * head_width
    )
    normed_grad = (
        times_rows(query_tok_grad, query_full)
        + times_rows(key_token_gradient, key_complete)
        + times_rows(value_token_gradient, value_full)
    )
    query_grad, key_grad, value_grad, out_grad = (
        lax.psum_scatter(
            outer_sum(normalized_input, query_tok_grad).astype(jnp.bfloat16),
            "head",
            scatter_dimension=1,
            tiled=True,
        ).astype(jnp.float32),
        lax.psum_scatter(
            outer_sum(normalized_input, key_token_gradient).astype(jnp.bfloat16),
            "head",
            scatter_dimension=1,
            tiled=True,
        ).astype(jnp.float32),
        lax.psum_scatter(
            outer_sum(normalized_input, value_token_gradient).astype(jnp.bfloat16),
            "head",
            scatter_dimension=1,
            tiled=True,
        ).astype(jnp.float32),
        lax.psum_scatter(
            out_grad.astype(jnp.bfloat16), "head", scatter_dimension=0, tiled=True
        ).astype(jnp.float32),
    )
    source_grad, gain_one_grad = norm_back(source, gain_one, inverse_one, normed_grad)
    tokens_grad = residual_grad + source_grad
    gain_one_grad, gain_two_grad = lax.psum((gain_one_grad, gain_two_grad), "head")
    summed = (
        lax.psum_scatter(
            gain_one_grad.astype(jnp.bfloat16), "blk", scatter_dimension=0, tiled=True
        ).astype(jnp.float32),
        lax.psum_scatter(
            query_grad.astype(jnp.bfloat16), "blk", scatter_dimension=0, tiled=True
        ).astype(jnp.float32),
        lax.psum_scatter(
            key_grad.astype(jnp.bfloat16), "blk", scatter_dimension=0, tiled=True
        ).astype(jnp.float32),
        lax.psum_scatter(
            value_grad.astype(jnp.bfloat16), "blk", scatter_dimension=0, tiled=True
        ).astype(jnp.float32),
        lax.psum_scatter(
            out_grad.astype(jnp.bfloat16), "blk", scatter_dimension=1, tiled=True
        ).astype(jnp.float32),
        lax.psum_scatter(
            gain_two_grad.astype(jnp.bfloat16), "blk", scatter_dimension=0, tiled=True
        ).astype(jnp.float32),
        lax.psum_scatter(
            gate_grad.astype(jnp.bfloat16), "blk", scatter_dimension=0, tiled=True
        ).astype(jnp.float32),
        lax.psum_scatter(
            up_grad.astype(jnp.bfloat16), "blk", scatter_dimension=0, tiled=True
        ).astype(jnp.float32),
        lax.psum_scatter(
            down_grad.astype(jnp.bfloat16), "blk", scatter_dimension=1, tiled=True
        ).astype(jnp.float32),
    )
    return (
        layer_out,
        tokens_grad,
        summed[0],
        summed[1],
        summed[2],
        summed[3],
        summed[4],
        summed[5],
        summed[6],
        summed[7],
        summed[8],
    )


def solution(mesh):
    return jax.shard_map(
        local,
        mesh=mesh,
        in_specs=(
            P(("blk", "head"), None),
            P("blk"),
            P("blk", "head"),
            P("blk", "head"),
            P("blk", "head"),
            P("head", "blk"),
            P("blk"),
            P("blk", "head"),
            P("blk", "head"),
            P("head", "blk"),
            P(),
            P(),
            P(("blk", "head"), None),
        ),
        out_specs=(
            P(("blk", "head"), None),
            P(("blk", "head"), None),
            P("blk"),
            P("blk", "head"),
            P("blk", "head"),
            P("blk", "head"),
            P("head", "blk"),
            P("blk"),
            P("blk", "head"),
            P("blk", "head"),
            P("head", "blk"),
        ),
        check_vma=False,
    )
```

profile of v0, /device:TPU:0, one launch (start us, length us, event | category | flops | bytes accessed | tf_op | source)
XLA Modules:
  0.0 2153.4 jit_solution(11954974877499144991)
XLA Ops:
  10.0 43.0 %all-gather.16.cloned.1.call-done = bf16[2048,256]{1,0:T(8,128)(2,1)} async-done(((bf16[256,256]{1,0:T(8,128)(2,1)}), bf16[2048,256]{1,0:T(8,128)(2,1)}) %all-gather.16.cloned.1.call-update) | async-done | bytes 1048592 | tf_op jit(solution)/shard_map/all_gather | solution.py:198
  53.1 41.0 %all-gather.20.cloned.1.call-done = bf16[2048,256]{1,0:T(8,128)(2,1)} async-done(((bf16[256,256]{1,0:T(8,128)(2,1)}), bf16[2048,256]{1,0:T(8,128)(2,1)}) %all-gather.20.cloned.1.call-update) | async-done | bytes 1048592 | tf_op jit(solution)/shard_map/all_gather | solution.py:199
  94.2 50.1 %all-gather.24.cloned.1.call-done = bf16[2048,512]{1,0:T(8,128)(2,1)} async-done(((bf16[256,512]{1,0:T(8,128)(2,1)}), bf16[2048,512]{1,0:T(8,128)(2,1)}) %all-gather.24.cloned.1.call-update) | async-done | bytes 2097168 | tf_op jit(solution)/shard_map/all_gather | solution.py:197
  144.4 51.4 %all-gather.28.cloned.1.call-done = bf16[512,2048]{1,0:T(8,128)(2,1)} async-done(((bf16[512,256]{1,0:T(8,128)(2,1)}), bf16[512,2048]{1,0:T(8,128)(2,1)}) %all-gather.28.cloned.1.call-update) | async-done | bytes 2097168 | tf_op jit(solution)/shard_map/all_gather | solution.py:200
  195.9 17.7 all-gather
  234.0 32.9 %all-gather.22.cloned.1.call-done = bf16[2048,1024]{1,0:T(8,128)(2,1)} async-done(((bf16[2048,256]{1,0:T(8,128)(2,1)}), bf16[2048,1024]{1,0:T(8,128)(2,1)}) %all-gather.22.cloned.1.call-update) | async-done | bytes 4194320 | tf_op jit(solution)/shard_map/all_gather | solution.py:221
  270.5 18.9 all_to_all.93
  293.8 16.1 collective-permute-done
  314.2 15.2 collective-permute-done.1
  450.0 19.4 all-gather.1
  480.1 45.2 %all-gather.34.cloned.1.call-done = bf16[2048,2048]{1,0:T(8,128)(2,1)} async-done(((bf16[256,2048]{1,0:T(8,128)(2,1)}), bf16[2048,2048]{1,0:T(8,128)(2,1)}) %all-gather.34.cloned.1.call-update) | async-done | bytes 8388624 | tf_op jit(solution)/shard_map/all_gather | solution.py:202
  525.3 28.8 %all-gather.32.cloned.1.call-done = bf16[768,2048]{1,0:T(8,128)(2,1)} async-done(((bf16[192,2048]{1,0:T(8,128)(2,1)}), bf16[768,2048]{1,0:T(8,128)(2,1)}) %all-gather.32.cloned.1.call-update) | async-done | bytes 3145744 | tf_op jit(solution)/shard_map/all_gather | solution.py:72
  565.8 115.4 %all-gather.36.cloned.1.call-done = bf16[2048,2048]{1,0:T(8,128)(2,1)} async-done(((bf16[256,2048]{1,0:T(8,128)(2,1)}), bf16[2048,2048]{1,0:T(8,128)(2,1)}) %all-gather.36.cloned.1.call-update) | async-done | bytes 8388624 | tf_op jit(solution)/shard_map/all_gather | solution.py:203
  693.0 16.3 all-gather.40.cloned.1.call-done
  709.3 127.5 %all-gather.38.cloned.1.call-done = bf16[2048,2048]{1,0:T(8,128)(2,1)} async-done(((bf16[2048,256]{1,0:T(8,128)(2,1)}), bf16[2048,2048]{1,0:T(8,128)(2,1)}) %all-gather.38.cloned.1.call-update) | async-done | bytes 8388624 | tf_op jit(solution)/shard_map/all_gather | solution.py:204
  836.8 16.7 multiply_convert_fusion
  888.5 24.1 %reduce-scatter.16.cloned.1.call-done = bf16[192,2048]{1,0:T(8,128)(2,1)} async-done(((bf16[768,2048]{1,0:T(8,128)(2,1)}), bf16[192,2048]{1,0:T(8,128)(2,1)}) %reduce-scatter.16.cloned.1.call-update) | async-done | bytes 786448 | tf_op jit(solution)/shard_map/reduce_scatter | solution.py:76
  914.8 38.3 %reduce-scatter.14.cloned.1.call-done = bf16[192,2048]{1,0:T(8,128)(2,1)} async-done(((bf16[768,2048]{1,0:T(8,128)(2,1)}), bf16[192,2048]{1,0:T(8,128)(2,1)}) %reduce-scatter.14.cloned.1.call-update) | async-done | bytes 786448 | tf_op jit(solution)/shard_map/reduce_scatter | solution.py:76
  1043.6 16.8 collective-permute-done.7
  1064.8 15.7 collective-permute-done.8
  1139.8 15.3 all_to_all.94
  1197.7 18.9 all_to_all.95
  1265.1 74.1 %reduce-scatter.30.cloned.1.call-done = bf16[512,2048]{1,0:T(8,128)(2,1)} async-done(((bf16[2048,2048]{1,0:T(8,128)(2,1)}), bf16[512,2048]{1,0:T(8,128)(2,1)}) %reduce-scatter.30.cloned.1.call-update) | async-done | bytes 2097168 | tf_op jit(solution)/shard_map/reduce_scatter | solution.py:395
  1339.5 74.2 %reduce-scatter.18.cloned.1.call-done = bf16[2048,512]{1,0:T(8,128)(2,1)} async-done(((bf16[2048,2048]{1,0:T(8,128)(2,1)}), bf16[2048,512]{1,0:T(8,128)(2,1)}) %reduce-scatter.18.cloned.1.call-update) | async-done | bytes 2097168 | tf_op jit(solution)/shard_map/reduce_scatter | solution.py:377
  1437.9 23.3 %all-reduce.3 = (bf16[2048]{0:T(1024)(128)(2,1)S(1)}, bf16[2048]{0:T(1024)(128)(2,1)S(1)}) all-reduce(bf16[2048]{0:T(1024)(128)(2,1)S(1)} %get-tuple-element.15, bf16[2048]{0:T(1024)(128)(2,1)S(1)} %get-tuple-element.16), channel_id=4, replica_groups=mesh['blk'=8,'head'=4] {'blk'}, use_global_device_ids=true, to_apply=%region_22.23.clone | all-reduce | flops 4096 | bytes 16384
  1465.5 101.4 %reduce-scatter.34.cloned.1.call-done = bf16[256,2048]{1,0:T(8,128)(2,1)} async-done(((bf16[2048,2048]{1,0:T(8,128)(2,1)}), bf16[256,2048]{1,0:T(8,128)(2,1)}) %reduce-scatter.34.cloned.1.call-update) | async-done | bytes 1048592 | tf_op jit(solution)/shard_map/reduce_scatter | solution.py:421
  1569.7 149.3 %reduce-scatter.36.cloned.1.call-done = bf16[256,2048]{1,0:T(8,128)(2,1)} async-done(((bf16[2048,2048]{1,0:T(8,128)(2,1)}), bf16[256,2048]{1,0:T(8,128)(2,1)}) %reduce-scatter.36.cloned.1.call-update) | async-done | bytes 1048592 | tf_op jit(solution)/shard_map/reduce_scatter | solution.py:424
  1721.8 149.3 %reduce-scatter.38.cloned.1.call-done = bf16[2048,256]{1,0:T(8,128)(2,1)} async-done(((bf16[2048,2048]{1,0:T(8,128)(2,1)}), bf16[2048,256]{1,0:T(8,128)(2,1)}) %reduce-scatter.38.cloned.1.call-update) | async-done | bytes 1048592 | tf_op jit(solution)/shard_map/reduce_scatter | solution.py:427
  1873.8 63.4 %reduce-scatter.24.cloned.1.call-done = bf16[256,256]{1,0:T(8,128)(2,1)} async-done(((bf16[2048,256]{1,0:T(8,128)(2,1)}), bf16[256,256]{1,0:T(8,128)(2,1)}) %reduce-scatter.24.cloned.1.call-update) | async-done | bytes 131088 | tf_op jit(solution)/shard_map/reduce_scatter | solution.py:409
  1938.8 64.0 %reduce-scatter.28.cloned.1.call-done = bf16[256,256]{1,0:T(8,128)(2,1)} async-done(((bf16[2048,256]{1,0:T(8,128)(2,1)}), bf16[256,256]{1,0:T(8,128)(2,1)}) %reduce-scatter.28.cloned.1.call-update) | async-done | bytes 131088 | tf_op jit(solution)/shard_map/reduce_scatter | solution.py:412
  2004.4 69.7 %reduce-scatter.32.cloned.1.call-done = bf16[512,256]{1,0:T(8,128)(2,1)} async-done(((bf16[512,2048]{1,0:T(8,128)(2,1)}), bf16[512,256]{1,0:T(8,128)(2,1)}) %reduce-scatter.32.cloned.1.call-update) | async-done | bytes 262160 | tf_op jit(solution)/shard_map/reduce_scatter | solution.py:415
  2075.9 68.8 %reduce-scatter.20.cloned.1.call-done = bf16[256,512]{1,0:T(8,128)(2,1)} async-done(((bf16[2048,512]{1,0:T(8,128)(2,1)}), bf16[256,512]{1,0:T(8,128)(2,1)}) %reduce-scatter.20.cloned.1.call-update) | async-done | bytes 262160 | tf_op jit(solution)/shard_map/reduce_scatter | solution.py:406
  (476 shorter events, 514.1 us)
Async XLA Ops:
  7.2 45.8 %all-gather.16.cloned.1.call-start = ((), (), s32[]{:S(2)}) async-start(), calls=%async_computation.19 | async-start | bytes 1179648 | tf_op jit(solution)/shard_map/all_gather | solution.py:198
  7.9 86.2 %all-gather.20.cloned.1.call-start = ((), (), s32[]{:S(2)}) async-start(), calls=%async_computation.21 | async-start | bytes 1179648 | tf_op jit(solution)/shard_map/all_gather | solution.py:199
  8.7 135.6 %all-gather.24.cloned.1.call-start = ((), (), s32[]{:S(2)}) async-start(), calls=%async_computation.23 | async-start | bytes 2359296 | tf_op jit(solution)/shard_map/all_gather | solution.py:197
  9.4 186.4 %all-gather.28.cloned.1.call-start = ((), (), s32[]{:S(2)}) async-start(), calls=%async_computation.25 | async-start | bytes 2359296 | tf_op jit(solution)/shard_map/all_gather | solution.py:200
  10.0 220.5 %all-gather.18.cloned.1.call-start = ((), (), s32[]{:S(2)}) async-start(), calls=%async_computation.20 | async-start | bytes 5242880 | tf_op jit(solution)/shard_map/all_gather | solution.py:220
  53.0 213.9 %all-gather.22.cloned.1.call-start = ((), (), s32[]{:S(2)}) async-start(), calls=%async_computation.22 | async-start | bytes 5242880 | tf_op jit(solution)/shard_map/all_gather | solution.py:221
  94.1 278.6 %all-gather.26.cloned.1.call-start = ((), (), s32[]{:S(2)}) async-start(), calls=%async_computation.24 | async-start | bytes 10485760 | tf_op jit(solution)/shard_map/all_gather | solution.py:219
  144.3 326.9 %all-gather.30.cloned.1.call-start = ((), (), s32[]{:S(2)}) async-start(), calls=%async_computation.26 | async-start | bytes 10485760 | tf_op jit(solution)/shard_map/all_gather | solution.py:222
  195.8 329.5 %all-gather.34.cloned.1.call-start = ((), (), s32[]{:S(2)}) async-start(), calls=%async_computation.28 | async-start | bytes 9437184 | tf_op jit(solution)/shard_map/all_gather | solution.py:202
  366.6 22.0 %collective-permute-start.4 = (bf16[768,512]{1,0:T(8,128)(2,1)}, bf16[768,512]{1,0:T(8,128)(2,1)}, u32[]{:S(2)}, u32[]{:S(2)}) collective-permute-start(bf16[768,512]{1,0:T(8,128)(2,1)} %collective-permute-done.3), channel_id=1, source_target_pairs={{0,4},{4,8},{8,12},{12,16},{16,20},{20,24},{24,28},{1,5},{5,9},{9,... | collective-permute-start | bytes 2359304 | tf_op jit(solution)/shard_map/ppermute | solution.py:22
  388.6 25.4 %collective-permute-start.5 = (bf16[768,512]{1,0:T(8,128)(2,1)}, bf16[768,512]{1,0:T(8,128)(2,1)}, u32[]{:S(2)}, u32[]{:S(2)}) collective-permute-start(bf16[768,512]{1,0:T(8,128)(2,1)} %collective-permute-done.4), channel_id=1, source_target_pairs={{0,4},{4,8},{8,12},{12,16},{16,20},{20,24},{24,28},{1,5},{5,9},{9,... | collective-permute-start | bytes 2359304 | tf_op jit(solution)/shard_map/ppermute | solution.py:22
  446.4 23.0 %all-to-all-start.2 = ((bf16[4,2,49152]{2,1,0:T(2,128)(2,1)}), bf16[4,2,49152]{2,1,0:T(2,128)(2,1)S(1)}, u32[]{:S(2)}, u32[]{:S(2)}) async-start(bf16[4,2,49152]{2,1,0:T(2,128)(2,1)} %reshape.1185), calls=%async_computation.2 | async-start | bytes 1572864 | tf_op jit(solution)/shard_map/all_to_all | solution.py:268
  449.9 104.2 %all-gather.32.cloned.1.call-start = ((), (), s32[]{:S(2)}) async-start(), calls=%async_computation.27 | async-start | bytes 3932160 | tf_op jit(solution)/shard_map/all_gather | solution.py:72
  478.0 203.2 %all-gather.36.cloned.1.call-start = ((), (), s32[]{:S(2)}) async-start(), calls=%async_computation.29 | async-start | bytes 9437184 | tf_op jit(solution)/shard_map/all_gather | solution.py:203
  478.7 230.6 %all-gather.40.cloned.1.call-start = ((), (), s32[]{:S(2)}) async-start(), calls=%async_computation.32 | async-start | bytes 3932160 | tf_op jit(solution)/shard_map/all_gather | solution.py:72
  479.3 357.5 %all-gather.38.cloned.1.call-start = ((), (), s32[]{:S(2)}) async-start(), calls=%async_computation.30 | async-start | bytes 9437184 | tf_op jit(solution)/shard_map/all_gather | solution.py:204
  480.0 432.6 %reduce-scatter.16.cloned.1.call-start = ((), (), s32[]{:S(2)}) async-start(), calls=%async_computation.33 | async-start | bytes 3932160 | tf_op jit(solution)/shard_map/reduce_scatter | solution.py:76
  876.4 76.8 %reduce-scatter.14.cloned.1.call-start = ((), (), s32[]{:S(2)}) async-start(), calls=%async_computation.31 | async-start | bytes 3932160 | tf_op jit(solution)/shard_map/reduce_scatter | solution.py:76
  967.0 295.8 %reduce-scatter.22.cloned.1.call-start = ((), (), s32[]{:S(2)}) async-start(), calls=%async_computation.36 | async-start | bytes 5242880 | tf_op jit(solution)/shard_map/reduce_scatter | solution.py:383
  1018.3 21.2 collective-permute-start.6
  1039.7 20.7 collective-permute-start.7
  1060.5 20.0 collective-permute-start.8
  1164.7 100.3 %reduce-scatter.26.cloned.1.call-start = ((), (), s32[]{:S(2)}) async-start(), calls=%async_computation.38 | async-start | bytes 5242880 | tf_op jit(solution)/shard_map/reduce_scatter | solution.py:389
  1168.3 170.9 %reduce-scatter.30.cloned.1.call-start = ((), (), s32[]{:S(2)}) async-start(), calls=%async_computation.40 | async-start | bytes 10485760 | tf_op jit(solution)/shard_map/reduce_scatter | solution.py:395
  1175.9 237.9 %reduce-scatter.18.cloned.1.call-start = ((), (), s32[]{:S(2)}) async-start(), calls=%async_computation.34 | async-start | bytes 10485760 | tf_op jit(solution)/shard_map/reduce_scatter | solution.py:377
  1227.0 339.9 %reduce-scatter.34.cloned.1.call-start = ((), (), s32[]{:S(2)}) async-start(), calls=%async_computation.42 | async-start | bytes 9437184 | tf_op jit(solution)/shard_map/reduce_scatter | solution.py:421
  1239.8 479.2 %reduce-scatter.36.cloned.1.call-start = ((), (), s32[]{:S(2)}) async-start(), calls=%async_computation.43 | async-start | bytes 9437184 | tf_op jit(solution)/shard_map/reduce_scatter | solution.py:424
  1251.3 619.7 %reduce-scatter.38.cloned.1.call-start = ((), (), s32[]{:S(2)}) async-start(), calls=%async_computation.44 | async-start | bytes 9437184 | tf_op jit(solution)/shard_map/reduce_scatter | solution.py:427
  1262.7 674.4 %reduce-scatter.24.cloned.1.call-start = ((), (), s32[]{:S(2)}) async-start(), calls=%async_computation.37 | async-start | bytes 1179648 | tf_op jit(solution)/shard_map/reduce_scatter | solution.py:409
  1263.5 739.3 %reduce-scatter.28.cloned.1.call-start = ((), (), s32[]{:S(2)}) async-start(), calls=%async_computation.39 | async-start | bytes 1179648 | tf_op jit(solution)/shard_map/reduce_scatter | solution.py:412
  1265.1 809.0 %reduce-scatter.32.cloned.1.call-start = ((), (), s32[]{:S(2)}) async-start(), calls=%async_computation.41 | async-start | bytes 2359296 | tf_op jit(solution)/shard_map/reduce_scatter | solution.py:415
  1339.2 805.4 %reduce-scatter.20.cloned.1.call-start = ((), (), s32[]{:S(2)}) async-start(), calls=%async_computation.35 | async-start | bytes 2359296 | tf_op jit(solution)/shard_map/reduce_scatter | solution.py:406
  (125 other events, 2243.6 us)
Sparse Core Ops, SparseCore 0:
  10.1 42.8 all-gather.15
  55.1 38.8 all-gather.19
  96.2 48.0 all-gather.23
  146.2 49.5 all-gather.27
  197.2 33.2 all-gather.17
  231.8 35.0 all-gather.21
  268.5 62.7 all-gather.25
  332.9 60.4 all-gather.29
  395.5 129.8 all-gather.33
  527.3 26.7 all-gather.31
  556.2 124.9 all-gather.35
  682.6 26.7 all-gather.39
  711.4 125.3 all-gather.37
  876.5 36.0 reduce-scatter.15
  915.2 37.9 reduce-scatter.13
  1164.8 48.4 reduce-scatter.21
  1215.9 49.0 reduce-scatter.25
  1267.5 71.6 reduce-scatter.29
  1342.0 71.7 reduce-scatter.17
  1417.2 149.5 reduce-scatter.33
  1570.9 148.0 reduce-scatter.35
  1722.6 148.3 reduce-scatter.37
  1874.8 62.2 reduce-scatter.23
  1940.4 62.3 reduce-scatter.27
  2006.7 67.3 reduce-scatter.31
  2077.9 66.7 reduce-scatter.19
where the time goes:
time: 2160 us; the launch traced here: 2150 us
  waiting for transfers between devices  1610 us (75%)
  matrix products  255 us (12%)
  blocking collectives  124 us (6%)
  other arithmetic  54.8 us (3%)
  starting transfers between devices  50.2 us (2%)
  local copies, waits for them, and re-layouts  42.8 us (2%)
    reduce_scatter x1, waiting for transfers between devices, local(): lax.psum_scatter(up_grad.astype(jnp.bfloat16), 'blk', scatter_dimension=0...  149 us
    reduce_scatter x1, waiting for transfers between devices, local(): lax.psum_scatter(down_grad.astype(jnp.bfloat16), 'blk', scatter_dimension...  149 us
    ppermute x12, waiting for transfers between devices, passed_along(): return lax.ppermute(block, axis, route)  145 us
    all_gather x1, waiting for transfers between devices, local(): lax.all_gather(down_weight, 'blk', axis=1, tiled=True)  127 us
    all_gather x1, waiting for transfers between devices, local(): lax.all_gather(up_weight, 'blk', axis=0, tiled=True)  115 us
    reduce_scatter x1, waiting for transfers between devices, local(): lax.psum_scatter(gate_grad.astype(jnp.bfloat16), 'blk', scatter_dimension...  101 us
    reduce_scatter x1, waiting for transfers between devices, local(): lax.psum_scatter(outer_sum(normalized_input, query_tok_grad).astype(jnp.b...  74.2 us
    reduce_scatter x1, waiting for transfers between devices, local(): lax.psum_scatter(out_grad.astype(jnp.bfloat16), 'head', scatter_dimension...  74.1 us
  transfers between devices with their start and end apart: 41, of which 36 were waited for; matrix products, arithmetic and copies ran while one was open for 11% of the time, Pallas kernels for 0%

commit v1 on v0

v1 whole, which is shorter than its diff:
```python
import math

import jax
import jax.numpy as jnp
from jax import lax
from jax.sharding import PartitionSpec as P

QUERY_HEADS_ALL = 8
KEY_VALUE_HEADS = 4
HEAD_WIDTH = 256
SEQ = 4096

EPSILON = 1e-06
THETA_BASE = 1000042.0
MASKED = -1e30
BF = jnp.bfloat16
F32 = jnp.float32


def after(value, *deps):
    return lax.optimization_barrier((value, *deps))[0]


def cycle_order(count):
    return list(range(0, count, 2)) + list(range(count - 1, 0, -2))


def cycle_place(index, count):
    return jnp.where(index % 2 == 0, index // 2, count // 2 + (count - 1 - index) // 2)


def cycle_owner(place, count):
    place = lax.rem(place + 2 * count, count)
    return jnp.where(place < count // 2, 2 * place, 2 * (count - 1 - place) + 1)


def ring_routes(count):
    order = cycle_order(count)
    up = [(order[i], order[(i + 1) % count]) for i in range(count)]
    return up, [(b, a) for a, b in up]


def ring_gather(shard):
    count = lax.axis_size("blk")
    me = lax.axis_index("blk")
    place = cycle_place(me, count)
    up, down = ring_routes(count)
    rows = shard.shape[0]
    half = rows // 2
    out = jnp.zeros((count * rows, *shard.shape[1:]), shard.dtype)
    out = lax.dynamic_update_slice_in_dim(out, shard, me * rows, 0)
    left, right = shard, shard
    steps = []
    for step in range(1, count // 2 + 1):
        if step < count // 2:
            left = lax.ppermute(left, "blk", up)
            right = lax.ppermute(right, "blk", down)
            low, high = cycle_owner(place - step, count), cycle_owner(place + step, count)
            out = lax.dynamic_update_slice_in_dim(out, left, low * rows, 0)
            out = lax.dynamic_update_slice_in_dim(out, right, high * rows, 0)
        else:
            left = lax.ppermute(left[:half], "blk", up)
            right = lax.ppermute(right[half:], "blk", down)
            far = cycle_owner(place - step, count)
            out = lax.dynamic_update_slice_in_dim(out, left, far * rows, 0)
            out = lax.dynamic_update_slice_in_dim(out, right, far * rows + half, 0)
        steps.append((left, right))
    return out, steps


def ring_sum(blocks):
    count = lax.axis_size("blk")
    me = lax.axis_index("blk")
    place = cycle_place(me, count)
    up, down = ring_routes(count)
    rows = blocks.shape[0] // count
    half = rows // 2

    def part(offset):
        return lax.dynamic_slice_in_dim(
            blocks, cycle_owner(place + offset, count) * rows, rows, 0
        )

    far = part(count // 2)
    left = lax.ppermute(far[:half], "blk", up)
    right = lax.ppermute(far[half:], "blk", down)
    for step in range(count // 2 - 1, -1, -1):
        if step == count // 2 - 1:
            low, high = part(step), part(-step)
            left = jnp.concatenate([(low[:half].astype(F32) + left.astype(F32)).astype(BF), low[half:]])
            right = jnp.concatenate([high[:half], (high[half:].astype(F32) + right.astype(F32)).astype(BF)])
        elif step > 0:
            left = (part(step).astype(F32) + left.astype(F32)).astype(BF)
            right = (part(-step).astype(F32) + right.astype(F32)).astype(BF)
        else:
            return part(0).astype(F32) + left.astype(F32) + right.astype(F32)
        left = lax.ppermute(left, "blk", up)
        right = lax.ppermute(right, "blk", down)


def flip(value, axis, bit):
    return lax.ppermute(value, axis, [(i, i ^ bit) for i in range(lax.axis_size(axis))])


def head_gather(rows):
    other = flip(rows, "head", 2)
    pair = jnp.concatenate([rows, other], axis=0)
    beside = flip(pair, "head", 1)
    count = rows.shape[0]
    return jnp.concatenate([rows, beside[:count], other, beside[count:]], axis=0)


def head_sum(partial):
    low = partial.astype(BF).reshape(2, 2, partial.shape[0] // 4, *partial.shape[1:])
    near = flip(low[:, 1], "head", 1)
    pair = low[:, 0].astype(F32) + near.astype(F32)
    far = flip(pair[1].astype(BF), "head", 2)
    return pair[0] + far.astype(F32)


def slots(values, head_index):
    values = values.reshape(values.shape[0], 2, 2, values.shape[-1])
    values = jnp.where(head_index % 2 == 1, values[:, :, ::-1], values)
    values = jnp.where(head_index // 2 == 1, values[:, ::-1], values)
    return values.reshape(values.shape[0], -1)


def gain_gather(gains):
    count = lax.axis_size("blk")
    me = lax.axis_index("blk")
    bit = 1
    while bit < count:
        other = flip(gains, "blk", bit)
        low = jnp.concatenate([gains, other], axis=1)
        high = jnp.concatenate([other, gains], axis=1)
        gains = jnp.where((me // bit) % 2 == 0, low, high)
        bit *= 2
    return gains


def gain_sum(grad):
    for bit in (1, 2):
        grad = grad + flip(grad, "head", bit)
    count = lax.axis_size("blk")
    me = lax.axis_index("blk")
    bit = count // 2
    while bit:
        size = grad.shape[0] // 2
        upper = (me // bit) % 2 == 1
        keep = jnp.where(upper, grad[size:], grad[:size])
        send = jnp.where(upper, grad[:size], grad[size:])
        grad = keep + flip(send, "blk", bit)
        bit //= 2
    return grad


def rotary_table(token_pos, width):
    half_size = width // 2
    frequency = THETA_BASE ** (-2.0 * jnp.arange(half_size, dtype=F32) / width)
    angles = token_pos.astype(F32)[:, None] * frequency[None, :]
    return jnp.cos(angles)[:, None, :], jnp.sin(angles)[:, None, :]


def apply_rotary(values, table, direction):
    cosine, sine_part = table
    sine_part = sine_part * direction
    half_size = values.shape[-1] // 2
    first_half = values[..., :half_size]
    second_half = values[..., half_size:]
    return jnp.concatenate(
        [
            first_half * cosine - second_half * sine_part,
            second_half * cosine + first_half * sine_part,
        ],
        axis=-1,
    )


def norm_scale(values):
    return lax.rsqrt(jnp.mean(values * values, axis=-1, keepdims=True) + EPSILON)


def norm_back(values, gain_vec, inverse, upstream):
    weighted = upstream * gain_vec
    inner_mean = jnp.mean(weighted * values, axis=-1, keepdims=True)
    return inverse * weighted - values * (inverse * inverse * inverse) * inner_mean


def simple_product(matrix_a, matrix_b):
    return jnp.dot(matrix_a, matrix_b, preferred_element_type=F32)


def outer_sum(matrix_a, matrix_b):
    return lax.dot_general(
        matrix_a, matrix_b, (((0,), (0,)), ((), ())), preferred_element_type=F32
    )


def times_rows(matrix_a, matrix_b):
    return lax.dot_general(
        matrix_a, matrix_b, (((1,), (1,)), ((), ())), preferred_element_type=F32
    )


def block_scores(queries, key_part, allowed):
    score_scale = 1.0 / math.sqrt(queries.shape[-1])
    raw = jnp.einsum("qrd,kd->rqk", queries, key_part, preferred_element_type=F32) * score_scale
    return jnp.where(allowed[None], raw, MASKED)


def local(
    tokens,
    attn_gain,
    query_weight,
    key_matrix,
    value_matrix,
    out_weight,
    mlp_gain,
    gate_weight,
    up_weight,
    down_weight,
    segment_ids,
    positions,
    cotangent,
):
    heads = lax.axis_size("head")
    blocks = lax.axis_size("blk")
    blk = lax.axis_index("blk")
    head = lax.axis_index("head")
    own_rows = tokens.shape[0]
    rows = own_rows * heads
    window = min((SEQ + rows - 2) // rows + 1, blocks)
    width = HEAD_WIDTH
    repeats = QUERY_HEADS_ALL // KEY_VALUE_HEADS
    query_cols = query_weight.shape[1]

    segs = slots(segment_ids.reshape(blocks, heads, own_rows), head)
    poss = slots(positions.reshape(blocks, heads, own_rows), head)
    index = slots(jnp.arange(blocks * rows, dtype=jnp.int32).reshape(blocks, heads, own_rows), head)
    own_seg = lax.dynamic_index_in_dim(segs, blk, 0, False)
    own_pos = lax.dynamic_index_in_dim(poss, blk, 0, False)
    own_index = lax.dynamic_index_in_dim(index, blk, 0, False)
    first = jnp.maximum(blk - (window - 1), 0)
    key_seg = lax.dynamic_slice_in_dim(segs, first, window, 0)
    key_index = lax.dynamic_slice_in_dim(index, first, window, 0)

    qkv_full, qkv_steps = ring_gather(
        jnp.concatenate([query_weight, key_matrix, value_matrix], axis=1)
    )
    gains = gain_gather(jnp.stack([attn_gain, mlp_gain])).astype(F32)
    gain_one, gain_two = gains[0], gains[1]
    source_all = head_gather(tokens).astype(F32)
    out_full, out_steps = ring_gather(after(out_weight.T, qkv_steps[-2][0]))
    gate_full, gate_steps = ring_gather(after(gate_weight, qkv_steps[-1][0]))
    up_full, up_steps = ring_gather(after(up_weight, gate_steps[1][0]))
    down_full, down_steps = ring_gather(after(down_weight.T, up_steps[1][0]))
    cotangent_all = head_gather(after(cotangent, qkv_steps[-1][0]))

    inverse_all = norm_scale(source_all)
    normed_all = (source_all * inverse_all * gain_one).astype(BF)
    source = source_all[:own_rows]
    inverse_one = inverse_all[:own_rows]
    linear = simple_product(normed_all, qkv_full)
    table = rotary_table(own_pos, width)
    queries = apply_rotary(
        linear[:, :query_cols].reshape(rows, repeats, width), table, 1.0
    ).astype(BF)
    key_rot = apply_rotary(
        linear[:, query_cols : query_cols + width].reshape(rows, 1, width), table, 1.0
    ).reshape(rows, width)
    pair = jnp.concatenate(
        [key_rot.astype(BF), linear[:, query_cols + width :].astype(BF)], axis=1
    )
    pairs_all, _ = ring_gather(pair)
    pairs = lax.dynamic_slice_in_dim(pairs_all, first * rows, window * rows, 0)
    masks = [
        (own_seg[:, None] == key_seg[j][None, :]) & (key_index[j][None, :] <= own_index[:, None])
        for j in range(window)
    ]
    key_parts = [pairs[j * rows : (j + 1) * rows, :width] for j in range(window)]
    value_parts = [pairs[j * rows : (j + 1) * rows, width:] for j in range(window)]
    run_max = jnp.full((repeats, rows), MASKED, F32)
    run_total = jnp.zeros((repeats, rows), F32)
    for j in range(window):
        scores = block_scores(queries, key_parts[j], masks[j])
        new_max = jnp.maximum(run_max, jnp.max(scores, axis=-1))
        run_total = run_total * jnp.exp(run_max - new_max) + jnp.sum(
            jnp.where(masks[j][None], jnp.exp(scores - new_max[..., None]), 0.0), axis=-1
        )
        run_max = new_max
    log_total = run_max + jnp.log(run_total)
    attn_full = jnp.zeros((rows, repeats, width), F32)
    for j in range(window):
        scores = block_scores(queries, key_parts[j], masks[j])
        probs = jnp.exp(scores - log_total[..., None]).astype(BF)
        attn_full = attn_full + jnp.einsum(
            "rqk,kd->qrd", probs, value_parts[j], preferred_element_type=F32
        )
    attn_low = attn_full.reshape(rows, query_cols).astype(BF)
    residual = source + head_sum(times_rows(attn_low, out_full))

    inverse_two = norm_scale(residual)
    normed_two = (residual * inverse_two * gain_two).astype(BF)
    normed_two_all = head_gather(normed_two)
    gate_lin = simple_product(normed_two_all, gate_full)
    up_lin = simple_product(normed_two_all, up_full)
    sigmoid_gate = jax.nn.sigmoid(gate_lin)
    silu_gate = gate_lin * sigmoid_gate
    hidden = (silu_gate * up_lin).astype(BF)
    down_grad = ring_sum(outer_sum(cotangent_all, hidden).astype(BF)).T
    hidden_grad = simple_product(cotangent_all, down_full)
    gate_act_grad = (
        hidden_grad * up_lin * sigmoid_gate * (1.0 + gate_lin * (1.0 - sigmoid_gate))
    ).astype(BF)
    up_act_grad = (hidden_grad * silu_gate).astype(BF)
    normed_two_grad = head_sum(
        times_rows(gate_act_grad, gate_full) + times_rows(up_act_grad, up_full)
    )
    gate_grad = ring_sum(outer_sum(normed_two_all, gate_act_grad).astype(BF))
    up_grad = ring_sum(outer_sum(normed_two_all, up_act_grad).astype(BF))
    layer_out = (residual + head_sum(times_rows(hidden, down_full))).astype(BF)

    residual_grad = cotangent.astype(F32) + norm_back(
        residual, gain_two, inverse_two, normed_two_grad
    )
    mlp_gain_grad = gain_sum(jnp.sum(normed_two_grad * residual * inverse_two, axis=0))
    branch_all = head_gather(residual_grad.astype(BF))
    out_grad = ring_sum(outer_sum(branch_all, attn_low).astype(BF)).T

    attn_grad = simple_product(branch_all, out_full).astype(BF).reshape(rows, repeats, width)
    row_delta = jnp.einsum("qrd,qrd->rq", attn_grad.astype(F32), attn_full)
    score_scale = 1.0 / math.sqrt(width)
    query_rot_grad = jnp.zeros((rows, repeats, width), F32)
    pair_grads = []
    for j in range(window):
        scores = block_scores(queries, key_parts[j], masks[j])
        probs = jnp.exp(scores - log_total[..., None])
        prob_grad = jnp.einsum("qrd,kd->rqk", attn_grad, value_parts[j], preferred_element_type=F32)
        score_grad = (probs * (prob_grad - row_delta[..., None])).astype(BF)
        query_rot_grad = (
            query_rot_grad
            + jnp.einsum("rqk,kd->qrd", score_grad, key_parts[j], preferred_element_type=F32)
            * score_scale
        )
        key_grad = (
            jnp.einsum("rqk,qrd->kd", score_grad, queries, preferred_element_type=F32) * score_scale
        )
        value_grad = jnp.einsum(
            "rqk,qrd->kd", probs.astype(BF), attn_grad, preferred_element_type=F32
        )
        pair_grads.append(jnp.concatenate([key_grad, value_grad], axis=1).astype(BF))
    pair_grad = jnp.zeros((blocks * rows, 2 * width), BF)
    pair_grad = lax.dynamic_update_slice_in_dim(
        pair_grad, jnp.concatenate(pair_grads, axis=0), first * rows, 0
    )
    pair_grad = ring_sum(pair_grad)
    query_lin_grad = apply_rotary(query_rot_grad, table, -1.0).astype(BF).reshape(rows, query_cols)
    key_lin_grad = apply_rotary(pair_grad[:, :width].reshape(rows, 1, width), table, -1.0)
    pair_lin_grad = jnp.concatenate(
        [key_lin_grad.reshape(rows, width), pair_grad[:, width:]], axis=1
    ).astype(BF)
    query_grad = ring_sum(outer_sum(normed_all, query_lin_grad).astype(BF))
    pair_weight_grad = ring_sum(outer_sum(normed_all, pair_lin_grad).astype(BF))
    normed_grad_part = times_rows(query_lin_grad, qkv_full[:, :query_cols]) + times_rows(
        pair_lin_grad, qkv_full[:, query_cols:]
    )
    attn_gain_grad = gain_sum(jnp.sum(normed_grad_part * source_all * inverse_all, axis=0))
    normed_grad = head_sum(normed_grad_part)
    tokens_grad = residual_grad + norm_back(source, gain_one, inverse_one, normed_grad)
    return (
        layer_out,
        tokens_grad,
        attn_gain_grad,
        query_grad,
        pair_weight_grad[:, :width],
        pair_weight_grad[:, width:],
        out_grad,
        mlp_gain_grad,
        gate_grad,
        up_grad,
        down_grad,
    )


def solution(mesh):
    return jax.shard_map(
        local,
        mesh=mesh,
        in_specs=(
            P(("blk", "head"), None),
            P("blk"),
            P("blk", "head"),
            P("blk", "head"),
            P("blk", "head"),
            P("head", "blk"),
            P("blk"),
            P("blk", "head"),
            P("blk", "head"),
            P("head", "blk"),
            P(),
            P(),
            P(("blk", "head"), None),
        ),
        out_specs=(
            P(("blk", "head"), None),
            P(("blk", "head"), None),
            P("blk"),
            P("blk", "head"),
            P("blk", "head"),
            P("blk", "head"),
            P("head", "blk"),
            P("blk"),
            P("blk", "head"),
            P("blk", "head"),
            P("head", "blk"),
        ),
        check_vma=False,
    )
```

time: 2160 us -> 1110 us (0.51)
  waiting for transfers between devices: 1610 us -> 443 us
  blocking collectives: 124 us -> 0 us
  local copies, waits for them, and re-layouts: 42.8 us -> 162 us
  starting transfers between devices: 50.2 us -> 150 us
  other arithmetic: 54.8 us -> 109 us
  matrix products: 255 us -> 226 us
    reduce_scatter x13 -> x0, waiting for transfers between devices: 878 us -> none  [the longest x1 149 us: local(): lax.psum_scatter(up_grad.astype(jnp.bfloat16), 'blk', scatter_dimension=0...]
    all_gather x13 -> x0, waiting for transfers between devices: 566 us -> none  [the longest x1 127 us: local(): lax.all_gather(down_weight, 'blk', axis=1, tiled=True)]
    ppermute x12 -> x133, waiting for transfers between devices: 145 us -> 443 us  [the longest x18 139 us: ring_gather(): left = lax.ppermute(left, 'blk', up)]
    ppermute x12 -> x133, starting transfers between devices: 38.2 us -> 150 us  [the longest x29 33.2 us: flip(): lax.ppermute(value, axis, [(i, i ^ bit) for i in range(lax.axis_size(axis...]
    dynamic_update_slice x0 -> x54, local copies, waits for them, and re-layouts: none -> 70.6 us  [the longest x18 25.1 us: ring_gather(): out = lax.dynamic_update_slice_in_dim(out, right, high * rows, 0)]
    all_to_all x3 -> x0, blocking collectives: 53.1 us -> none  [the longest x1 18.9 us: local(): lax.all_to_all(pair_tok, 'head', split_axis=1, concat_axis=0, tiled=True)]
    all_gather x2 -> x0, blocking collectives: 37.1 us -> none  [the longest x1 19.4 us: local(): lax.all_gather(mlp_gain, 'blk', axis=0, tiled=True)]
    ppermute x0 -> x16, local copies, waits for them, and re-layouts: none -> 25.1 us  [the longest x6 9.74 us: ring_gather(): left = lax.ppermute(left, 'blk', up)]
  transfers between devices with their start and end apart: 41 -> 133, of which waited for: 36 -> 51; matrix products, arithmetic and copies ran while one was open for 11% -> 39% of each run, Pallas kernels for 0% -> 0%
where the time goes in v1:
time: 1110 us; the launch traced here: 1090 us
  waiting for transfers between devices  443 us (40%)
  matrix products  226 us (20%)
  local copies, waits for them, and re-layouts  162 us (15%)
  starting transfers between devices  150 us (14%)
  other arithmetic  109 us (10%)
    ppermute x18, waiting for transfers between devices, ring_gather(): left = lax.ppermute(left, 'blk', up)  139 us
    ppermute x21, waiting for transfers between devices, ring_sum(): right = lax.ppermute(right, 'blk', down)  118 us
    ppermute x21, waiting for transfers between devices, ring_sum(): left = lax.ppermute(left, 'blk', up)  88.9 us
    dot_general x5, matrix products, simple_product(): return jnp.dot(matrix_a, matrix_b, preferred_element_type=F32)  49.9 us
    dot_general x6, matrix products, times_rows(): lax.dot_general(matrix_a, matrix_b, (((1,), (1,)), ((), ())), preferred_e...  47.5 us
    ppermute x29, waiting for transfers between devices, flip(): lax.ppermute(value, axis, [(i, i ^ bit) for i in range(lax.axis_size(axis...  44.6 us
    ppermute x29, starting transfers between devices, flip(): lax.ppermute(value, axis, [(i, i ^ bit) for i in range(lax.axis_size(axis...  33.2 us
    dot_general x6, matrix products, outer_sum(): lax.dot_general(matrix_a, matrix_b, (((0,), (0,)), ((), ())), preferred_e...  32.2 us
  transfers between devices with their start and end apart: 133, of which 51 were waited for; matrix products, arithmetic and copies ran while one was open for 39% of the time, Pallas kernels for 0%

profile of v1, /device:TPU:0, one launch (start us, length us, event | category | flops | bytes accessed | tf_op | source)
XLA Modules:
  0.0 1094.0 jit_solution(6761392991743665193)
XLA Ops:
  36.9 9.2 collective-permute-done.7
  81.4 15.8 %collective-permute-done.23 = bf16[256,512]{0,1:T(8,128)(2,1)} collective-permute-done((bf16[256,512]{0,1:T(8,128)(2,1)S(1)}, bf16[256,512]{0,1:T(8,128)(2,1)}, u32[]{:S(2)}, u32[]{:S(2)}) %collective-permute-start.23) | collective-permute-done | bytes 262176 | tf_op jit(solution)/shard_map/ppermute | solution.py:56
  196.4 51.2 %collective-permute-done.17 = bf16[768,512]{1,0:T(8,128)(2,1)S(1)} collective-permute-done((bf16[768,512]{1,0:T(8,128)(2,1)}, bf16[768,512]{1,0:T(8,128)(2,1)S(1)}, u32[]{:S(2)}, u32[]{:S(2)}) %collective-permute-start.17) | collective-permute-done | bytes 786464 | tf_op jit(solution)/shard_map/ppermute | solution.py:56
  267.4 6.4 collective-permute-done.42
  364.3 29.5 %collective-permute-done.45 = bf16[256,2048]{1,0:T(8,128)(2,1)} collective-permute-done((bf16[256,2048]{1,0:T(8,128)(2,1)}, bf16[256,2048]{1,0:T(8,128)(2,1)}, u32[]{:S(2)}, u32[]{:S(2)}) %collective-permute-start.45) | collective-permute-done | bytes 1048608 | tf_op jit(solution)/shard_map/ppermute | solution.py:56
  418.0 12.9 %collective-permute-done.51 = bf16[256,2048]{0,1:T(8,128)(2,1)} collective-permute-done((bf16[256,2048]{0,1:T(8,128)(2,1)}, bf16[256,2048]{0,1:T(8,128)(2,1)}, u32[]{:S(2)}, u32[]{:S(2)}) %collective-permute-start.51) | collective-permute-done | bytes 1048608 | tf_op jit(solution)/shard_map/ppermute | solution.py:56
  447.5 6.9 collective-permute-done.53
  473.2 11.9 %fusion.73 = f32[768,2048]{1,0:T(8,128)} fusion(bf16[2048,2048]{0,1:T(8,128)(2,1)} %constant_dynamic-update-slice_fusion.1, bf16[192,2048]{1,0:T(8,128)(2,1)S(1)} %copy-done.70, bf16[192,2048]{1,0:T(8,128)(2,1)} %collective-permute-done.59, bf16[192,2048]{1,0:T(8,128)(2,1)S(1)} %copy-done.68, bf16[192,2048]{1,0:T(8,128)(2,1)} %param.25), kind=kOutput, calls=%fused_computation.238 | convolution fusion | flops 6455033856 | bytes 17825792 | tf_op jit(solution)/shard_map/dot_general | solution.py:190
  485.2 10.5 fusion.160
  495.7 18.3 %multiply_convert_fusion.1 = (bf16[768,2048]{1,0:T(8,128)(2,1)}, bf16[768,2048]{1,0:T(8,128)(2,1)}, bf16[768,2048]{1,0:T(8,128)(2,1)}) fusion(f32[768,2048]{1,0:T(8,128)} %fusion.73, f32[768,2048]{1,0:T(8,128)} %fusion.160, bf16[2048,2048]{0,1:T(8,128)(2,1)} %constant_dynamic-update-slice_fusion.19, bf16[192,2048]{1,0:T(8,128)(2,1)S(1)} %get-tuple-element.142, ...), kind=kOutput, calls=%fused_computation.6 | convolution fusion | flops 6478626816 | bytes 33554432 | tf_op jit(solution)/shard_map/dot_general | solution.py:190
  514.1 12.2 %convolution_convert_fusion.3 = bf16[768,2048]{1,0:T(8,128)(2,1)} fusion(bf16[768,2048]{1,0:T(8,128)(2,1)} %get-tuple-element.73, bf16[2048,2048]{0,1:T(8,128)(2,1)} %constant_dynamic-update-slice_fusion.1), kind=kOutput, calls=%fused_computation.62 | convolution fusion | flops 6444023808 | bytes 14680064 | tf_op jit(solution)/shard_map/dot_general | solution.py:200
  526.3 8.5 convolution_convert_fusion
  539.0 8.6 fusion.174
  547.6 8.1 convolution_convert_fusion.1
  559.3 8.8 convolution_convert_fusion.2
  570.0 13.1 %add_convert_fusion = bf16[768,2048]{1,0:T(8,128)(2,1)S(1)} fusion(f32[768,2048]{1,0:T(8,128)} %fusion.174, bf16[768,2048]{1,0:T(8,128)(2,1)} %get-tuple-element.71, bf16[2048,2048]{0,1:T(8,128)(2,1)} %constant_dynamic-update-slice_fusion.19), kind=kOutput, calls=%fused_computation.4 | convolution fusion | flops 6445596672 | bytes 20971520 | tf_op jit(solution)/shard_map/dot_general | solution.py:200
  608.6 10.0 collective-permute-done.126
  624.9 16.1 %collective-permute-done.118 = bf16[256,2048]{1,0:T(8,128)(2,1)S(1)} collective-permute-done((bf16[256,2048]{1,0:T(8,128)(2,1)S(1)}, bf16[256,2048]{1,0:T(8,128)(2,1)S(1)}, u32[]{:S(2)}, u32[]{:S(2)}) %collective-permute-start.118) | collective-permute-done | bytes 1048608 | tf_op jit(solution)/shard_map/ppermute | solution.py:97
  644.1 19.3 %collective-permute-done.110 = bf16[256,2048]{1,0:T(8,128)(2,1)S(1)} collective-permute-done((bf16[256,2048]{1,0:T(8,128)(2,1)S(1)}, bf16[256,2048]{1,0:T(8,128)(2,1)S(1)}, u32[]{:S(2)}, u32[]{:S(2)}) %collective-permute-start.110) | collective-permute-done | bytes 1048608 | tf_op jit(solution)/shard_map/ppermute | solution.py:97
  669.5 14.5 %collective-permute-done.106 = f32[1024]{0:T(1024)S(1)} collective-permute-done((f32[1024]{0:T(1024)S(1)}, f32[1024]{0:T(1024)S(1)}, u32[]{:S(2)}, u32[]{:S(2)}) %collective-permute-start.106) | collective-permute-done | bytes 4128 | tf_op jit(solution)/shard_map/ppermute | solution.py:102
  691.6 15.5 %collective-permute-done.107 = f32[512]{0:T(512)S(1)} collective-permute-done((f32[512]{0:T(512)S(1)}, f32[512]{0:T(512)S(1)}, u32[]{:S(2)}, u32[]{:S(2)}) %collective-permute-start.107) | collective-permute-done | bytes 2080 | tf_op jit(solution)/shard_map/ppermute | solution.py:102
  719.9 13.9 %collective-permute-done.114 = bf16[256,2048]{1,0:T(8,128)(2,1)S(1)} collective-permute-done((bf16[256,2048]{1,0:T(8,128)(2,1)}, bf16[256,2048]{1,0:T(8,128)(2,1)S(1)}, u32[]{:S(2)}, u32[]{:S(2)}) %collective-permute-start.114) | collective-permute-done | bytes 1048608 | tf_op jit(solution)/shard_map/ppermute | solution.py:98
  740.1 16.3 %collective-permute-done.131 = bf16[256,2048]{1,0:T(8,128)(2,1)S(1)} collective-permute-done((bf16[256,2048]{1,0:T(8,128)(2,1)S(1)}, bf16[256,2048]{1,0:T(8,128)(2,1)S(1)}, u32[]{:S(2)}, u32[]{:S(2)}) %collective-permute-start.131) | collective-permute-done | bytes 1048608 | tf_op jit(solution)/shard_map/ppermute | solution.py:98
  759.7 19.1 %collective-permute-done.123 = bf16[256,2048]{1,0:T(8,128)(2,1)S(1)} collective-permute-done((bf16[256,2048]{1,0:T(8,128)(2,1)S(1)}, bf16[256,2048]{1,0:T(8,128)(2,1)S(1)}, u32[]{:S(2)}, u32[]{:S(2)}) %collective-permute-start.123) | collective-permute-done | bytes 1048608 | tf_op jit(solution)/shard_map/ppermute | solution.py:98
  781.9 19.4 %collective-permute-done.115 = bf16[256,2048]{1,0:T(8,128)(2,1)S(1)} collective-permute-done((bf16[256,2048]{1,0:T(8,128)(2,1)S(1)}, bf16[256,2048]{1,0:T(8,128)(2,1)S(1)}, u32[]{:S(2)}, u32[]{:S(2)}) %collective-permute-start.115) | collective-permute-done | bytes 1048608 | tf_op jit(solution)/shard_map/ppermute | solution.py:98
  885.1 7.0 collective-permute-done.65
  904.3 15.1 %collective-permute-done.66 = bf16[768,512]{1,0:T(8,128)(2,1)S(1)} collective-permute-done((bf16[768,512]{1,0:T(8,128)(2,1)S(1)}, bf16[768,512]{1,0:T(8,128)(2,1)S(1)}, u32[]{:S(2)}, u32[]{:S(2)}) %collective-permute-start.66) | collective-permute-done | bytes 786464 | tf_op jit(solution)/shard_map/ppermute | solution.py:97
  932.8 17.2 %collective-permute-done.98 = bf16[256,512]{1,0:T(8,128)(2,1)S(1)} collective-permute-done((bf16[256,512]{1,0:T(8,128)(2,1)S(1)}, bf16[256,512]{1,0:T(8,128)(2,1)S(1)}, u32[]{:S(2)}, u32[]{:S(2)}) %collective-permute-start.98) | collective-permute-done | bytes 262176 | tf_op jit(solution)/shard_map/ppermute | solution.py:97
  958.7 26.2 %collective-permute-done.85 = bf16[256,512]{1,0:T(8,128)(2,1)S(1)} collective-permute-done((bf16[256,512]{1,0:T(8,128)(2,1)S(1)}, bf16[256,512]{1,0:T(8,128)(2,1)S(1)}, u32[]{:S(2)}, u32[]{:S(2)}) %collective-permute-start.85) | collective-permute-done | bytes 262176 | tf_op jit(solution)/shard_map/ppermute | solution.py:98
  992.4 13.8 %collective-permute-done.71 = bf16[768,512]{1,0:T(8,128)(2,1)S(1)} collective-permute-done((bf16[768,512]{1,0:T(8,128)(2,1)S(1)}, bf16[768,512]{1,0:T(8,128)(2,1)S(1)}, u32[]{:S(2)}, u32[]{:S(2)}) %collective-permute-start.71) | collective-permute-done | bytes 786464 | tf_op jit(solution)/shard_map/ppermute | solution.py:98
  1029.2 6.4 multiply_reduce_fusion
  1080.4 8.1 collective-permute-done.74
  (828 shorter events, 620.7 us)
Async XLA Ops:
  50.3 59.2 %collective-permute-start.1 = (bf16[384,2048]{1,0:T(8,128)(2,1)}, bf16[384,2048]{1,0:T(8,128)(2,1)}, u32[]{:S(2)}, u32[]{:S(2)}) collective-permute-start(bf16[384,2048]{1,0:T(8,128)(2,1)} %pad_maximum_fusion.4), channel_id=1, source_target_pairs={{0,1},{1,0},{2,3},{3,2},{4,5},{5,4},{6,7},{7,6},{8,9},{9,8},{10,11... | collective-permute-start | bytes 4718600 | tf_op jit(solution)/shard_map/ppermute | solution.py:102
  68.2 74.9 %collective-permute-start.33 = (bf16[256,2048]{1,0:T(8,128)(2,1)}, bf16[256,2048]{1,0:T(8,128)(2,1)}, u32[]{:S(2)}, u32[]{:S(2)}) collective-permute-start(bf16[256,2048]{1,0:T(8,128)(2,1)} %param.20), channel_id=1, source_target_pairs={{0,8},{8,16},{16,24},{24,28},{28,20},{20,12},{12,4},{4,0},{1,9},{9... | collective-permute-start | bytes 3145736 | tf_op jit(solution)/shard_map/ppermute | solution.py:56
  81.1 63.7 %collective-permute-start.34 = (bf16[256,2048]{1,0:T(8,128)(2,1)}, bf16[256,2048]{1,0:T(8,128)(2,1)}, u32[]{:S(2)}, u32[]{:S(2)}) collective-permute-start(bf16[256,2048]{1,0:T(8,128)(2,1)} %param.20), channel_id=1, source_target_pairs={{8,0},{16,8},{24,16},{28,24},{20,28},{12,20},{4,12},{0,4},{9,1},{1... | collective-permute-start | bytes 3145736 | tf_op jit(solution)/shard_map/ppermute | solution.py:57
  143.1 49.7 %collective-permute-start.60 = (bf16[384,2048]{1,0:T(8,128)(2,1)}, bf16[384,2048]{1,0:T(8,128)(2,1)}, u32[]{:S(2)}, u32[]{:S(2)}) collective-permute-start(bf16[384,2048]{1,0:T(8,128)(2,1)} %pad_maximum_fusion.6), channel_id=1, source_target_pairs={{0,1},{1,0},{2,3},{3,2},{4,5},{5,4},{6,7},{7,6},{8,9},{9,8},{10,11... | collective-permute-start | bytes 4718600 | tf_op jit(solution)/shard_map/ppermute | solution.py:102
  171.1 91.5 %collective-permute-start.41 = (bf16[256,2048]{1,0:T(8,128)(2,1)}, bf16[256,2048]{1,0:T(8,128)(2,1)}, u32[]{:S(2)}, u32[]{:S(2)}) collective-permute-start(bf16[256,2048]{1,0:T(8,128)(2,1)} %param.21), channel_id=1, source_target_pairs={{0,8},{8,16},{16,24},{24,28},{28,20},{20,12},{12,4},{4,0},{1,9},{9... | collective-permute-start | bytes 3145736 | tf_op jit(solution)/shard_map/ppermute | solution.py:56
  180.6 77.3 %collective-permute-start.37 = (bf16[256,2048]{1,0:T(8,128)(2,1)}, bf16[256,2048]{1,0:T(8,128)(2,1)}, u32[]{:S(2)}, u32[]{:S(2)}) collective-permute-start(bf16[256,2048]{1,0:T(8,128)(2,1)} %copy-done.63), channel_id=1, source_target_pairs={{0,8},{8,16},{16,24},{24,28},{28,20},{20,12},{12,4},{4,0},{1,9},{9... | collective-permute-start | bytes 3145736 | tf_op jit(solution)/shard_map/ppermute | solution.py:56
  186.2 61.3 %collective-permute-start.17 = (bf16[768,512]{1,0:T(8,128)(2,1)}, bf16[768,512]{1,0:T(8,128)(2,1)S(1)}, u32[]{:S(2)}, u32[]{:S(2)}) collective-permute-start(bf16[768,512]{1,0:T(8,128)(2,1)} %collective-permute-done.15), channel_id=1, source_target_pairs={{0,8},{8,16},{16,24},{24,28},{28,20},{20,12},{12,4},{4,0},{1,9},{9... | collective-permute-start | bytes 2359304 | tf_op jit(solution)/shard_map/ppermute | solution.py:56
  192.4 68.0 %collective-permute-start.38 = (bf16[256,2048]{1,0:T(8,128)(2,1)}, bf16[256,2048]{1,0:T(8,128)(2,1)S(1)}, u32[]{:S(2)}, u32[]{:S(2)}) collective-permute-start(bf16[256,2048]{1,0:T(8,128)(2,1)} %collective-permute-done.36), channel_id=1, source_target_pairs={{8,0},{16,8},{24,16},{28,24},{20,28},{12,20},{4,12},{0,4},{9,1},{1... | collective-permute-start | bytes 3145736 | tf_op jit(solution)/shard_map/ppermute | solution.py:57
  192.8 60.9 %collective-permute-start.18 = (bf16[768,512]{1,0:T(8,128)(2,1)}, bf16[768,512]{1,0:T(8,128)(2,1)S(1)}, u32[]{:S(2)}, u32[]{:S(2)}) collective-permute-start(bf16[768,512]{1,0:T(8,128)(2,1)} %collective-permute-done.16), channel_id=1, source_target_pairs={{8,0},{16,8},{24,16},{28,24},{20,28},{12,20},{4,12},{0,4},{9,1},{1... | collective-permute-start | bytes 2359304 | tf_op jit(solution)/shard_map/ppermute | solution.py:57
  260.3 81.5 %collective-permute-start.39 = (bf16[128,2048]{1,0:T(8,128)(2,1)}, bf16[128,2048]{1,0:T(8,128)(2,1)}, u32[]{:S(2)}, u32[]{:S(2)}) collective-permute-start(bf16[128,2048]{1,0:T(8,128)(2,1)} %slice.644), channel_id=1, source_target_pairs={{0,8},{8,16},{16,24},{24,28},{28,20},{20,12},{12,4},{4,0},{1,9},{9... | collective-permute-start | bytes 1572872 | tf_op jit(solution)/shard_map/ppermute | solution.py:62
  262.6 80.6 %collective-permute-start.40 = (bf16[128,2048]{1,0:T(8,128)(2,1)}, bf16[128,2048]{1,0:T(8,128)(2,1)}, u32[]{:S(2)}, u32[]{:S(2)}) collective-permute-start(bf16[128,2048]{1,0:T(8,128)(2,1)} %slice.645), channel_id=1, source_target_pairs={{8,0},{16,8},{24,16},{28,24},{20,28},{12,20},{4,12},{0,4},{9,1},{1... | collective-permute-start | bytes 1572872 | tf_op jit(solution)/shard_map/ppermute | solution.py:63
  274.8 71.6 %collective-permute-start.43 = (bf16[256,2048]{1,0:T(8,128)(2,1)}, bf16[256,2048]{1,0:T(8,128)(2,1)}, u32[]{:S(2)}, u32[]{:S(2)}) collective-permute-start(bf16[256,2048]{1,0:T(8,128)(2,1)} %collective-permute-done.41), channel_id=1, source_target_pairs={{0,8},{8,16},{16,24},{24,28},{28,20},{20,12},{12,4},{4,0},{1,9},{9... | collective-permute-start | bytes 3145736 | tf_op jit(solution)/shard_map/ppermute | solution.py:56
  279.1 72.5 %collective-permute-start.44 = (bf16[256,2048]{1,0:T(8,128)(2,1)}, bf16[256,2048]{1,0:T(8,128)(2,1)}, u32[]{:S(2)}, u32[]{:S(2)}) collective-permute-start(bf16[256,2048]{1,0:T(8,128)(2,1)} %copy-done.62), channel_id=1, source_target_pairs={{8,0},{16,8},{24,16},{28,24},{20,28},{12,20},{4,12},{0,4},{9,1},{1... | collective-permute-start | bytes 3145736 | tf_op jit(solution)/shard_map/ppermute | solution.py:57
  346.4 60.0 %collective-permute-start.49 = (bf16[256,2048]{0,1:T(8,128)(2,1)}, bf16[256,2048]{0,1:T(8,128)(2,1)}, u32[]{:S(2)}, u32[]{:S(2)}) collective-permute-start(bf16[256,2048]{0,1:T(8,128)(2,1)} %bitcast.35), channel_id=1, source_target_pairs={{0,8},{8,16},{16,24},{24,28},{28,20},{20,12},{12,4},{4,0},{1,9},{9... | collective-permute-start | bytes 3145736 | tf_op jit(solution)/shard_map/ppermute | solution.py:56
  348.0 59.9 %collective-permute-start.50 = (bf16[256,2048]{0,1:T(8,128)(2,1)}, bf16[256,2048]{0,1:T(8,128)(2,1)}, u32[]{:S(2)}, u32[]{:S(2)}) collective-permute-start(bf16[256,2048]{0,1:T(8,128)(2,1)} %bitcast.35), channel_id=1, source_target_pairs={{8,0},{16,8},{24,16},{28,24},{20,28},{12,20},{4,12},{0,4},{9,1},{1... | collective-permute-start | bytes 3145736 | tf_op jit(solution)/shard_map/ppermute | solution.py:57
  362.6 52.8 %collective-permute-start.30 = (bf16[192,2048]{1,0:T(8,128)(2,1)}, bf16[192,2048]{1,0:T(8,128)(2,1)}, u32[]{:S(2)}, u32[]{:S(2)}) collective-permute-start(bf16[192,2048]{1,0:T(8,128)(2,1)} %fusion.62), channel_id=1, source_target_pairs={{0,2},{1,3},{2,0},{3,1},{4,6},{5,7},{6,4},{7,5},{8,10},{9,11},{10,... | collective-permute-start | bytes 2359304 | tf_op jit(solution)/shard_map/ppermute | solution.py:102
  536.0 49.1 %collective-permute-start.125 = (bf16[128,2048]{1,0:T(8,128)(2,1)}, bf16[128,2048]{1,0:T(8,128)(2,1)}, u32[]{:S(2)}, u32[]{:S(2)}) collective-permute-start(bf16[128,2048]{1,0:T(8,128)(2,1)} %get-tuple-element.78), channel_id=1, source_target_pairs={{0,8},{8,16},{16,24},{24,28},{28,20},{20,12},{12,4},{4,0},{1,9},{9... | collective-permute-start | bytes 1572872 | tf_op jit(solution)/shard_map/ppermute | solution.py:85
  536.4 49.5 %collective-permute-start.129 = (bf16[128,2048]{1,0:T(8,128)(2,1)}, bf16[128,2048]{1,0:T(8,128)(2,1)}, u32[]{:S(2)}, u32[]{:S(2)}) collective-permute-start(bf16[128,2048]{1,0:T(8,128)(2,1)} %get-tuple-element.80), channel_id=1, source_target_pairs={{8,0},{16,8},{24,16},{28,24},{20,28},{12,20},{4,12},{0,4},{9,1},{1... | collective-permute-start | bytes 1572872 | tf_op jit(solution)/shard_map/ppermute | solution.py:86
  589.1 120.2 %collective-permute-start.130 = (bf16[256,2048]{1,0:T(8,128)(2,1)}, bf16[256,2048]{1,0:T(8,128)(2,1)}, u32[]{:S(2)}, u32[]{:S(2)}) collective-permute-start(bf16[256,2048]{1,0:T(8,128)(2,1)} %pad_maximum_fusion.13), channel_id=1, source_target_pairs={{8,0},{16,8},{24,16},{28,24},{20,28},{12,20},{4,12},{0,4},{9,1},{1... | collective-permute-start | bytes 3145736 | tf_op jit(solution)/shard_map/ppermute | solution.py:98
  600.0 114.6 %collective-permute-start.122 = (bf16[256,2048]{1,0:T(8,128)(2,1)}, bf16[256,2048]{1,0:T(8,128)(2,1)}, u32[]{:S(2)}, u32[]{:S(2)}) collective-permute-start(bf16[256,2048]{1,0:T(8,128)(2,1)} %pad_maximum_fusion.11), channel_id=1, source_target_pairs={{8,0},{16,8},{24,16},{28,24},{20,28},{12,20},{4,12},{0,4},{9,1},{1... | collective-permute-start | bytes 3145736 | tf_op jit(solution)/shard_map/ppermute | solution.py:98
  622.8 86.9 %collective-permute-start.127 = (bf16[256,2048]{1,0:T(8,128)(2,1)}, bf16[256,2048]{1,0:T(8,128)(2,1)}, u32[]{:S(2)}, u32[]{:S(2)}) collective-permute-start(bf16[256,2048]{1,0:T(8,128)(2,1)} %add_convert_fusion.4), channel_id=1, source_target_pairs={{0,8},{8,16},{16,24},{24,28},{28,20},{20,12},{12,4},{4,0},{1,9},{9... | collective-permute-start | bytes 3145736 | tf_op jit(solution)/shard_map/ppermute | solution.py:97
  733.9 44.9 %collective-permute-start.123 = (bf16[256,2048]{1,0:T(8,128)(2,1)S(1)}, bf16[256,2048]{1,0:T(8,128)(2,1)S(1)}, u32[]{:S(2)}, u32[]{:S(2)}) collective-permute-start(bf16[256,2048]{1,0:T(8,128)(2,1)S(1)} %get-tuple-element.83), channel_id=1, source_target_pairs={{8,0},{16,8},{24,16},{28,24},{20,28},{12,20},{4,12},{0,4},{9,1},{1... | collective-permute-start | bytes 3145736 | tf_op jit(solution)/shard_map/ppermute | solution.py:98
  737.2 64.1 %collective-permute-start.115 = (bf16[256,2048]{1,0:T(8,128)(2,1)S(1)}, bf16[256,2048]{1,0:T(8,128)(2,1)S(1)}, u32[]{:S(2)}, u32[]{:S(2)}) collective-permute-start(bf16[256,2048]{1,0:T(8,128)(2,1)S(1)} %get-tuple-element.91), channel_id=1, source_target_pairs={{8,0},{16,8},{24,16},{28,24},{20,28},{12,20},{4,12},{0,4},{9,1},{1... | collective-permute-start | bytes 3145736 | tf_op jit(solution)/shard_map/ppermute | solution.py:98
  737.4 67.1 %collective-permute-start.64 = (bf16[384,2048]{1,0:T(8,128)(2,1)S(1)}, bf16[384,2048]{1,0:T(8,128)(2,1)S(1)}, u32[]{:S(2)}, u32[]{:S(2)}) collective-permute-start(bf16[384,2048]{1,0:T(8,128)(2,1)S(1)} %pad_maximum_fusion.7), channel_id=1, source_target_pairs={{0,1},{1,0},{2,3},{3,2},{4,5},{5,4},{6,7},{7,6},{8,9},{9,8},{10,11... | collective-permute-start | bytes 4718600 | tf_op jit(solution)/shard_map/ppermute | solution.py:102
  738.1 142.4 %collective-permute-start.128 = (bf16[256,2048]{1,0:T(8,128)(2,1)}, bf16[256,2048]{1,0:T(8,128)(2,1)}, u32[]{:S(2)}, u32[]{:S(2)}) collective-permute-start(bf16[256,2048]{1,0:T(8,128)(2,1)} %get-tuple-element.74), channel_id=1, source_target_pairs={{0,8},{8,16},{16,24},{24,28},{28,20},{20,12},{12,4},{4,0},{1,9},{9... | collective-permute-start | bytes 3145736 | tf_op jit(solution)/shard_map/ppermute | solution.py:97
  756.3 200.3 %collective-permute-start.120 = (bf16[256,2048]{1,0:T(8,128)(2,1)}, bf16[256,2048]{1,0:T(8,128)(2,1)}, u32[]{:S(2)}, u32[]{:S(2)}) collective-permute-start(bf16[256,2048]{1,0:T(8,128)(2,1)} %get-tuple-element.82), channel_id=1, source_target_pairs={{0,8},{8,16},{16,24},{24,28},{28,20},{20,12},{12,4},{4,0},{1,9},{9... | collective-permute-start | bytes 3145736 | tf_op jit(solution)/shard_map/ppermute | solution.py:97
  778.8 103.7 %collective-permute-start.132 = (bf16[256,2048]{1,0:T(8,128)(2,1)}, bf16[256,2048]{1,0:T(8,128)(2,1)}, u32[]{:S(2)}, u32[]{:S(2)}) collective-permute-start(bf16[256,2048]{1,0:T(8,128)(2,1)} %add_convert_fusion.1), channel_id=1, source_target_pairs={{8,0},{16,8},{24,16},{28,24},{20,28},{12,20},{4,12},{0,4},{9,1},{1... | collective-permute-start | bytes 3145736 | tf_op jit(solution)/shard_map/ppermute | solution.py:98
  801.3 155.4 %collective-permute-start.124 = (bf16[256,2048]{1,0:T(8,128)(2,1)}, bf16[256,2048]{1,0:T(8,128)(2,1)}, u32[]{:S(2)}, u32[]{:S(2)}) collective-permute-start(bf16[256,2048]{1,0:T(8,128)(2,1)} %add_convert_fusion.5), channel_id=1, source_target_pairs={{8,0},{16,8},{24,16},{28,24},{20,28},{12,20},{4,12},{0,4},{9,1},{1... | collective-permute-start | bytes 3145736 | tf_op jit(solution)/shard_map/ppermute | solution.py:98
  950.1 57.9 %collective-permute-start.112 = (bf16[256,2048]{1,0:T(8,128)(2,1)S(1)}, bf16[256,2048]{1,0:T(8,128)(2,1)S(1)}, u32[]{:S(2)}, u32[]{:S(2)}) collective-permute-start(bf16[256,2048]{1,0:T(8,128)(2,1)S(1)} %copy-done.64), channel_id=1, source_target_pairs={{0,8},{8,16},{16,24},{24,28},{28,20},{20,12},{12,4},{4,0},{1,9},{9... | collective-permute-start | bytes 3145736 | tf_op jit(solution)/shard_map/ppermute | solution.py:97
  953.2 56.2 %collective-permute-start.116 = (bf16[256,2048]{1,0:T(8,128)(2,1)S(1)}, bf16[256,2048]{1,0:T(8,128)(2,1)S(1)}, u32[]{:S(2)}, u32[]{:S(2)}) collective-permute-start(bf16[256,2048]{1,0:T(8,128)(2,1)S(1)} %copy-done.61), channel_id=1, source_target_pairs={{8,0},{16,8},{24,16},{28,24},{20,28},{12,20},{4,12},{0,4},{9,1},{1... | collective-permute-start | bytes 3145736 | tf_op jit(solution)/shard_map/ppermute | solution.py:98
  1014.8 57.6 %collective-permute-start.83 = (bf16[256,512]{1,0:T(8,128)(2,1)}, bf16[256,512]{1,0:T(8,128)(2,1)S(1)}, u32[]{:S(2)}, u32[]{:S(2)}) collective-permute-start(bf16[256,512]{1,0:T(8,128)(2,1)} %get-tuple-element.128), channel_id=1, source_target_pairs={{0,8},{8,16},{16,24},{24,28},{28,20},{20,12},{12,4},{4,0},{1,9},{9... | collective-permute-start | bytes 786440 | tf_op jit(solution)/shard_map/ppermute | solution.py:97
  1017.4 56.5 %collective-permute-start.87 = (bf16[256,512]{1,0:T(8,128)(2,1)S(1)}, bf16[256,512]{1,0:T(8,128)(2,1)S(1)}, u32[]{:S(2)}, u32[]{:S(2)}) collective-permute-start(bf16[256,512]{1,0:T(8,128)(2,1)S(1)} %add_convert_fusion.35), channel_id=1, source_target_pairs={{8,0},{16,8},{24,16},{28,24},{20,28},{12,20},{4,12},{0,4},{9,1},{1... | collective-permute-start | bytes 786440 | tf_op jit(solution)/shard_map/ppermute | solution.py:98
  (233 other events, 5030.6 us)

commit v2 on v1

--- a/solution.py
+++ b/solution.py
@@ -3,6 +3,8 @@
 import jax
 import jax.numpy as jnp
 from jax import lax
+from jax.experimental import pallas as pl
+from jax.experimental.pallas import tpu as pltpu
 from jax.sharding import PartitionSpec as P
 
 QUERY_HEADS_ALL = 8
@@ -202,10 +204,174 @@
     )
 
 
-def block_scores(queries, key_part, allowed):
-    score_scale = 1.0 / math.sqrt(queries.shape[-1])
-    raw = jnp.einsum("qrd,kd->rqk", queries, key_part, preferred_element_type=F32) * score_scale
-    return jnp.where(allowed[None], raw, MASKED)
+CHUNK = 256
+
+
+def contract(a, b, dim_a, dim_b):
+    return lax.dot_general(
+        a, b, (((dim_a,), (dim_b,)), ((), ())), preferred_element_type=F32
+    )
+
+
+def attend_kernel(repeats, width, kind, q_ref, kv_ref, low_ref, high_ref, index_ref, out_ref, lse_ref, acc, top, total):
+    step = pl.program_id(0)
+    rows = q_ref.shape[0]
+
+    @pl.when(step == 0)
+    def _():
+        acc[...] = jnp.zeros_like(acc)
+        top[...] = jnp.full_like(top, MASKED)
+        total[...] = jnp.zeros_like(total)
+
+    def block(masked):
+        keys = kv_ref[:, :width]
+        values = kv_ref[:, width:]
+        for start in range(0, rows, CHUNK):
+            part = pl.ds(start, CHUNK)
+            if masked:
+                index = index_ref[0]
+                allowed = (index >= low_ref[part, :]) & (index <= high_ref[part, :])
+            for r in range(repeats):
+                cols = slice(r * width, (r + 1) * width)
+                scores = contract(q_ref[part, cols], keys, 1, 1)
+                if masked:
+                    scores = jnp.where(allowed, scores, MASKED)
+                old = top[r, part, :]
+                new = jnp.maximum(old, jnp.max(scores, axis=1, keepdims=True))
+                probs = jnp.exp(scores - new)
+                if masked:
+                    probs = jnp.where(allowed, probs, 0.0)
+                factor = jnp.exp(old - new)
+                total[r, part, :] = total[r, part, :] * factor + jnp.sum(probs, axis=1, keepdims=True)
+                top[r, part, :] = new
+                acc[part, cols] = acc[part, cols] * factor + contract(probs.astype(BF), values, 1, 0)
+
+    pl.when(kind[step] == 1)(lambda: block(False))
+    pl.when(kind[step] == 2)(lambda: block(True))
+
+    @pl.when(step == pl.num_programs(0) - 1)
+    def _():
+        for r in range(repeats):
+            cols = slice(r * width, (r + 1) * width)
+            out_ref[:, cols] = acc[:, cols] / total[r]
+            lse_ref[r] = top[r] + jnp.log(total[r])
+
+
+def attend(kind, queries, pairs, low, high, index, repeats, width):
+    rows = queries.shape[0]
+    blocks = pairs.shape[0] // rows
+    whole = lambda shape: pl.BlockSpec(shape, lambda j, kind: (0,) * len(shape))
+    return pl.pallas_call(
+        lambda *refs: attend_kernel(repeats, width, *refs),
+        grid_spec=pltpu.PrefetchScalarGridSpec(
+            num_scalar_prefetch=1,
+            grid=(blocks,),
+            in_specs=[
+                whole((rows, repeats * width)),
+                pl.BlockSpec((rows, 2 * width), lambda j, kind: (j, 0)),
+                whole((rows, 1)),
+                whole((rows, 1)),
+                pl.BlockSpec((1, 1, rows), lambda j, kind: (j, 0, 0)),
+            ],
+            out_specs=[whole((rows, repeats * width)), whole((repeats, rows, 1))],
+            scratch_shapes=[
+                pltpu.VMEM((rows, repeats * width), F32),
+                pltpu.VMEM((repeats, rows, 1), F32),
+                pltpu.VMEM((repeats, rows, 1), F32),
+            ],
+        ),
+        out_shape=[
+            jax.ShapeDtypeStruct((rows, repeats * width), F32),
+            jax.ShapeDtypeStruct((repeats, rows, 1), F32),
+        ],
+        compiler_params=pltpu.CompilerParams(vmem_limit_bytes=40 * 2**20),
+        cost_estimate=pl.CostEstimate(
+            flops=4 * repeats * width * rows * rows * 7,
+            bytes_accessed=12 * 2**20,
+            transcendentals=repeats * rows * rows * 7,
+        ),
+        name="attend",
+    )(kind, queries, pairs, low, high, index)
+
+
+def attend_back_kernel(
+    repeats, width, kind, q_ref, kv_ref, up_ref, low_ref, high_ref, index_ref, lse_ref, delta_ref, dq_ref, dkv_ref
+):
+    step = pl.program_id(0)
+    rows = q_ref.shape[0]
+
+    @pl.when(step == 0)
+    def _():
+        dq_ref[...] = jnp.zeros_like(dq_ref)
+
+    def block(masked):
+        for start in range(0, rows, CHUNK):
+            part = pl.ds(start, CHUNK)
+            keys = kv_ref[part, :width]
+            values = kv_ref[part, width:]
+            key_grad = jnp.zeros((CHUNK, width), F32)
+            value_grad = jnp.zeros((CHUNK, width), F32)
+            if masked:
+                index = index_ref[0, part, :]
+                allowed = (index >= low_ref[...]) & (index <= high_ref[...])
+            for r in range(repeats):
+                cols = slice(r * width, (r + 1) * width)
+                queries, upstream = q_ref[:, cols], up_ref[:, cols]
+                probs = jnp.exp(contract(keys, queries, 1, 1) - lse_ref[r])
+                if masked:
+                    probs = jnp.where(allowed, probs, 0.0)
+                prob_grad = contract(values, upstream, 1, 1)
+                score_grad = (probs * (prob_grad - delta_ref[r])).astype(BF)
+                value_grad += contract(probs.astype(BF), upstream, 1, 0)
+                key_grad += contract(score_grad, queries, 1, 0)
+                dq_ref[:, cols] += contract(score_grad, keys, 0, 0)
+            dkv_ref[part, :width] = key_grad.astype(BF)
+            dkv_ref[part, width:] = value_grad.astype(BF)
+
+    @pl.when(kind[step] == 0)
+    def _():
+        dkv_ref[...] = jnp.zeros_like(dkv_ref)
+
+    pl.when(kind[step] == 1)(lambda: block(False))
+    pl.when(kind[step] == 2)(lambda: block(True))
+
+
+def attend_back(kind, queries, pairs, upstream, low, high, index, lse, delta, repeats, width):
+    rows = queries.shape[0]
+    blocks = pairs.shape[0] // rows
+    whole = lambda shape: pl.BlockSpec(shape, lambda j, kind: (0,) * len(shape))
+    return pl.pallas_call(
+        lambda *refs: attend_back_kernel(repeats, width, *refs),
+        grid_spec=pltpu.PrefetchScalarGridSpec(
+            num_scalar_prefetch=1,
+            grid=(blocks,),
+            in_specs=[
+                whole((rows, repeats * width)),
+                pl.BlockSpec((rows, 2 * width), lambda j, kind: (j, 0)),
+                whole((rows, repeats * width)),
+                whole((1, rows)),
+                whole((1, rows)),
+                pl.BlockSpec((1, rows, 1), lambda j, kind: (j, 0, 0)),
+                whole((repeats, 1, rows)),
+                whole((repeats, 1, rows)),
+            ],
+            out_specs=[
+                whole((rows, repeats * width)),
+                pl.BlockSpec((rows, 2 * width), lambda j, kind: (j, 0)),
+            ],
+        ),
+        out_shape=[
+            jax.ShapeDtypeStruct((rows, repeats * width), F32),
+            jax.ShapeDtypeStruct((blocks * rows, 2 * width), BF),
+        ],
+        compiler_params=pltpu.CompilerParams(vmem_limit_bytes=40 * 2**20),
+        cost_estimate=pl.CostEstimate(
+            flops=10 * repeats * width * rows * rows * 7,
+            bytes_accessed=20 * 2**20,
+            transcendentals=repeats * rows * rows * 7,
+        ),
+        name="attend_back",
+    )(kind, queries, pairs, upstream, low, high, index, lse, delta)
 
 
 def local(
@@ -229,7 +395,6 @@
     head = lax.axis_index("head")
     own_rows = tokens.shape[0]
     rows = own_rows * heads
-    window = min((SEQ + rows - 2) // rows + 1, blocks)
     width = HEAD_WIDTH
     repeats = QUERY_HEADS_ALL // KEY_VALUE_HEADS
     query_cols = query_weight.shape[1]
@@ -239,10 +404,17 @@
     index = slots(jnp.arange(blocks * rows, dtype=jnp.int32).reshape(blocks, heads, own_rows), head)
     own_seg = lax.dynamic_index_in_dim(segs, blk, 0, False)
     own_pos = lax.dynamic_index_in_dim(poss, blk, 0, False)
-    own_index = lax.dynamic_index_in_dim(index, blk, 0, False)
-    first = jnp.maximum(blk - (window - 1), 0)
-    key_seg = lax.dynamic_slice_in_dim(segs, first, window, 0)
-    key_index = lax.dynamic_slice_in_dim(index, first, window, 0)
+    high = lax.dynamic_index_in_dim(index, blk, 0, False)
+    low = jnp.sum(
+        (segment_ids[None, :] < own_seg[:, None]).astype(jnp.int32), axis=1
+    )
+    block_seg = segment_ids.reshape(blocks, rows)
+    seg_first, seg_last = block_seg[:, 0], block_seg[:, -1]
+    ids = jnp.arange(blocks, dtype=jnp.int32)
+    some = (ids <= blk) & (seg_last >= seg_first[blk])
+    every = (ids < blk) & (seg_first == seg_last[blk])
+    kind = jnp.where(every, 1, jnp.where(some, 2, 0)).astype(jnp.int32)
+    table = rotary_table(own_pos, width)
 
     qkv_full, qkv_steps = ring_gather(
         jnp.concatenate([query_weight, key_matrix, value_matrix], axis=1)
@@ -261,42 +433,21 @@
     source = source_all[:own_rows]
     inverse_one = inverse_all[:own_rows]
     linear = simple_product(normed_all, qkv_full)
-    table = rotary_table(own_pos, width)
-    queries = apply_rotary(
-        linear[:, :query_cols].reshape(rows, repeats, width), table, 1.0
-    ).astype(BF)
+    score_scale = 1.0 / math.sqrt(width)
+    queries = (
+        apply_rotary(linear[:, :query_cols].reshape(rows, repeats, width), table, 1.0).astype(BF)
+        * score_scale
+    ).reshape(rows, query_cols)
     key_rot = apply_rotary(
         linear[:, query_cols : query_cols + width].reshape(rows, 1, width), table, 1.0
     ).reshape(rows, width)
     pair = jnp.concatenate(
         [key_rot.astype(BF), linear[:, query_cols + width :].astype(BF)], axis=1
     )
-    pairs_all, _ = ring_gather(pair)
-    pairs = lax.dynamic_slice_in_dim(pairs_all, first * rows, window * rows, 0)
-    masks = [
-        (own_seg[:, None] == key_seg[j][None, :]) & (key_index[j][None, :] <= own_index[:, None])
-        for j in range(window)
-    ]
-    key_parts = [pairs[j * rows : (j + 1) * rows, :width] for j in range(window)]
-    value_parts = [pairs[j * rows : (j + 1) * rows, width:] for j in range(window)]
-    run_max = jnp.full((repeats, rows), MASKED, F32)
-    run_total = jnp.zeros((repeats, rows), F32)
-    for j in range(window):
-        scores = block_scores(queries, key_parts[j], masks[j])
-        new_max = jnp.maximum(run_max, jnp.max(scores, axis=-1))
-        run_total = run_total * jnp.exp(run_max - new_max) + jnp.sum(
-            jnp.where(masks[j][None], jnp.exp(scores - new_max[..., None]), 0.0), axis=-1
-        )
-        run_max = new_max
-    log_total = run_max + jnp.log(run_total)
-    attn_full = jnp.zeros((rows, repeats, width), F32)
-    for j in range(window):
-        scores = block_scores(queries, key_parts[j], masks[j])
-        probs = jnp.exp(scores - log_total[..., None]).astype(BF)
-        attn_full = attn_full + jnp.einsum(
-            "rqk,kd->qrd", probs, value_parts[j], preferred_element_type=F32
-        )
-    attn_low = attn_full.reshape(rows, query_cols).astype(BF)
+    pairs, _ = ring_gather(pair)
+    index = index.reshape(blocks, 1, rows)
+    attn_full, lse = attend(kind, queries, pairs, low[:, None], high[:, None], index, repeats, width)
+    attn_low = attn_full.astype(BF)
     residual = source + head_sum(times_rows(attn_low, out_full))
 
     inverse_two = norm_scale(residual)
@@ -327,34 +478,29 @@
     branch_all = head_gather(residual_grad.astype(BF))
     out_grad = ring_sum(outer_sum(branch_all, attn_low).astype(BF)).T
 
-    attn_grad = simple_product(branch_all, out_full).astype(BF).reshape(rows, repeats, width)
-    row_delta = jnp.einsum("qrd,qrd->rq", attn_grad.astype(F32), attn_full)
-    score_scale = 1.0 / math.sqrt(width)
-    query_rot_grad = jnp.zeros((rows, repeats, width), F32)
-    pair_grads = []
-    for j in range(window):
-        scores = block_scores(queries, key_parts[j], masks[j])
-        probs = jnp.exp(scores - log_total[..., None])
-        prob_grad = jnp.einsum("qrd,kd->rqk", attn_grad, value_parts[j], preferred_element_type=F32)
-        score_grad = (probs * (prob_grad - row_delta[..., None])).astype(BF)
-        query_rot_grad = (
-            query_rot_grad
-            + jnp.einsum("rqk,kd->qrd", score_grad, key_parts[j], preferred_element_type=F32)
-            * score_scale
-        )
-        key_grad = (
-            jnp.einsum("rqk,qrd->kd", score_grad, queries, preferred_element_type=F32) * score_scale
-        )
-        value_grad = jnp.einsum(
-            "rqk,qrd->kd", probs.astype(BF), attn_grad, preferred_element_type=F32
-        )
-        pair_grads.append(jnp.concatenate([key_grad, value_grad], axis=1).astype(BF))
-    pair_grad = jnp.zeros((blocks * rows, 2 * width), BF)
-    pair_grad = lax.dynamic_update_slice_in_dim(
-        pair_grad, jnp.concatenate(pair_grads, axis=0), first * rows, 0
+    attn_grad = simple_product(branch_all, out_full).astype(BF)
+    row_delta = jnp.sum(
+        (attn_grad.astype(F32) * attn_full).reshape(rows, repeats, width), axis=-1
+    ).T.reshape(repeats, 1, rows)
+    query_rot_grad, pair_grad = attend_back(
+        kind,
+        queries,
+        pairs,
+        attn_grad,
+        low[None, :],
+        high[None, :],
+        index.reshape(blocks, rows, 1),
+        lse.reshape(repeats, 1, rows),
+        row_delta,
+        repeats,
+        width,
     )
     pair_grad = ring_sum(pair_grad)
-    query_lin_grad = apply_rotary(query_rot_grad, table, -1.0).astype(BF).reshape(rows, query_cols)
+    query_lin_grad = (
+        apply_rotary(query_rot_grad.reshape(rows, repeats, width) * score_scale, table, -1.0)
+        .astype(BF)
+        .reshape(rows, query_cols)
+    )
     key_lin_grad = apply_rotary(pair_grad[:, :width].reshape(rows, 1, width), table, -1.0)
     pair_lin_grad = jnp.concatenate(
         [key_lin_grad.reshape(rows, width), pair_grad[:, width:]], axis=1

time: 1110 us -> 1080 us (0.973)
  matrix products: 226 us -> 130 us
  local copies, waits for them, and re-layouts: 162 us -> 213 us
  starting transfers between devices: 150 us -> 181 us
  waiting for transfers between devices: 443 us -> 421 us
  Pallas kernels: 0 us -> 19 us
    dot_general x42 -> x0, matrix products: 96.3 us -> none  [the longest x7 21.1 us: local(): jnp.einsum('rqk,kd->qrd', probs, value_parts[j], preferred_element_type=F32)]
    pallas_call x0 -> x2, Pallas kernels: none -> 19 us  [the longest x1 9.74 us: attend_back(): pl.pallas_call(lambda *refs: attend_back_kernel(repeats, width, *refs), g...]
    ppermute x18, waiting for transfers between devices: 139 us -> 123 us  [ring_gather(): left = lax.ppermute(left, 'blk', up)]
    ppermute x21, starting transfers between devices: 31.8 us -> 47.4 us  [ring_sum(): left = lax.ppermute(left, 'blk', up)]
    ppermute x7, starting transfers between devices: 7.38 us -> 22.4 us  [ring_sum(): left = lax.ppermute(far[:half], 'blk', up)]
    unnamed x268 -> x204, local copies, waits for them, and re-layouts: 12.9 us -> 24.7 us
  transfers between devices with their start and end apart: 133 -> 133, of which waited for: 51 -> 49; matrix products, arithmetic and copies ran while one was open for 39% -> 35% of each run, Pallas kernels for 0% -> 2%
where the time goes in v2:
time: 1080 us; the launch traced here: 1070 us
  waiting for transfers between devices  421 us (39%)
  local copies, waits for them, and re-layouts  213 us (20%)
  starting transfers between devices  181 us (17%)
  matrix products  130 us (12%)
  other arithmetic  108 us (10%)
  Pallas kernels  19 us (2%)
    ppermute x18, waiting for transfers between devices, ring_gather(): left = lax.ppermute(left, 'blk', up)  123 us
    ppermute x21, waiting for transfers between devices, ring_sum(): right = lax.ppermute(right, 'blk', down)  113 us
    ppermute x21, waiting for transfers between devices, ring_sum(): left = lax.ppermute(left, 'blk', up)  90.1 us
    dot_general x5, matrix products, simple_product(): return jnp.dot(matrix_a, matrix_b, preferred_element_type=F32)  50 us
    ppermute x29, waiting for transfers between devices, flip(): lax.ppermute(value, axis, [(i, i ^ bit) for i in range(lax.axis_size(axis...  48.6 us
    ppermute x21, starting transfers between devices, ring_sum(): left = lax.ppermute(left, 'blk', up)  47.4 us
    dot_general x6, matrix products, times_rows(): lax.dot_general(matrix_a, matrix_b, (((1,), (1,)), ((), ())), preferred_e...  43.1 us
    dot_general x6, matrix products, outer_sum(): lax.dot_general(matrix_a, matrix_b, (((0,), (0,)), ((), ())), preferred_e...  36.3 us
  transfers between devices with their start and end apart: 133, of which 49 were waited for; matrix products, arithmetic and copies ran while one was open for 35% of the time, Pallas kernels for 2%

profile of v2, /device:TPU:0, one launch (start us, length us, event | category | flops | bytes accessed | tf_op | source)
XLA Modules:
  0.0 1073.6 jit_solution(7772010499923014472)
XLA Ops:
  91.1 12.9 %collective-permute-done.23 = bf16[256,512]{0,1:T(8,128)(2,1)} collective-permute-done((bf16[256,512]{0,1:T(8,128)(2,1)}, bf16[256,512]{0,1:T(8,128)(2,1)}, u32[]{:S(2)}, u32[]{:S(2)}) %collective-permute-start.23) | collective-permute-done | bytes 262176 | tf_op jit(solution)/shard_map/ppermute | solution.py:58
  211.4 47.5 %collective-permute-done.17 = bf16[768,512]{1,0:T(8,128)(2,1)S(1)} collective-permute-done((bf16[768,512]{1,0:T(8,128)(2,1)}, bf16[768,512]{1,0:T(8,128)(2,1)S(1)}, u32[]{:S(2)}, u32[]{:S(2)}) %collective-permute-start.17) | collective-permute-done | bytes 786464 | tf_op jit(solution)/shard_map/ppermute | solution.py:58
  295.5 9.2 attend.1
  350.9 28.1 %collective-permute-done.45 = bf16[256,2048]{1,0:T(8,128)(2,1)} collective-permute-done((bf16[256,2048]{1,0:T(8,128)(2,1)}, bf16[256,2048]{1,0:T(8,128)(2,1)}, u32[]{:S(2)}, u32[]{:S(2)}) %collective-permute-start.45) | collective-permute-done | bytes 1048608 | tf_op jit(solution)/shard_map/ppermute | solution.py:58
  404.6 13.3 %collective-permute-done.51 = bf16[256,2048]{0,1:T(8,128)(2,1)} collective-permute-done((bf16[256,2048]{0,1:T(8,128)(2,1)}, bf16[256,2048]{0,1:T(8,128)(2,1)}, u32[]{:S(2)}, u32[]{:S(2)}) %collective-permute-start.51) | collective-permute-done | bytes 1048608 | tf_op jit(solution)/shard_map/ppermute | solution.py:58
  439.6 8.5 collective-permute-done.53
  468.4 11.2 %fusion.23 = f32[768,2048]{1,0:T(8,128)} fusion(bf16[2048,2048]{0,1:T(8,128)(2,1)} %constant_dynamic-update-slice_fusion, bf16[192,2048]{1,0:T(8,128)(2,1)S(1)} %copy-done.64, bf16[192,2048]{1,0:T(8,128)(2,1)} %collective-permute-done.59, bf16[192,2048]{1,0:T(8,128)(2,1)S(1)} %copy-done.62, bf16[192,2048]{1,0:T(8,128)(2,1)} %param.25), kind=kOutput, calls=%fused_computation.131 | convolution fusion | flops 6455033856 | bytes 17825792 | tf_op jit(solution)/shard_map/dot_general | solution.py:192
  480.9 11.2 %fusion.47 = f32[768,2048]{1,0:T(8,128)} fusion(bf16[2048,2048]{0,1:T(8,128)(2,1)} %constant_dynamic-update-slice_fusion.9, bf16[192,2048]{1,0:T(8,128)(2,1)S(1)} %get-tuple-element.163, bf16[192,2048]{1,0:T(8,128)(2,1)} %collective-permute-done.31, bf16[192,2048]{1,0:T(8,128)(2,1)S(1)} %get-tuple-element.162, bf16[192,2048]{1,0:T(8,128)(2,1)} %multiply_convert_fusion.4), kind=kOutput, calls=%fused_computation.309 | convolution fusion | flops 6455033856 | bytes 17825792 | tf_op jit(solution)/shard_map/dot_general | solution.py:192
  492.0 18.2 %multiply_convert_fusion.1 = (bf16[768,2048]{1,0:T(8,128)(2,1)}, bf16[768,2048]{1,0:T(8,128)(2,1)}, bf16[768,2048]{1,0:T(8,128)(2,1)}) fusion(f32[768,2048]{1,0:T(8,128)} %fusion.23, f32[768,2048]{1,0:T(8,128)} %fusion.47, bf16[2048,2048]{0,1:T(8,128)(2,1)} %constant_dynamic-update-slice_fusion.18, bf16[192,2048]{1,0:T(8,128)(2,1)} %copy-done.68, ...), kind=kOutput, calls=%fused_computation.7 | convolution fusion | flops 6478626816 | bytes 33554432 | tf_op jit(solution)/shard_map/dot_general | solution.py:192
  510.3 10.4 convolution_convert_fusion.3
  520.7 9.8 convolution_convert_fusion
  535.1 11.2 %fusion.59 = f32[768,2048]{1,0:T(8,128)} fusion(bf16[768,2048]{1,0:T(8,128)(2,1)S(1)} %copy-done.95, bf16[2048,2048]{0,1:T(8,128)(2,1)} %constant_dynamic-update-slice_fusion.9), kind=kOutput, calls=%fused_computation.320 | convolution fusion | flops 6442450944 | bytes 17825792 | tf_op jit(solution)/shard_map/dot_general | solution.py:202
  546.3 8.7 convolution_convert_fusion.1
  559.0 9.1 convolution_convert_fusion.2
  572.1 12.0 %add_convert_fusion = bf16[768,2048]{1,0:T(8,128)(2,1)S(1)} fusion(f32[768,2048]{1,0:T(8,128)} %fusion.59, bf16[768,2048]{1,0:T(8,128)(2,1)} %get-tuple-element.92, bf16[2048,2048]{0,1:T(8,128)(2,1)} %constant_dynamic-update-slice_fusion.18), kind=kOutput, calls=%fused_computation.5 | convolution fusion | flops 6445596672 | bytes 20971520 | tf_op jit(solution)/shard_map/dot_general | solution.py:202
  606.6 13.5 %collective-permute-done.126 = bf16[256,2048]{1,0:T(8,128)(2,1)S(1)} collective-permute-done((bf16[256,2048]{1,0:T(8,128)(2,1)S(1)}, bf16[256,2048]{1,0:T(8,128)(2,1)S(1)}, u32[]{:S(2)}, u32[]{:S(2)}) %collective-permute-start.126) | collective-permute-done | bytes 1048608 | tf_op jit(solution)/shard_map/ppermute | solution.py:99
  624.1 18.6 %collective-permute-done.118 = bf16[256,2048]{1,0:T(8,128)(2,1)S(1)} collective-permute-done((bf16[256,2048]{1,0:T(8,128)(2,1)S(1)}, bf16[256,2048]{1,0:T(8,128)(2,1)S(1)}, u32[]{:S(2)}, u32[]{:S(2)}) %collective-permute-start.118) | collective-permute-done | bytes 1048608 | tf_op jit(solution)/shard_map/ppermute | solution.py:99
  644.3 20.8 %collective-permute-done.110 = bf16[256,2048]{1,0:T(8,128)(2,1)S(1)} collective-permute-done((bf16[256,2048]{1,0:T(8,128)(2,1)S(1)}, bf16[256,2048]{1,0:T(8,128)(2,1)S(1)}, u32[]{:S(2)}, u32[]{:S(2)}) %collective-permute-start.110) | collective-permute-done | bytes 1048608 | tf_op jit(solution)/shard_map/ppermute | solution.py:99
  669.8 14.5 %collective-permute-done.106 = f32[1024]{0:T(1024)S(1)} collective-permute-done((f32[1024]{0:T(1024)S(1)}, f32[1024]{0:T(1024)S(1)}, u32[]{:S(2)}, u32[]{:S(2)}) %collective-permute-start.106) | collective-permute-done | bytes 4128 | tf_op jit(solution)/shard_map/ppermute | solution.py:104
  692.1 15.6 %collective-permute-done.107 = f32[512]{0:T(512)S(1)} collective-permute-done((f32[512]{0:T(512)S(1)}, f32[512]{0:T(512)S(1)}, u32[]{:S(2)}, u32[]{:S(2)}) %collective-permute-start.107) | collective-permute-done | bytes 2080 | tf_op jit(solution)/shard_map/ppermute | solution.py:104
  723.1 13.4 %collective-permute-done.114 = bf16[256,2048]{1,0:T(8,128)(2,1)S(1)} collective-permute-done((bf16[256,2048]{1,0:T(8,128)(2,1)S(1)}, bf16[256,2048]{1,0:T(8,128)(2,1)S(1)}, u32[]{:S(2)}, u32[]{:S(2)}) %collective-permute-start.114) | collective-permute-done | bytes 1048608 | tf_op jit(solution)/shard_map/ppermute | solution.py:100
  744.0 14.9 %collective-permute-done.131 = bf16[256,2048]{1,0:T(8,128)(2,1)S(1)} collective-permute-done((bf16[256,2048]{1,0:T(8,128)(2,1)S(1)}, bf16[256,2048]{1,0:T(8,128)(2,1)S(1)}, u32[]{:S(2)}, u32[]{:S(2)}) %collective-permute-start.131) | collective-permute-done | bytes 1048608 | tf_op jit(solution)/shard_map/ppermute | solution.py:100
  761.5 19.9 %collective-permute-done.123 = bf16[256,2048]{1,0:T(8,128)(2,1)S(1)} collective-permute-done((bf16[256,2048]{1,0:T(8,128)(2,1)S(1)}, bf16[256,2048]{1,0:T(8,128)(2,1)S(1)}, u32[]{:S(2)}, u32[]{:S(2)}) %collective-permute-start.123) | collective-permute-done | bytes 1048608 | tf_op jit(solution)/shard_map/ppermute | solution.py:100
  785.3 18.6 %collective-permute-done.115 = bf16[256,2048]{1,0:T(8,128)(2,1)S(1)} collective-permute-done((bf16[256,2048]{1,0:T(8,128)(2,1)S(1)}, bf16[256,2048]{1,0:T(8,128)(2,1)S(1)}, u32[]{:S(2)}, u32[]{:S(2)}) %collective-permute-start.115) | collective-permute-done | bytes 1048608 | tf_op jit(solution)/shard_map/ppermute | solution.py:100
  826.5 9.7 attend_back.1
  847.2 8.8 collective-permute-start.65
  869.0 8.4 collective-permute-start.66
  883.0 12.5 %collective-permute-done.66 = bf16[768,512]{1,0:T(8,128)(2,1)S(1)} collective-permute-done((bf16[768,512]{1,0:T(8,128)(2,1)S(1)}, bf16[768,512]{1,0:T(8,128)(2,1)S(1)}, u32[]{:S(2)}, u32[]{:S(2)}) %collective-permute-start.66) | collective-permute-done | bytes 786464 | tf_op jit(solution)/shard_map/ppermute | solution.py:99
  909.9 16.5 %collective-permute-done.98 = bf16[256,512]{1,0:T(8,128)(2,1)S(1)} collective-permute-done((bf16[256,512]{1,0:T(8,128)(2,1)S(1)}, bf16[256,512]{1,0:T(8,128)(2,1)S(1)}, u32[]{:S(2)}, u32[]{:S(2)}) %collective-permute-start.98) | collective-permute-done | bytes 262176 | tf_op jit(solution)/shard_map/ppermute | solution.py:99
  937.6 21.0 %collective-permute-done.85 = bf16[256,512]{1,0:T(8,128)(2,1)S(1)} collective-permute-done((bf16[256,512]{1,0:T(8,128)(2,1)S(1)}, bf16[256,512]{1,0:T(8,128)(2,1)S(1)}, u32[]{:S(2)}, u32[]{:S(2)}) %collective-permute-start.85) | collective-permute-done | bytes 262176 | tf_op jit(solution)/shard_map/ppermute | solution.py:100
  970.9 12.9 %collective-permute-done.71 = bf16[768,512]{1,0:T(8,128)(2,1)S(1)} collective-permute-done((bf16[768,512]{1,0:T(8,128)(2,1)S(1)}, bf16[768,512]{1,0:T(8,128)(2,1)S(1)}, u32[]{:S(2)}, u32[]{:S(2)}) %collective-permute-start.71) | collective-permute-done | bytes 786464 | tf_op jit(solution)/shard_map/ppermute | solution.py:100
  1058.4 9.6 collective-permute-done.74
  (716 shorter events, 600.3 us)
Async XLA Ops:
  59.0 61.5 %collective-permute-start.1 = (bf16[384,2048]{1,0:T(8,128)(2,1)}, bf16[384,2048]{1,0:T(8,128)(2,1)}, u32[]{:S(2)}, u32[]{:S(2)}) collective-permute-start(bf16[384,2048]{1,0:T(8,128)(2,1)} %pad_maximum_fusion.4), channel_id=1, source_target_pairs={{0,1},{1,0},{2,3},{3,2},{4,5},{5,4},{6,7},{7,6},{8,9},{9,8},{10,11... | collective-permute-start | bytes 4718600 | tf_op jit(solution)/shard_map/ppermute | solution.py:104
  75.0 79.4 %collective-permute-start.33 = (bf16[256,2048]{1,0:T(8,128)(2,1)}, bf16[256,2048]{1,0:T(8,128)(2,1)}, u32[]{:S(2)}, u32[]{:S(2)}) collective-permute-start(bf16[256,2048]{1,0:T(8,128)(2,1)} %param.20), channel_id=1, source_target_pairs={{0,8},{8,16},{16,24},{24,28},{28,20},{20,12},{12,4},{4,0},{1,9},{9... | collective-permute-start | bytes 3145736 | tf_op jit(solution)/shard_map/ppermute | solution.py:58
  90.4 64.5 %collective-permute-start.34 = (bf16[256,2048]{1,0:T(8,128)(2,1)}, bf16[256,2048]{1,0:T(8,128)(2,1)}, u32[]{:S(2)}, u32[]{:S(2)}) collective-permute-start(bf16[256,2048]{1,0:T(8,128)(2,1)} %param.20), channel_id=1, source_target_pairs={{8,0},{16,8},{24,16},{28,24},{20,28},{12,20},{4,12},{0,4},{9,1},{1... | collective-permute-start | bytes 3145736 | tf_op jit(solution)/shard_map/ppermute | solution.py:59
  154.4 51.9 %collective-permute-start.60 = (bf16[384,2048]{1,0:T(8,128)(2,1)}, bf16[384,2048]{1,0:T(8,128)(2,1)}, u32[]{:S(2)}, u32[]{:S(2)}) collective-permute-start(bf16[384,2048]{1,0:T(8,128)(2,1)} %pad_maximum_fusion.6), channel_id=1, source_target_pairs={{0,1},{1,0},{2,3},{3,2},{4,5},{5,4},{6,7},{7,6},{8,9},{9,8},{10,11... | collective-permute-start | bytes 4718600 | tf_op jit(solution)/shard_map/ppermute | solution.py:104
  182.9 91.2 %collective-permute-start.41 = (bf16[256,2048]{1,0:T(8,128)(2,1)}, bf16[256,2048]{1,0:T(8,128)(2,1)}, u32[]{:S(2)}, u32[]{:S(2)}) collective-permute-start(bf16[256,2048]{1,0:T(8,128)(2,1)} %param.21), channel_id=1, source_target_pairs={{0,8},{8,16},{16,24},{24,28},{28,20},{20,12},{12,4},{4,0},{1,9},{9... | collective-permute-start | bytes 3145736 | tf_op jit(solution)/shard_map/ppermute | solution.py:58
  193.8 75.2 %collective-permute-start.37 = (bf16[256,2048]{1,0:T(8,128)(2,1)}, bf16[256,2048]{1,0:T(8,128)(2,1)}, u32[]{:S(2)}, u32[]{:S(2)}) collective-permute-start(bf16[256,2048]{1,0:T(8,128)(2,1)} %collective-permute-done.35), channel_id=1, source_target_pairs={{0,8},{8,16},{16,24},{24,28},{28,20},{20,12},{12,4},{4,0},{1,9},{9... | collective-permute-start | bytes 3145736 | tf_op jit(solution)/shard_map/ppermute | solution.py:58
  197.5 61.3 %collective-permute-start.17 = (bf16[768,512]{1,0:T(8,128)(2,1)}, bf16[768,512]{1,0:T(8,128)(2,1)S(1)}, u32[]{:S(2)}, u32[]{:S(2)}) collective-permute-start(bf16[768,512]{1,0:T(8,128)(2,1)} %collective-permute-done.15), channel_id=1, source_target_pairs={{0,8},{8,16},{16,24},{24,28},{28,20},{20,12},{12,4},{4,0},{1,9},{9... | collective-permute-start | bytes 2359304 | tf_op jit(solution)/shard_map/ppermute | solution.py:58
  204.8 67.5 %collective-permute-start.38 = (bf16[256,2048]{1,0:T(8,128)(2,1)}, bf16[256,2048]{1,0:T(8,128)(2,1)S(1)}, u32[]{:S(2)}, u32[]{:S(2)}) collective-permute-start(bf16[256,2048]{1,0:T(8,128)(2,1)} %collective-permute-done.36), channel_id=1, source_target_pairs={{8,0},{16,8},{24,16},{28,24},{20,28},{12,20},{4,12},{0,4},{9,1},{1... | collective-permute-start | bytes 3145736 | tf_op jit(solution)/shard_map/ppermute | solution.py:59
  206.3 59.5 %collective-permute-start.18 = (bf16[768,512]{1,0:T(8,128)(2,1)}, bf16[768,512]{1,0:T(8,128)(2,1)S(1)}, u32[]{:S(2)}, u32[]{:S(2)}) collective-permute-start(bf16[768,512]{1,0:T(8,128)(2,1)} %collective-permute-done.16), channel_id=1, source_target_pairs={{8,0},{16,8},{24,16},{28,24},{20,28},{12,20},{4,12},{0,4},{9,1},{1... | collective-permute-start | bytes 2359304 | tf_op jit(solution)/shard_map/ppermute | solution.py:59
  272.3 46.8 %collective-permute-start.39 = (bf16[128,2048]{1,0:T(8,128)(2,1)}, bf16[128,2048]{1,0:T(8,128)(2,1)}, u32[]{:S(2)}, u32[]{:S(2)}) collective-permute-start(bf16[128,2048]{1,0:T(8,128)(2,1)} %slice.500), channel_id=1, source_target_pairs={{0,8},{8,16},{16,24},{24,28},{28,20},{20,12},{12,4},{4,0},{1,9},{9... | collective-permute-start | bytes 1572872 | tf_op jit(solution)/shard_map/ppermute | solution.py:64
  274.1 47.0 %collective-permute-start.40 = (bf16[128,2048]{1,0:T(8,128)(2,1)}, bf16[128,2048]{1,0:T(8,128)(2,1)}, u32[]{:S(2)}, u32[]{:S(2)}) collective-permute-start(bf16[128,2048]{1,0:T(8,128)(2,1)} %slice.501), channel_id=1, source_target_pairs={{8,0},{16,8},{24,16},{28,24},{20,28},{12,20},{4,12},{0,4},{9,1},{1... | collective-permute-start | bytes 1572872 | tf_op jit(solution)/shard_map/ppermute | solution.py:65
  290.5 46.9 %collective-permute-start.44 = (bf16[256,2048]{1,0:T(8,128)(2,1)}, bf16[256,2048]{1,0:T(8,128)(2,1)}, u32[]{:S(2)}, u32[]{:S(2)}) collective-permute-start(bf16[256,2048]{1,0:T(8,128)(2,1)} %collective-permute-done.42), channel_id=1, source_target_pairs={{8,0},{16,8},{24,16},{28,24},{20,28},{12,20},{4,12},{0,4},{9,1},{1... | collective-permute-start | bytes 3145736 | tf_op jit(solution)/shard_map/ppermute | solution.py:59
  327.1 64.9 %collective-permute-start.49 = (bf16[256,2048]{0,1:T(8,128)(2,1)}, bf16[256,2048]{0,1:T(8,128)(2,1)}, u32[]{:S(2)}, u32[]{:S(2)}) collective-permute-start(bf16[256,2048]{0,1:T(8,128)(2,1)} %bitcast.150), channel_id=1, source_target_pairs={{0,8},{8,16},{16,24},{24,28},{28,20},{20,12},{12,4},{4,0},{1,9},{9... | collective-permute-start | bytes 3145736 | tf_op jit(solution)/shard_map/ppermute | solution.py:58
  333.1 61.8 %collective-permute-start.50 = (bf16[256,2048]{0,1:T(8,128)(2,1)}, bf16[256,2048]{0,1:T(8,128)(2,1)}, u32[]{:S(2)}, u32[]{:S(2)}) collective-permute-start(bf16[256,2048]{0,1:T(8,128)(2,1)} %bitcast.151), channel_id=1, source_target_pairs={{8,0},{16,8},{24,16},{28,24},{20,28},{12,20},{4,12},{0,4},{9,1},{1... | collective-permute-start | bytes 3145736 | tf_op jit(solution)/shard_map/ppermute | solution.py:59
  350.4 51.6 %collective-permute-start.30 = (bf16[192,2048]{1,0:T(8,128)(2,1)}, bf16[192,2048]{1,0:T(8,128)(2,1)}, u32[]{:S(2)}, u32[]{:S(2)}) collective-permute-start(bf16[192,2048]{1,0:T(8,128)(2,1)} %fusion.12), channel_id=1, source_target_pairs={{0,2},{1,3},{2,0},{3,1},{4,6},{5,7},{6,4},{7,5},{8,10},{9,11},{10,... | collective-permute-start | bytes 2359304 | tf_op jit(solution)/shard_map/ppermute | solution.py:104
  385.1 45.8 %collective-permute-start.48 = (bf16[128,2048]{1,0:T(8,128)(2,1)}, bf16[128,2048]{1,0:T(8,128)(2,1)}, u32[]{:S(2)}, u32[]{:S(2)}) collective-permute-start(bf16[128,2048]{1,0:T(8,128)(2,1)} %slice.503), channel_id=1, source_target_pairs={{8,0},{16,8},{24,16},{28,24},{20,28},{12,20},{4,12},{0,4},{9,1},{1... | collective-permute-start | bytes 1572872 | tf_op jit(solution)/shard_map/ppermute | solution.py:65
  531.9 52.5 %collective-permute-start.125 = (bf16[128,2048]{1,0:T(8,128)(2,1)}, bf16[128,2048]{1,0:T(8,128)(2,1)S(1)}, u32[]{:S(2)}, u32[]{:S(2)}) collective-permute-start(bf16[128,2048]{1,0:T(8,128)(2,1)} %get-tuple-element.99), channel_id=1, source_target_pairs={{0,8},{8,16},{16,24},{24,28},{28,20},{20,12},{12,4},{4,0},{1,9},{9... | collective-permute-start | bytes 1572872 | tf_op jit(solution)/shard_map/ppermute | solution.py:87
  534.4 51.2 %collective-permute-start.129 = (bf16[128,2048]{1,0:T(8,128)(2,1)}, bf16[128,2048]{1,0:T(8,128)(2,1)}, u32[]{:S(2)}, u32[]{:S(2)}) collective-permute-start(bf16[128,2048]{1,0:T(8,128)(2,1)} %get-tuple-element.101), channel_id=1, source_target_pairs={{8,0},{16,8},{24,16},{28,24},{20,28},{12,20},{4,12},{0,4},{9,1},{1... | collective-permute-start | bytes 1572872 | tf_op jit(solution)/shard_map/ppermute | solution.py:88
  589.1 123.7 %collective-permute-start.130 = (bf16[256,2048]{1,0:T(8,128)(2,1)}, bf16[256,2048]{1,0:T(8,128)(2,1)}, u32[]{:S(2)}, u32[]{:S(2)}) collective-permute-start(bf16[256,2048]{1,0:T(8,128)(2,1)} %pad_maximum_fusion.13), channel_id=1, source_target_pairs={{8,0},{16,8},{24,16},{28,24},{20,28},{12,20},{4,12},{0,4},{9,1},{1... | collective-permute-start | bytes 3145736 | tf_op jit(solution)/shard_map/ppermute | solution.py:100
  600.0 117.6 %collective-permute-start.122 = (bf16[256,2048]{1,0:T(8,128)(2,1)}, bf16[256,2048]{1,0:T(8,128)(2,1)}, u32[]{:S(2)}, u32[]{:S(2)}) collective-permute-start(bf16[256,2048]{1,0:T(8,128)(2,1)} %pad_maximum_fusion.11), channel_id=1, source_target_pairs={{8,0},{16,8},{24,16},{28,24},{20,28},{12,20},{4,12},{0,4},{9,1},{1... | collective-permute-start | bytes 3145736 | tf_op jit(solution)/shard_map/ppermute | solution.py:100
  621.7 91.2 %collective-permute-start.127 = (bf16[256,2048]{1,0:T(8,128)(2,1)S(1)}, bf16[256,2048]{1,0:T(8,128)(2,1)}, u32[]{:S(2)}, u32[]{:S(2)}) collective-permute-start(bf16[256,2048]{1,0:T(8,128)(2,1)S(1)} %add_convert_fusion.4), channel_id=1, source_target_pairs={{0,8},{8,16},{16,24},{24,28},{28,20},{20,12},{12,4},{4,0},{1,9},{9... | collective-permute-start | bytes 3145736 | tf_op jit(solution)/shard_map/ppermute | solution.py:99
  741.2 62.7 %collective-permute-start.115 = (bf16[256,2048]{1,0:T(8,128)(2,1)S(1)}, bf16[256,2048]{1,0:T(8,128)(2,1)S(1)}, u32[]{:S(2)}, u32[]{:S(2)}) collective-permute-start(bf16[256,2048]{1,0:T(8,128)(2,1)S(1)} %get-tuple-element.112), channel_id=1, source_target_pairs={{8,0},{16,8},{24,16},{28,24},{20,28},{12,20},{4,12},{0,4},{9,1},{1... | collective-permute-start | bytes 3145736 | tf_op jit(solution)/shard_map/ppermute | solution.py:100
  741.4 66.4 %collective-permute-start.64 = (bf16[384,2048]{1,0:T(8,128)(2,1)S(1)}, bf16[384,2048]{1,0:T(8,128)(2,1)S(1)}, u32[]{:S(2)}, u32[]{:S(2)}) collective-permute-start(bf16[384,2048]{1,0:T(8,128)(2,1)S(1)} %pad_maximum_fusion.7), channel_id=1, source_target_pairs={{0,1},{1,0},{2,3},{3,2},{4,5},{5,4},{6,7},{7,6},{8,9},{9,8},{10,11... | collective-permute-start | bytes 4718600 | tf_op jit(solution)/shard_map/ppermute | solution.py:104
  742.0 105.2 %collective-permute-start.128 = (bf16[256,2048]{1,0:T(8,128)(2,1)}, bf16[256,2048]{1,0:T(8,128)(2,1)}, u32[]{:S(2)}, u32[]{:S(2)}) collective-permute-start(bf16[256,2048]{1,0:T(8,128)(2,1)} %get-tuple-element.95), channel_id=1, source_target_pairs={{0,8},{8,16},{16,24},{24,28},{28,20},{20,12},{12,4},{4,0},{1,9},{9... | collective-permute-start | bytes 3145736 | tf_op jit(solution)/shard_map/ppermute | solution.py:99
  759.0 174.0 %collective-permute-start.120 = (bf16[256,2048]{1,0:T(8,128)(2,1)}, bf16[256,2048]{1,0:T(8,128)(2,1)}, u32[]{:S(2)}, u32[]{:S(2)}) collective-permute-start(bf16[256,2048]{1,0:T(8,128)(2,1)} %get-tuple-element.103), channel_id=1, source_target_pairs={{0,8},{8,16},{16,24},{24,28},{28,20},{20,12},{12,4},{4,0},{1,9},{9... | collective-permute-start | bytes 3145736 | tf_op jit(solution)/shard_map/ppermute | solution.py:99
  781.4 74.6 %collective-permute-start.132 = (bf16[256,2048]{1,0:T(8,128)(2,1)}, bf16[256,2048]{1,0:T(8,128)(2,1)}, u32[]{:S(2)}, u32[]{:S(2)}) collective-permute-start(bf16[256,2048]{1,0:T(8,128)(2,1)} %add_convert_fusion.1), channel_id=1, source_target_pairs={{8,0},{16,8},{24,16},{28,24},{20,28},{12,20},{4,12},{0,4},{9,1},{1... | collective-permute-start | bytes 3145736 | tf_op jit(solution)/shard_map/ppermute | solution.py:100
  803.9 129.3 %collective-permute-start.124 = (bf16[256,2048]{1,0:T(8,128)(2,1)}, bf16[256,2048]{1,0:T(8,128)(2,1)}, u32[]{:S(2)}, u32[]{:S(2)}) collective-permute-start(bf16[256,2048]{1,0:T(8,128)(2,1)} %add_convert_fusion.5), channel_id=1, source_target_pairs={{8,0},{16,8},{24,16},{28,24},{20,28},{12,20},{4,12},{0,4},{9,1},{1... | collective-permute-start | bytes 3145736 | tf_op jit(solution)/shard_map/ppermute | solution.py:100
  812.2 54.9 %collective-permute-start.100 = (bf16[128,512]{1,0:T(8,128)(2,1)}, bf16[128,512]{1,0:T(8,128)(2,1)}, u32[]{:S(2)}, u32[]{:S(2)}) collective-permute-start(bf16[128,512]{1,0:T(8,128)(2,1)} %get-tuple-element.139), channel_id=1, source_target_pairs={{8,0},{16,8},{24,16},{28,24},{20,28},{12,20},{4,12},{0,4},{9,1},{1... | collective-permute-start | bytes 393224 | tf_op jit(solution)/shard_map/ppermute | solution.py:88
  926.4 58.5 %collective-permute-start.112 = (bf16[256,2048]{1,0:T(8,128)(2,1)S(1)}, bf16[256,2048]{1,0:T(8,128)(2,1)S(1)}, u32[]{:S(2)}, u32[]{:S(2)}) collective-permute-start(bf16[256,2048]{1,0:T(8,128)(2,1)S(1)} %copy-done.58), channel_id=1, source_target_pairs={{0,8},{8,16},{16,24},{24,28},{28,20},{20,12},{12,4},{4,0},{1,9},{9... | collective-permute-start | bytes 3145736 | tf_op jit(solution)/shard_map/ppermute | solution.py:99
  929.7 59.2 %collective-permute-start.116 = (bf16[256,2048]{1,0:T(8,128)(2,1)S(1)}, bf16[256,2048]{1,0:T(8,128)(2,1)S(1)}, u32[]{:S(2)}, u32[]{:S(2)}) collective-permute-start(bf16[256,2048]{1,0:T(8,128)(2,1)S(1)} %copy-done.56), channel_id=1, source_target_pairs={{8,0},{16,8},{24,16},{28,24},{20,28},{12,20},{4,12},{0,4},{9,1},{1... | collective-permute-start | bytes 3145736 | tf_op jit(solution)/shard_map/ppermute | solution.py:100
  993.9 57.5 %collective-permute-start.83 = (bf16[256,512]{1,0:T(8,128)(2,1)}, bf16[256,512]{1,0:T(8,128)(2,1)S(1)}, u32[]{:S(2)}, u32[]{:S(2)}) collective-permute-start(bf16[256,512]{1,0:T(8,128)(2,1)} %get-tuple-element.149), channel_id=1, source_target_pairs={{0,8},{8,16},{16,24},{24,28},{28,20},{20,12},{12,4},{4,0},{1,9},{9... | collective-permute-start | bytes 786440 | tf_op jit(solution)/shard_map/ppermute | solution.py:99
  997.4 54.4 %collective-permute-start.87 = (bf16[256,512]{1,0:T(8,128)(2,1)S(1)}, bf16[256,512]{1,0:T(8,128)(2,1)S(1)}, u32[]{:S(2)}, u32[]{:S(2)}) collective-permute-start(bf16[256,512]{1,0:T(8,128)(2,1)S(1)} %add_convert_fusion.35), channel_id=1, source_target_pairs={{8,0},{16,8},{24,16},{28,24},{20,28},{12,20},{4,12},{0,4},{9,1},{1... | collective-permute-start | bytes 786440 | tf_op jit(solution)/shard_map/ppermute | solution.py:100
  (200 other events, 3829.2 us)

commit v3 on v2

--- a/solution.py
+++ b/solution.py
@@ -15,6 +15,7 @@
 EPSILON = 1e-06
 THETA_BASE = 1000042.0
 MASKED = -1e30
+PAIR_BIT = 1
 BF = jnp.bfloat16
 F32 = jnp.float32
 
@@ -42,82 +43,137 @@
     return up, [(b, a) for a, b in up]
 
 
-def ring_gather(shard):
-    count = lax.axis_size("blk")
-    me = lax.axis_index("blk")
-    place = cycle_place(me, count)
-    up, down = ring_routes(count)
-    rows = shard.shape[0]
-    half = rows // 2
-    out = jnp.zeros((count * rows, *shard.shape[1:]), shard.dtype)
-    out = lax.dynamic_update_slice_in_dim(out, shard, me * rows, 0)
-    left, right = shard, shard
-    steps = []
-    for step in range(1, count // 2 + 1):
-        if step < count // 2:
-            left = lax.ppermute(left, "blk", up)
-            right = lax.ppermute(right, "blk", down)
-            low, high = cycle_owner(place - step, count), cycle_owner(place + step, count)
-            out = lax.dynamic_update_slice_in_dim(out, left, low * rows, 0)
-            out = lax.dynamic_update_slice_in_dim(out, right, high * rows, 0)
+def barrier(*values):
+    return lax.optimization_barrier(values)
+
+
+def join(movers, *values):
+    flights = [mover.flight() for mover in movers]
+    flat = [value for flight in flights for value in flight]
+    done = lax.optimization_barrier((*flat, *values))
+    place = 0
+    for mover, flight in zip(movers, flights):
+        mover.land(list(done[place : place + len(flight)]))
+        place += len(flight)
+    rest = done[place:]
+    return rest[0] if len(rest) == 1 else rest
+
+
+class RingGather:
+    def __init__(self, shard):
+        self.count = lax.axis_size("blk")
+        self.me = lax.axis_index("blk")
+        self.place = cycle_place(self.me, self.count)
+        self.routes = ring_routes(self.count)
+        self.shard = self.left = self.right = shard
+        self.step = 0
+        self.parts = []
+
+    def go(self):
+        self.step += 1
+        half = self.shard.shape[0] // 2
+        left, right = self.left, self.right
+        if self.step == self.count // 2:
+            left, right = left[:half], right[half:]
+        self.left = lax.ppermute(left, "blk", self.routes[0])
+        self.right = lax.ppermute(right, "blk", self.routes[1])
+
+    def rest(self):
+        while self.step < self.count // 2 - 1:
+            self.go()
+            join([self])
+
+    def flight(self):
+        return [self.left, self.right]
+
+    def land(self, values):
+        self.left, self.right = values
+        self.parts.append((self.step, self.left, self.right))
+
+    def full(self):
+        rows = self.shard.shape[0]
+        out = jnp.zeros((self.count * rows, *self.shard.shape[1:]), self.shard.dtype)
+        out = lax.dynamic_update_slice_in_dim(out, self.shard, self.me * rows, 0)
+        for step, left, right in self.parts:
+            low = cycle_owner(self.place - step, self.count) * rows
+            high = cycle_owner(self.place + step, self.count) * rows
+            if step == self.count // 2:
+                high = low + rows // 2
+            out = lax.dynamic_update_slice_in_dim(out, left, low, 0)
+            out = lax.dynamic_update_slice_in_dim(out, right, high, 0)
+        return out
+
+
+class RingSum:
+    def __init__(self, blocks):
+        self.count = lax.axis_size("blk")
+        self.place = cycle_place(lax.axis_index("blk"), self.count)
+        self.routes = ring_routes(self.count)
+        self.blocks = blocks
+        self.rows = blocks.shape[0] // self.count
+        self.step = self.count // 2
+
+    def part(self, offset):
+        return lax.dynamic_slice_in_dim(
+            self.blocks, cycle_owner(self.place + offset, self.count) * self.rows, self.rows, 0
+        )
+
+    def go(self):
+        half = self.rows // 2
+        if self.step == self.count // 2:
+            far = self.part(self.step)
+            left, right = far[:half], far[half:]
         else:
-            left = lax.ppermute(left[:half], "blk", up)
-            right = lax.ppermute(right[half:], "blk", down)
-            far = cycle_owner(place - step, count)
-            out = lax.dynamic_update_slice_in_dim(out, left, far * rows, 0)
-            out = lax.dynamic_update_slice_in_dim(out, right, far * rows + half, 0)
-        steps.append((left, right))
-    return out, steps
-
-
-def ring_sum(blocks):
-    count = lax.axis_size("blk")
-    me = lax.axis_index("blk")
-    place = cycle_place(me, count)
-    up, down = ring_routes(count)
-    rows = blocks.shape[0] // count
-    half = rows // 2
-
-    def part(offset):
-        return lax.dynamic_slice_in_dim(
-            blocks, cycle_owner(place + offset, count) * rows, rows, 0
-        )
-
-    far = part(count // 2)
-    left = lax.ppermute(far[:half], "blk", up)
-    right = lax.ppermute(far[half:], "blk", down)
-    for step in range(count // 2 - 1, -1, -1):
-        if step == count // 2 - 1:
-            low, high = part(step), part(-step)
-            left = jnp.concatenate([(low[:half].astype(F32) + left.astype(F32)).astype(BF), low[half:]])
-            right = jnp.concatenate([high[:half], (high[half:].astype(F32) + right.astype(F32)).astype(BF)])
-        elif step > 0:
-            left = (part(step).astype(F32) + left.astype(F32)).astype(BF)
-            right = (part(-step).astype(F32) + right.astype(F32)).astype(BF)
-        else:
-            return part(0).astype(F32) + left.astype(F32) + right.astype(F32)
-        left = lax.ppermute(left, "blk", up)
-        right = lax.ppermute(right, "blk", down)
+            low, high = self.part(self.step), self.part(-self.step)
+            left, right = self.left.astype(F32), self.right.astype(F32)
+            if self.step == self.count // 2 - 1:
+                left = jnp.concatenate([(low[:half].astype(F32) + left).astype(BF), low[half:]])
+                right = jnp.concatenate([high[:half], (high[half:].astype(F32) + right).astype(BF)])
+            else:
+                left = (low.astype(F32) + left).astype(BF)
+                right = (high.astype(F32) + right).astype(BF)
+        self.left = lax.ppermute(left, "blk", self.routes[0])
+        self.right = lax.ppermute(right, "blk", self.routes[1])
+        self.step -= 1
+        return left, right
+
+    def rest(self):
+        while self.step > 1:
+            self.go()
+            join([self])
+
+    def flight(self):
+        return [self.left, self.right]
+
+    def land(self, values):
+        self.left, self.right = values
+
+    def total(self):
+        return self.part(0).astype(F32) + self.left.astype(F32) + self.right.astype(F32)
 
 
 def flip(value, axis, bit):
     return lax.ppermute(value, axis, [(i, i ^ bit) for i in range(lax.axis_size(axis))])
 
 
-def head_gather(rows):
-    other = flip(rows, "head", 2)
+def head_rest(rows, other):
     pair = jnp.concatenate([rows, other], axis=0)
-    beside = flip(pair, "head", 1)
+    return rows, other, flip(pair, "head", 1)
+
+
+def head_all(rows, other, beside):
     count = rows.shape[0]
     return jnp.concatenate([rows, beside[:count], other, beside[count:]], axis=0)
 
 
-def head_sum(partial):
+def head_near(partial):
     low = partial.astype(BF).reshape(2, 2, partial.shape[0] // 4, *partial.shape[1:])
-    near = flip(low[:, 1], "head", 1)
-    pair = low[:, 0].astype(F32) + near.astype(F32)
-    far = flip(pair[1].astype(BF), "head", 2)
-    return pair[0] + far.astype(F32)
+    return low[:, 0], flip(low[:, 1], "head", 1)
+
+
+def head_far(kept, near):
+    pair = kept.astype(F32) + near.astype(F32)
+    return pair[0], flip(pair[1].astype(BF), "head", 2)
 
 
 def slots(values, head_index):
@@ -127,55 +183,39 @@
     return values.reshape(values.shape[0], -1)
 
 
-def gain_gather(gains):
-    count = lax.axis_size("blk")
+def gain_hop(gains, bit):
+    if bit >= lax.axis_size("blk"):
+        return gains
     me = lax.axis_index("blk")
-    bit = 1
-    while bit < count:
-        other = flip(gains, "blk", bit)
-        low = jnp.concatenate([gains, other], axis=1)
-        high = jnp.concatenate([other, gains], axis=1)
-        gains = jnp.where((me // bit) % 2 == 0, low, high)
-        bit *= 2
-    return gains
-
-
-def gain_sum(grad):
-    for bit in (1, 2):
-        grad = grad + flip(grad, "head", bit)
-    count = lax.axis_size("blk")
-    me = lax.axis_index("blk")
-    bit = count // 2
-    while bit:
-        size = grad.shape[0] // 2
-        upper = (me // bit) % 2 == 1
-        keep = jnp.where(upper, grad[size:], grad[:size])
-        send = jnp.where(upper, grad[:size], grad[size:])
-        grad = keep + flip(send, "blk", bit)
-        bit //= 2
-    return grad
+    other = flip(gains, "blk", bit)
+    low = jnp.concatenate([gains, other], axis=1)
+    high = jnp.concatenate([other, gains], axis=1)
+    return jnp.where((me // bit) % 2 == 0, low, high)
+
+
+def gain_back(grads, bit):
+    low, high = jnp.split(grads, 2, axis=1)
+    upper = (lax.axis_index("blk") // bit) % 2 == 1
+    return jnp.where(upper, high, low) + flip(jnp.where(upper, low, high), "blk", bit)
 
 
 def rotary_table(token_pos, width):
     half_size = width // 2
     frequency = THETA_BASE ** (-2.0 * jnp.arange(half_size, dtype=F32) / width)
     angles = token_pos.astype(F32)[:, None] * frequency[None, :]
-    return jnp.cos(angles)[:, None, :], jnp.sin(angles)[:, None, :]
+    return jnp.cos(angles), jnp.sin(angles)
 
 
 def apply_rotary(values, table, direction):
     cosine, sine_part = table
     sine_part = sine_part * direction
-    half_size = values.shape[-1] // 2
-    first_half = values[..., :half_size]
-    second_half = values[..., half_size:]
-    return jnp.concatenate(
-        [
-            first_half * cosine - second_half * sine_part,
-            second_half * cosine + first_half * sine_part,
-        ],
-        axis=-1,
-    )
+    half = cosine.shape[1]
+    out = []
+    for start in range(0, values.shape[1], 2 * half):
+        first = values[:, start : start + half]
+        second = values[:, start + half : start + 2 * half]
+        out += [first * cosine - second * sine_part, second * cosine + first * sine_part]
+    return jnp.concatenate(out, axis=1)
 
 
 def norm_scale(values):
@@ -204,7 +244,110 @@
     )
 
 
+def pair_side(blk):
+    return jnp.where((blk & PAIR_BIT) != 0, 1, 0)
+
+
+def halves(shard, axis):
+    side = pair_side(lax.axis_index("blk"))
+    low, high = jnp.split(shard, 2, axis=axis)
+    return jnp.where(side == 0, low, high), jnp.where(side == 0, high, low)
+
+
+def plane_groups():
+    count = lax.axis_size("blk")
+    return [[i for i in range(count) if i & PAIR_BIT == side] for side in (0, PAIR_BIT)]
+
+
+def group_gather(rows):
+    return lax.all_gather(rows, "blk", axis=0, tiled=True, axis_index_groups=plane_groups())
+
+
+def group_sum(partial):
+    return lax.psum_scatter(
+        partial.astype(BF),
+        "blk",
+        scatter_dimension=0,
+        tiled=True,
+        axis_index_groups=plane_groups(),
+    )
+
+
+def send_half(both):
+    mine, other = halves(both, 0)
+    return mine, flip(other, "blk", PAIR_BIT)
+
+
+def narrow_half(mine, other):
+    side = pair_side(lax.axis_index("blk"))
+    mine, other = mine.astype(F32), other.astype(F32)
+    return jnp.concatenate(
+        [jnp.where(side == 0, mine, other), jnp.where(side == 0, other, mine)], axis=1
+    )
+
+
+def place_half(mine, other):
+    side = pair_side(lax.axis_index("blk"))
+    return jnp.concatenate(
+        [jnp.where(side == 0, mine, other), jnp.where(side == 0, other, mine)], axis=0
+    )
+
+
+def wide_near(rows):
+    return flip(rows, "head", 2), flip(rows, "blk", PAIR_BIT)
+
+
+def wide_far(near_y, near_z):
+    half = near_y.shape[1] // 2
+    return flip(near_z[:, :half], "head", 2), flip(near_y[:, half:], "blk", PAIR_BIT)
+
+
+def wide_rest(rows, near_y, near_z, far):
+    far = jnp.concatenate(far, axis=1)
+    trio = jnp.concatenate([rows, near_y, near_z], axis=0)
+    return jnp.concatenate([trio, flip(trio, "head", 1), far, flip(far, "head", 1)], axis=0)
+
+
+class WideSum:
+    def __init__(self, partial):
+        self.rows = partial.shape[0] // 8
+        rows = self.rows
+        self.far, self.trio = partial[6 * rows : 7 * rows], partial[: 3 * rows]
+        self.moving = [
+            flip(partial[7 * rows :], "head", 1),
+            flip(partial[3 * rows : 6 * rows], "head", 1),
+        ]
+
+    def flight(self):
+        return self.moving
+
+    def land(self, values):
+        self.moving = values
+
+    def go_far(self):
+        far = self.far.astype(F32) + self.moving[0].astype(F32)
+        self.trio = self.trio.astype(F32) + self.moving[1].astype(F32)
+        half = far.shape[1] // 2
+        sent = far[:, :half].astype(BF), far[:, half:].astype(BF)
+        self.moving = [flip(sent[0], "head", 2), flip(sent[1], "blk", PAIR_BIT)]
+        return sent
+
+    def go_near(self):
+        rows, half = self.rows, self.trio.shape[1] // 2
+        to_z, to_y = (value.astype(F32) for value in self.moving)
+        near_y, near_z = self.trio[rows : 2 * rows], self.trio[2 * rows :]
+        near_z = jnp.concatenate([near_z[:, :half] + to_z, near_z[:, half:]], axis=1)
+        near_y = jnp.concatenate([near_y[:, :half], near_y[:, half:] + to_y], axis=1)
+        sent = near_y.astype(BF), near_z.astype(BF)
+        self.moving = [flip(sent[0], "head", 2), flip(sent[1], "blk", PAIR_BIT)]
+        return sent
+
+    def total(self):
+        return self.trio[: self.rows] + self.moving[0].astype(F32) + self.moving[1].astype(F32)
+
+
 CHUNK = 256
+COST = 40
 
 
 def contract(a, b, dim_a, dim_b):
@@ -286,9 +429,9 @@
         ],
         compiler_params=pltpu.CompilerParams(vmem_limit_bytes=40 * 2**20),
         cost_estimate=pl.CostEstimate(
-            flops=4 * repeats * width * rows * rows * 7,
+            flops=COST * repeats * width * rows * rows,
             bytes_accessed=12 * 2**20,
-            transcendentals=repeats * rows * rows * 7,
+            transcendentals=0,
         ),
         name="attend",
     )(kind, queries, pairs, low, high, index)
@@ -366,9 +509,9 @@
         ],
         compiler_params=pltpu.CompilerParams(vmem_limit_bytes=40 * 2**20),
         cost_estimate=pl.CostEstimate(
-            flops=10 * repeats * width * rows * rows * 7,
-            bytes_accessed=20 * 2**20,
-            transcendentals=repeats * rows * rows * 7,
+            flops=COST * repeats * width * rows * rows,
+            bytes_accessed=12 * 2**20,
+            transcendentals=0,
         ),
         name="attend_back",
     )(kind, queries, pairs, upstream, low, high, index, lse, delta)
@@ -399,93 +542,169 @@
     repeats = QUERY_HEADS_ALL // KEY_VALUE_HEADS
     query_cols = query_weight.shape[1]
 
+    score_scale = 1.0 / math.sqrt(width)
+
+    qkv = RingGather(jnp.concatenate([query_weight, key_matrix, value_matrix], axis=1))
+    qkv.go()
+    gate_mine, gate_other = halves(gate_weight, 1)
+    gate_got = flip(gate_other, "blk", PAIR_BIT)
+    tokens_y = flip(tokens, "head", 2)
+    gains = gain_hop(jnp.stack([attn_gain, mlp_gain]), 1)
+    gains, gate_got, segment_ids, positions = join([qkv], gains, gate_got, segment_ids, positions)
+
+    qkv.go()
+    gate_full = group_gather(place_half(gate_mine, gate_got))
+    gains = gain_hop(gains, 2)
     segs = slots(segment_ids.reshape(blocks, heads, own_rows), head)
     poss = slots(positions.reshape(blocks, heads, own_rows), head)
     index = slots(jnp.arange(blocks * rows, dtype=jnp.int32).reshape(blocks, heads, own_rows), head)
     own_seg = lax.dynamic_index_in_dim(segs, blk, 0, False)
     own_pos = lax.dynamic_index_in_dim(poss, blk, 0, False)
     high = lax.dynamic_index_in_dim(index, blk, 0, False)
-    low = jnp.sum(
-        (segment_ids[None, :] < own_seg[:, None]).astype(jnp.int32), axis=1
-    )
+    low = jnp.sum((segment_ids[None, :] < own_seg[:, None]).astype(jnp.int32), axis=1)
     block_seg = segment_ids.reshape(blocks, rows)
     seg_first, seg_last = block_seg[:, 0], block_seg[:, -1]
     ids = jnp.arange(blocks, dtype=jnp.int32)
     some = (ids <= blk) & (seg_last >= seg_first[blk])
     every = (ids < blk) & (seg_first == seg_last[blk])
     kind = jnp.where(every, 1, jnp.where(some, 2, 0)).astype(jnp.int32)
+    index = index.reshape(blocks, 1, rows)
+    up_mine, up_other = halves(up_weight, 1)
+    tokens_y, gains, low, own_pos, up_other = join([qkv], tokens_y, gains, low, own_pos, up_other)
+
+    qkv.go()
+    up_got = flip(up_other, "blk", PAIR_BIT)
+    tokens_parts = head_rest(tokens, tokens_y)
+    gains = gain_hop(gains, 4)
+    for bit in (8, 16, 32):
+        gains = gain_hop(gains, bit)
+    tokens_all = head_all(*tokens_parts)
+    source_all = tokens_all.astype(F32)
+    inverse_all = norm_scale(source_all)
     table = rotary_table(own_pos, width)
-
-    qkv_full, qkv_steps = ring_gather(
-        jnp.concatenate([query_weight, key_matrix, value_matrix], axis=1)
-    )
-    gains = gain_gather(jnp.stack([attn_gain, mlp_gain])).astype(F32)
+    inverse_all, gains, up_got, cosine, sine = join([qkv], inverse_all, gains, up_got, *table)
+    table = (cosine, sine)
+    qkv.rest()
+
+    qkv.go()
+    up_full = group_gather(place_half(up_mine, up_got))
+    gains = gains.astype(F32)
     gain_one, gain_two = gains[0], gains[1]
-    source_all = head_gather(tokens).astype(F32)
-    out_full, out_steps = ring_gather(after(out_weight.T, qkv_steps[-2][0]))
-    gate_full, gate_steps = ring_gather(after(gate_weight, qkv_steps[-1][0]))
-    up_full, up_steps = ring_gather(after(up_weight, gate_steps[1][0]))
-    down_full, down_steps = ring_gather(after(down_weight.T, up_steps[1][0]))
-    cotangent_all = head_gather(after(cotangent, qkv_steps[-1][0]))
-
-    inverse_all = norm_scale(source_all)
     normed_all = (source_all * inverse_all * gain_one).astype(BF)
     source = source_all[:own_rows]
     inverse_one = inverse_all[:own_rows]
-    linear = simple_product(normed_all, qkv_full)
-    score_scale = 1.0 / math.sqrt(width)
+    cot_y = flip(cotangent, "head", 2)
+    normed_all, out_in = join([qkv], normed_all, out_weight.T)
+
+    qkv_full = qkv.full()
+    out = RingGather(out_in)
+    out.go()
+    pair_linear = simple_product(normed_all, qkv_full[:, query_cols:])
+    pair = jnp.concatenate(
+        [
+            apply_rotary(pair_linear[:, :width], table, 1.0).astype(BF),
+            pair_linear[:, width:].astype(BF),
+        ],
+        axis=1,
+    )
+    pair, cot_y, normed_low = join([out], pair, cot_y, normed_all)
+    pairs = RingGather(pair)
+    pairs.go()
+    out.go()
     queries = (
-        apply_rotary(linear[:, :query_cols].reshape(rows, repeats, width), table, 1.0).astype(BF)
+        apply_rotary(simple_product(normed_low, qkv_full[:, :query_cols]), table, 1.0).astype(BF)
         * score_scale
-    ).reshape(rows, query_cols)
-    key_rot = apply_rotary(
-        linear[:, query_cols : query_cols + width].reshape(rows, 1, width), table, 1.0
-    ).reshape(rows, width)
-    pair = jnp.concatenate(
-        [key_rot.astype(BF), linear[:, query_cols + width :].astype(BF)], axis=1
-    )
-    pairs, _ = ring_gather(pair)
-    index = index.reshape(blocks, 1, rows)
-    attn_full, lse = attend(kind, queries, pairs, low[:, None], high[:, None], index, repeats, width)
+    )
+    down_mine, down_other = halves(down_weight, 0)
+    down_mine, down_other = down_mine.T, down_other.T
+    queries, down_mine, down_other = join([pairs, out], queries, down_mine, down_other)
+    pairs.go()
+    out.go()
+    down_got = flip(down_other, "blk", PAIR_BIT)
+    down_got = join([pairs, out], down_got)
+    pairs.go()
+    out.rest()
+    out.go()
+    down_full = group_gather(place_half(down_mine, down_got))
+    cot_x = flip(cotangent, "blk", PAIR_BIT)
+    cot_x = join([pairs, out], cot_x)
+    pairs.rest()
+    pairs.go()
+    cot_far = wide_far(cot_y, cot_x)
+    cot_y, cot_x, *cot_far = join([pairs], cot_y, cot_x, *cot_far)
+
+    pairs_full = pairs.full()
+    attn_full, lse = attend(
+        kind, queries, pairs_full, low[:, None], high[:, None], index, repeats, width
+    )
     attn_low = attn_full.astype(BF)
-    residual = source + head_sum(times_rows(attn_low, out_full))
+    kept, near = head_near(times_rows(attn_low, out.full()))
+    kept, near = barrier(kept, near)
+    kept, far = head_far(kept, near)
+    cotangent_all = wide_rest(cotangent, cot_y, cot_x, cot_far)
+    kept, far, cotangent_all = barrier(kept, far, cotangent_all)
+    residual = source + kept + far.astype(F32)
 
     inverse_two = norm_scale(residual)
     normed_two = (residual * inverse_two * gain_two).astype(BF)
-    normed_two_all = head_gather(normed_two)
+    near_y, near_x = barrier(*wide_near(normed_two))
+    far_y, far_x = wide_far(near_y, near_x)
+    trio = jnp.concatenate([normed_two, near_y, near_x], axis=0)
+    far_y, far_x, trio, beside = barrier(far_y, far_x, trio, flip(trio, "head", 1))
+    far = jnp.concatenate([far_y, far_x], axis=1)
+    normed_two_all = jnp.concatenate([trio, beside, far, flip(far, "head", 1)], axis=0)
     gate_lin = simple_product(normed_two_all, gate_full)
-    up_lin = simple_product(normed_two_all, up_full)
+    up_lin = simple_product(after(normed_two_all, gate_lin), up_full)
     sigmoid_gate = jax.nn.sigmoid(gate_lin)
     silu_gate = gate_lin * sigmoid_gate
     hidden = (silu_gate * up_lin).astype(BF)
-    down_grad = ring_sum(outer_sum(cotangent_all, hidden).astype(BF)).T
-    hidden_grad = simple_product(cotangent_all, down_full)
+    down_part = outer_sum(cotangent_all, hidden).astype(BF)
+    down_sum = group_sum(down_part)
+    hidden_grad = simple_product(after(cotangent_all, down_part), down_full)
     gate_act_grad = (
         hidden_grad * up_lin * sigmoid_gate * (1.0 + gate_lin * (1.0 - sigmoid_gate))
     ).astype(BF)
     up_act_grad = (hidden_grad * silu_gate).astype(BF)
-    normed_two_grad = head_sum(
-        times_rows(gate_act_grad, gate_full) + times_rows(up_act_grad, up_full)
-    )
-    gate_grad = ring_sum(outer_sum(normed_two_all, gate_act_grad).astype(BF))
-    up_grad = ring_sum(outer_sum(normed_two_all, up_act_grad).astype(BF))
-    layer_out = (residual + head_sum(times_rows(hidden, down_full))).astype(BF)
-
+
+    back = WideSum(
+        (times_rows(gate_act_grad, gate_full) + times_rows(up_act_grad, up_full)).astype(BF)
+    )
+    gate_act_grad, up_act_grad, hidden = join([back], gate_act_grad, up_act_grad, hidden)
+    sent = back.go_far()
+    gate_part = outer_sum(normed_two_all, after(gate_act_grad, *sent)).astype(BF)
+    hidden, up_act_grad, gate_part = join([back], hidden, up_act_grad, gate_part)
+    gate_sum = group_sum(gate_part)
+    sent = back.go_near()
+    up_part = outer_sum(normed_two_all, after(up_act_grad, *sent)).astype(BF)
+    hidden, up_part = join([back], hidden, up_part)
+    up_sum = group_sum(up_part)
+    normed_two_grad = back.total()
     residual_grad = cotangent.astype(F32) + norm_back(
         residual, gain_two, inverse_two, normed_two_grad
     )
-    mlp_gain_grad = gain_sum(jnp.sum(normed_two_grad * residual * inverse_two, axis=0))
-    branch_all = head_gather(residual_grad.astype(BF))
-    out_grad = ring_sum(outer_sum(branch_all, attn_low).astype(BF)).T
-
-    attn_grad = simple_product(branch_all, out_full).astype(BF)
-    row_delta = jnp.sum(
-        (attn_grad.astype(F32) * attn_full).reshape(rows, repeats, width), axis=-1
-    ).T.reshape(repeats, 1, rows)
+    branch_grad = residual_grad.astype(BF)
+    branch_y = flip(branch_grad, "head", 2)
+    layer_part = times_rows(after(hidden, branch_grad), down_full).astype(BF)
+    mlp_gain_part = jnp.sum(after(normed_two_grad, branch_grad) * residual * inverse_two, axis=0)
+    branch_y, mlp_gain_part, layer_part = barrier(branch_y, mlp_gain_part, layer_part)
+    branch_all = head_all(*head_rest(branch_grad, branch_y))
+    attn_grad = simple_product(branch_all, out.full()).astype(BF)
+    attn_grad, branch_all, layer_part = barrier(attn_grad, branch_all, layer_part)
+
+    row_delta = jnp.stack(
+        [
+            jnp.sum(
+                attn_grad[:, r * width : (r + 1) * width].astype(F32)
+                * attn_full[:, r * width : (r + 1) * width],
+                axis=1,
+            )
+            for r in range(repeats)
+        ]
+    ).reshape(repeats, 1, rows)
     query_rot_grad, pair_grad = attend_back(
         kind,
         queries,
-        pairs,
+        pairs_full,
         attn_grad,
         low[None, :],
         high[None, :],
@@ -495,33 +714,70 @@
         repeats,
         width,
     )
-    pair_grad = ring_sum(pair_grad)
-    query_lin_grad = (
-        apply_rotary(query_rot_grad.reshape(rows, repeats, width) * score_scale, table, -1.0)
-        .astype(BF)
-        .reshape(rows, query_cols)
-    )
-    key_lin_grad = apply_rotary(pair_grad[:, :width].reshape(rows, 1, width), table, -1.0)
+    layer = WideSum(layer_part)
+    query_rot_grad, pair_grad = join([layer], query_rot_grad, pair_grad)
+    pair_sum = RingSum(pair_grad)
+    sent = pair_sum.go()
+    layer.go_far()
+    out_part = outer_sum(branch_all, after(attn_low, *sent)).astype(BF)
+    out_sum = lax.psum_scatter(out_part, "blk", scatter_dimension=0, tiled=True)
+    out_part = join([pair_sum, layer], out_part)
+    sent = pair_sum.go()
+    layer.go_near()
+    query_lin_grad = apply_rotary(
+        after(query_rot_grad, *sent) * score_scale, table, -1.0
+    ).astype(BF)
+    query_lin_grad = join([pair_sum, layer], query_lin_grad)
+    sent = pair_sum.go()
+    layer_out = (residual + layer.total()).astype(BF)
+    layer_out = join([pair_sum], layer_out)
+    pair_sum.rest()
+    pair_sum.go()
+    join([pair_sum])
+    pair_total = pair_sum.total()
     pair_lin_grad = jnp.concatenate(
-        [key_lin_grad.reshape(rows, width), pair_grad[:, width:]], axis=1
+        [apply_rotary(pair_total[:, :width], table, -1.0), pair_total[:, width:]], axis=1
     ).astype(BF)
-    query_grad = ring_sum(outer_sum(normed_all, query_lin_grad).astype(BF))
-    pair_weight_grad = ring_sum(outer_sum(normed_all, pair_lin_grad).astype(BF))
-    normed_grad_part = times_rows(query_lin_grad, qkv_full[:, :query_cols]) + times_rows(
-        pair_lin_grad, qkv_full[:, query_cols:]
-    )
-    attn_gain_grad = gain_sum(jnp.sum(normed_grad_part * source_all * inverse_all, axis=0))
-    normed_grad = head_sum(normed_grad_part)
+    lin_grad = jnp.concatenate([query_lin_grad, pair_lin_grad], axis=1)
+    qkv_sum = RingSum(outer_sum(normed_all, lin_grad).astype(BF))
+    sent = qkv_sum.go()
+    lin_grad = after(lin_grad, *sent)
+    normed_grad_part = times_rows(lin_grad, qkv_full)
+    gain_part = jnp.sum(normed_grad_part * source_all * inverse_all, axis=0)
+    kept, near = head_near(normed_grad_part)
+    gain_grads = jnp.stack([gain_part, mlp_gain_part])
+    gain_grads = gain_grads + flip(gain_grads, "head", 1)
+    kept, near, gain_grads = join([qkv_sum], kept, near, gain_grads)
+    qkv_sum.go()
+    kept, far = head_far(kept, near)
+    gain_grads = gain_grads + flip(gain_grads, "head", 2)
+    kept, far, gain_grads = join([qkv_sum], kept, far, gain_grads)
+    qkv_sum.go()
+    bit = blocks // 2
+    gain_grads = gain_back(gain_grads, bit)
+    normed_grad = kept + far.astype(F32)
     tokens_grad = residual_grad + norm_back(source, gain_one, inverse_one, normed_grad)
+    gain_grads, tokens_grad = join([qkv_sum], gain_grads, tokens_grad)
+    qkv_sum.rest()
+    qkv_sum.go()
+    while bit > 1:
+        bit //= 2
+        gain_grads = gain_back(gain_grads, bit)
+    down_grad = narrow_half(*send_half(down_sum)).T
+    gate_grad = narrow_half(*send_half(gate_sum))
+    up_grad = narrow_half(*send_half(up_sum))
+    out_grad = out_sum.astype(F32).T
+    join([qkv_sum])
+    qkv_grad = qkv_sum.total()
     return (
         layer_out,
         tokens_grad,
-        attn_gain_grad,
-        query_grad,
-        pair_weight_grad[:, :width],
-        pair_weight_grad[:, width:],
+        gain_grads[0],
+        qkv_grad[:, :query_cols],
+        qkv_grad[:, query_cols : query_cols + width],
+        qkv_grad[:, query_cols + width :],
         out_grad,
-        mlp_gain_grad,
+        gain_grads[1],
         gate_grad,
         up_grad,
         down_grad,

time: 1080 us -> 897 us (0.83)
  local copies, waits for them, and re-layouts: 213 us -> 81.5 us
  starting transfers between devices: 181 us -> 112 us
  between operations: 2.95 us -> 16.9 us
    ppermute x104 -> x40, waiting for transfers between devices: 372 us -> 224 us  [the longest x20 126 us: go(): self.left = lax.ppermute(left, 'blk', self.routes[0])]
    ppermute x104 -> x40, starting transfers between devices: 158 us -> 60.6 us  [the longest x20 38.8 us: go(): self.left = lax.ppermute(left, 'blk', self.routes[0])]
    ppermute x29 -> x46, waiting for transfers between devices: 48.6 us -> 145 us  [flip(): lax.ppermute(value, axis, [(i, i ^ bit) for i in range(lax.axis_size(axis...]
    dynamic_update_slice x53 -> x27, local copies, waits for them, and re-layouts: 83.2 us -> 14.8 us  [the longest x12 7.01 us: full(): out = lax.dynamic_update_slice_in_dim(out, right, high, 0)]
    all_gather x0 -> x3, waiting for transfers between devices: none -> 55.4 us  [group_gather(): lax.all_gather(rows, 'blk', axis=0, tiled=True, axis_index_groups=plane_g...]
    ppermute x16 -> x0, local copies, waits for them, and re-layouts: 35.3 us -> none  [the longest x6 13.6 us: ring_gather(): right = lax.ppermute(right, 'blk', down)]
    ppermute x29 -> x46, starting transfers between devices: 22.5 us -> 51 us  [flip(): lax.ppermute(value, axis, [(i, i ^ bit) for i in range(lax.axis_size(axis...]
    convert_element_type x32 -> x11, other arithmetic: 40.4 us -> 22.3 us  [the longest x4 7.64 us: go(): right = (high.astype(F32) + right).astype(BF)]
  transfers between devices with their start and end apart: 133 -> 93, of which waited for: 49 -> 45; matrix products, arithmetic and copies ran while one was open for 35% -> 33% of each run, Pallas kernels for 2% -> 2%
where the time goes in v3:
time: 897 us; the launch traced here: 881 us
  waiting for transfers between devices  424 us (47%)
  matrix products  129 us (14%)
  starting transfers between devices  112 us (12%)
  other arithmetic  102 us (11%)
  local copies, waits for them, and re-layouts  81.5 us (9%)
  between operations  16.9 us (2%)
  Pallas kernels  15.2 us (2%)
    ppermute x46, waiting for transfers between devices, flip(): lax.ppermute(value, axis, [(i, i ^ bit) for i in range(lax.axis_size(axis...  145 us
    ppermute x20, waiting for transfers between devices, go(): self.left = lax.ppermute(left, 'blk', self.routes[0])  126 us
    ppermute x20, waiting for transfers between devices, go(): self.right = lax.ppermute(right, 'blk', self.routes[1])  97.3 us
    all_gather x3, waiting for transfers between devices, group_gather(): lax.all_gather(rows, 'blk', axis=0, tiled=True, axis_index_groups=plane_g...  55.4 us
    dot_general x6, matrix products, simple_product(): return jnp.dot(matrix_a, matrix_b, preferred_element_type=F32)  51.8 us
    ppermute x46, starting transfers between devices, flip(): lax.ppermute(value, axis, [(i, i ^ bit) for i in range(lax.axis_size(axis...  51 us
    dot_general x5, matrix products, times_rows(): lax.dot_general(matrix_a, matrix_b, (((1,), (1,)), ((), ())), preferred_e...  38.8 us
    ppermute x20, starting transfers between devices, go(): self.left = lax.ppermute(left, 'blk', self.routes[0])  38.8 us
  transfers between devices with their start and end apart: 93, of which 45 were waited for; matrix products, arithmetic and copies ran while one was open for 33% of the time, Pallas kernels for 2%

profile of v3, /device:TPU:0, one launch (start us, length us, event | category | flops | bytes accessed | tf_op | source)
XLA Modules:
  0.0 881.1 jit_solution(17834984151447363187)
XLA Ops:
  43.6 9.2 %collective-permute-done.7 = bf16[2,512]{1,0:T(2,128)(2,1)S(1)} collective-permute-done((bf16[2,512]{1,0:T(2,128)(2,1)S(1)}, bf16[2,512]{1,0:T(2,128)(2,1)S(1)}, u32[]{:S(2)}, u32[]{:S(2)}) %collective-permute-start.7) | collective-permute-done | bytes 2080 | tf_op jit(solution)/shard_map/ppermute | solution.py:156
  83.7 20.7 %collective-permute-done.10 = bf16[256,1024]{1,0:T(8,128)(2,1)S(1)} collective-permute-done((bf16[256,1024]{1,0:T(8,128)(2,1)}, bf16[256,1024]{1,0:T(8,128)(2,1)S(1)}, u32[]{:S(2)}, u32[]{:S(2)}) %collective-permute-start.10) | collective-permute-done | bytes 524320 | tf_op jit(solution)/shard_map/ppermute | solution.py:79
  122.9 8.9 %collective-permute-done.14 = bf16[128,1024]{1,0:T(8,128)(2,1)} collective-permute-done((bf16[128,1024]{1,0:T(8,128)(2,1)}, bf16[128,1024]{1,0:T(8,128)(2,1)}, u32[]{:S(2)}, u32[]{:S(2)}) %collective-permute-start.14) | collective-permute-done | bytes 262176 | tf_op jit(solution)/shard_map/ppermute | solution.py:79
  144.9 9.6 %collective-permute-done.16 = bf16[256,512]{0,1:T(8,128)(2,1)S(1)} collective-permute-done((bf16[256,512]{0,1:T(8,128)(2,1)S(1)}, bf16[256,512]{0,1:T(8,128)(2,1)S(1)}, u32[]{:S(2)}, u32[]{:S(2)}) %collective-permute-start.16) | collective-permute-done | bytes 262176 | tf_op jit(solution)/shard_map/ppermute | solution.py:79
  162.3 22.8 %collective-permute-done.20 = bf16[256,512]{0,1:T(8,128)(2,1)S(1)} collective-permute-done((bf16[256,512]{0,1:T(8,128)(2,1)S(1)}, bf16[256,512]{0,1:T(8,128)(2,1)S(1)}, u32[]{:S(2)}, u32[]{:S(2)}) %collective-permute-start.20) | collective-permute-done | bytes 262176 | tf_op jit(solution)/shard_map/ppermute | solution.py:78
  194.9 27.6 %collective-permute-done.24 = bf16[256,512]{0,1:T(8,128)(2,1)S(1)} collective-permute-done((bf16[256,512]{0,1:T(8,128)(2,1)S(1)}, bf16[256,512]{0,1:T(8,128)(2,1)S(1)}, u32[]{:S(2)}, u32[]{:S(2)}) %collective-permute-start.24) | collective-permute-done | bytes 262176 | tf_op jit(solution)/shard_map/ppermute | solution.py:78
  227.9 15.1 %collective-permute-done.31 = bf16[192,2048]{1,0:T(8,128)(2,1)S(1)} collective-permute-done((bf16[192,2048]{1,0:T(8,128)(2,1)S(1)}, bf16[192,2048]{1,0:T(8,128)(2,1)S(1)}, u32[]{:S(2)}, u32[]{:S(2)}) %collective-permute-start.31) | collective-permute-done | bytes 786464 | tf_op jit(solution)/shard_map/ppermute | solution.py:156
  243.0 19.7 %collective-permute-done.29 = bf16[128,512]{0,1:T(8,128)(2,1)S(1)} collective-permute-done((bf16[128,512]{0,1:T(8,128)(2,1)S(1)}, bf16[128,512]{0,1:T(8,128)(2,1)S(1)}, u32[]{:S(2)}, u32[]{:S(2)}) %collective-permute-start.29) | collective-permute-done | bytes 131104 | tf_op jit(solution)/shard_map/ppermute | solution.py:78
  303.9 13.7 %collective-permute-done.37 = bf16[192,2048]{1,0:T(8,128)(2,1)S(1)} collective-permute-done((bf16[192,2048]{1,0:T(8,128)(2,1)S(1)}, bf16[192,2048]{1,0:T(8,128)(2,1)S(1)}, u32[]{:S(2)}, u32[]{:S(2)}) %collective-permute-start.37) | collective-permute-done | bytes 786464 | tf_op jit(solution)/shard_map/ppermute | solution.py:156
  323.8 13.8 %collective-permute-done.40 = bf16[192,2048]{1,0:T(8,128)(2,1)S(1)} collective-permute-done((bf16[192,2048]{1,0:T(8,128)(2,1)S(1)}, bf16[192,2048]{1,0:T(8,128)(2,1)S(1)}, u32[]{:S(2)}, u32[]{:S(2)}) %collective-permute-start.40) | collective-permute-done | bytes 786464 | tf_op jit(solution)/shard_map/ppermute | solution.py:156
  345.1 9.3 %collective-permute-done.42 = bf16[192,1024]{1,0:T(8,128)(2,1)S(1)} collective-permute-done((bf16[192,1024]{1,0:T(8,128)(2,1)S(1)}, bf16[192,1024]{1,0:T(8,128)(2,1)S(1)}, u32[]{:S(2)}, u32[]{:S(2)}) %collective-permute-start.42) | collective-permute-done | bytes 393248 | tf_op jit(solution)/shard_map/ppermute | solution.py:156
  366.3 11.6 %fusion.35 = f32[1536,1024]{1,0:T(8,128)} fusion(bf16[1536,2048]{1,0:T(8,128)(2,1)} %pad_maximum_fusion, bf16[2048,1024]{1,0:T(8,128)(2,1)} %all-gather.4.cloned.1.call-done), kind=kOutput, calls=%fused_computation.246 | convolution fusion | flops 6442450944 | bytes 16777216 | tf_op jit(solution)/shard_map/dot_general | solution.py:232
  377.9 12.9 %multiply_convert_fusion.2 = (bf16[1536,1024]{1,0:T(8,128)(2,1)S(1)}, f32[1536,1024]{1,0:T(8,128)}) fusion(f32[1536,1024]{1,0:T(8,128)} %fusion.35, bf16[1536,2048]{1,0:T(8,128)(2,1)} %pad_maximum_fusion, bf16[2048,1024]{1,0:T(8,128)(2,1)} %all-gather.6.cloned.1.call-done), kind=kOutput, calls=%fused_computation.7 | convolution fusion | flops 6451888128 | bytes 26214400 | tf_op jit(solution)/shard_map/dot_general | solution.py:232
  392.4 11.2 %convolution_convert_fusion.3 = bf16[2048,1024]{1,0:T(8,128)(2,1)} fusion(bf16[1536,2048]{1,0:T(8,128)(2,1)} %constant_dynamic-update-slice_fusion.3, bf16[1536,1024]{1,0:T(8,128)(2,1)S(1)} %get-tuple-element.222), kind=kOutput, calls=%fused_computation.16 | convolution fusion | flops 6444548096 | bytes 13631488 | tf_op jit(solution)/shard_map/dot_general | solution.py:236
  403.9 55.4 %all-gather.8.cloned.1.call-done = bf16[2048,1024]{1,0:T(8,128)(2,1)} async-done(((bf16[512,1024]{1,0:T(8,128)(2,1)}), bf16[2048,1024]{1,0:T(8,128)(2,1)}) %all-gather.8.cloned.1.call-update) | async-done | bytes 4194320 | tf_op jit(solution)/shard_map/all_gather | solution.py:263
  459.3 15.7 %multiply_convert_fusion = (bf16[1536,1024]{1,0:T(8,128)(2,1)}, bf16[1536,1024]{1,0:T(8,128)(2,1)S(1)}) fusion(f32[1536,1024]{1,0:T(8,128)} %fusion.35, f32[1536,1024]{1,0:T(8,128)} %get-tuple-element.416, bf16[1536,2048]{1,0:T(8,128)(2,1)} %constant_dynamic-update-slice_fusion.3, bf16[2048,1024]{1,0:T(8,128)(2,1)} %all-gather.8.cloned.1.call-done), kind=kOutput, calls=%fused_computation.5 | convolution fusion | flops 6462898176 | bytes 29360128 | tf_op jit(solution)/shard_map/dot_general | solution.py:232
  475.0 9.2 %fusion.36 = f32[1536,2048]{1,0:T(8,128)} fusion(bf16[1536,1024]{1,0:T(8,128)(2,1)S(1)} %get-tuple-element.212, bf16[2048,1024]{1,0:T(8,128)(2,1)S(1)} %copy-done.81), kind=kOutput, calls=%fused_computation.247 | convolution fusion | flops 6442450944 | bytes 19922944 | tf_op jit(solution)/shard_map/dot_general | solution.py:242
  484.2 12.7 %add_convert_fusion = bf16[1536,2048]{1,0:T(8,128)(2,1)} fusion(f32[1536,2048]{1,0:T(8,128)} %fusion.36, bf16[1536,1024]{1,0:T(8,128)(2,1)} %get-tuple-element.217, bf16[2048,1024]{1,0:T(8,128)(2,1)S(1)} %copy-done.82), kind=kOutput, calls=%fused_computation.1 | convolution fusion | flops 6448742400 | bytes 26214400 | tf_op jit(solution)/shard_map/dot_general | solution.py:242
  510.3 8.5 convolution_convert_fusion.2
  528.8 11.8 %convolution_convert_fusion.1 = bf16[2048,1024]{1,0:T(8,128)(2,1)} fusion(bf16[1536,2048]{1,0:T(8,128)(2,1)} %pad_maximum_fusion, bf16[1536,1024]{1,0:T(8,128)(2,1)} %get-tuple-element.217), kind=kOutput, calls=%fused_computation.14 | convolution fusion | flops 6444548096 | bytes 13631488 | tf_op jit(solution)/shard_map/dot_general | solution.py:236
  552.6 7.1 convolution_convert_fusion
  560.1 9.6 %collective-permute-done.52 = bf16[192,2048]{1,0:T(8,128)(2,1)S(1)} collective-permute-done((bf16[192,2048]{1,0:T(8,128)(2,1)S(1)}, bf16[192,2048]{1,0:T(8,128)(2,1)S(1)}, u32[]{:S(2)}, u32[]{:S(2)}) %collective-permute-start.52) | collective-permute-done | bytes 786464 | tf_op jit(solution)/shard_map/ppermute | solution.py:156
  592.4 10.4 %attend_back.1 = (f32[768,512]{1,0:T(8,128)S(1)}, bf16[6144,512]{1,0:T(8,128)(2,1)S(1)}) custom-call(s32[8]{0:T(128)S(1)} %copy-done.9, bf16[768,512]{1,0:T(8,128)(2,1)S(1)} %copy-done.6, bf16[6144,512]{1,0:T(8,128)(2,1)} %copy-done.1, bf16[768,512]{1,0:T(8,128)(2,1)S(1)} %copy-done.7, s32[1,768]{1,0:T(1,128)S(1)} %broadcast_in_dim.43.refs_4_, ...), custom_call_target="tpu_custom_call" | custom-call | flops 12079595520 | bytes 12582912 | tf_op jit(solution)/shard_map/attend_back/pallas_call | solution.py:486
  637.5 7.6 collective-permute-start.60
  652.0 42.6 %collective-permute-done.61 = bf16[768,512]{1,0:T(8,128)(2,1)} collective-permute-done((bf16[768,512]{1,0:T(8,128)(2,1)}, bf16[768,512]{1,0:T(8,128)(2,1)}, u32[]{:S(2)}, u32[]{:S(2)}) %collective-permute-start.61) | collective-permute-done | bytes 786464 | tf_op jit(solution)/shard_map/ppermute | solution.py:136
  714.2 16.0 %collective-permute-done.64 = bf16[768,512]{1,0:T(8,128)(2,1)} collective-permute-done((bf16[768,512]{1,0:T(8,128)(2,1)}, bf16[768,512]{1,0:T(8,128)(2,1)}, u32[]{:S(2)}, u32[]{:S(2)}) %collective-permute-start.64) | collective-permute-done | bytes 786464 | tf_op jit(solution)/shard_map/ppermute | solution.py:135
  744.0 18.7 %collective-permute-done.66 = bf16[768,512]{1,0:T(8,128)(2,1)} collective-permute-done((bf16[768,512]{1,0:T(8,128)(2,1)}, bf16[768,512]{1,0:T(8,128)(2,1)}, u32[]{:S(2)}, u32[]{:S(2)}) %collective-permute-start.66) | collective-permute-done | bytes 786464 | tf_op jit(solution)/shard_map/ppermute | solution.py:135
  776.9 8.0 multiply_reduce_fusion
  792.6 14.5 %collective-permute-done.83 = bf16[256,1024]{1,0:T(8,128)(2,1)} collective-permute-done((bf16[256,1024]{1,0:T(8,128)(2,1)}, bf16[256,1024]{1,0:T(8,128)(2,1)}, u32[]{:S(2)}, u32[]{:S(2)}) %collective-permute-start.83) | collective-permute-done | bytes 524320 | tf_op jit(solution)/shard_map/ppermute | solution.py:156
  809.9 7.4 collective-permute-done.84
  829.2 10.1 %collective-permute-done.73 = bf16[256,1024]{1,0:T(8,128)(2,1)S(1)} collective-permute-done((bf16[256,1024]{1,0:T(8,128)(2,1)S(1)}, bf16[256,1024]{1,0:T(8,128)(2,1)S(1)}, u32[]{:S(2)}, u32[]{:S(2)}) %collective-permute-start.73) | collective-permute-done | bytes 524320 | tf_op jit(solution)/shard_map/ppermute | solution.py:136
  849.9 7.8 collective-permute-done.76
  (583 shorter events, 385.2 us)
Async XLA Ops:
  7.2 359.0 %all-gather.4.cloned.1.call-start = ((), (), s32[]{:S(2)}) async-start(), calls=%async_computation.4 | async-start | bytes 5242880 | tf_op jit(solution)/shard_map/all_gather | solution.py:263
  20.7 120.0 %collective-permute-start.17 = (bf16[192,2048]{1,0:T(8,128)(2,1)}, bf16[192,2048]{1,0:T(8,128)(2,1)}, u32[]{:S(2)}, u32[]{:S(2)}) collective-permute-start(bf16[192,2048]{1,0:T(8,128)(2,1)} %param.25), channel_id=1, source_target_pairs={{0,2},{1,3},{2,0},{3,1},{4,6},{5,7},{6,4},{7,5},{8,10},{9,11},{10,... | collective-permute-start | bytes 2359304 | tf_op jit(solution)/shard_map/ppermute | solution.py:156
  62.0 315.9 %all-gather.6.cloned.1.call-start = ((), (), s32[]{:S(2)}) async-start(), calls=%async_computation.5 | async-start | bytes 5242880 | tf_op jit(solution)/shard_map/all_gather | solution.py:263
  70.7 33.7 %collective-permute-start.10 = (bf16[256,1024]{1,0:T(8,128)(2,1)}, bf16[256,1024]{1,0:T(8,128)(2,1)S(1)}, u32[]{:S(2)}, u32[]{:S(2)}) collective-permute-start(bf16[256,1024]{1,0:T(8,128)(2,1)} %collective-permute-done.5), channel_id=1, source_target_pairs={{8,0},{16,8},{24,16},{28,24},{20,28},{12,20},{4,12},{0,4},{9,1},{1... | collective-permute-start | bytes 1572872 | tf_op jit(solution)/shard_map/ppermute | solution.py:79
  72.1 32.2 %collective-permute-start.9 = (bf16[256,1024]{1,0:T(8,128)(2,1)}, bf16[256,1024]{1,0:T(8,128)(2,1)S(1)}, u32[]{:S(2)}, u32[]{:S(2)}) collective-permute-start(bf16[256,1024]{1,0:T(8,128)(2,1)} %collective-permute-done.4), channel_id=1, source_target_pairs={{0,8},{8,16},{16,24},{24,28},{28,20},{20,12},{12,4},{4,0},{1,9},{9... | collective-permute-start | bytes 1572872 | tf_op jit(solution)/shard_map/ppermute | solution.py:78
  154.4 31.6 %collective-permute-start.18 = (bf16[768,512]{1,0:T(8,128)(2,1)S(1)}, bf16[768,512]{1,0:T(8,128)(2,1)S(1)}, u32[]{:S(2)}, u32[]{:S(2)}) collective-permute-start(bf16[768,512]{1,0:T(8,128)(2,1)S(1)} %pad_maximum_fusion.13), channel_id=1, source_target_pairs={{0,8},{8,16},{16,24},{24,28},{28,20},{20,12},{12,4},{4,0},{1,9},{9... | collective-permute-start | bytes 2359304 | tf_op jit(solution)/shard_map/ppermute | solution.py:78
  154.6 31.4 %collective-permute-start.19 = (bf16[768,512]{1,0:T(8,128)(2,1)S(1)}, bf16[768,512]{1,0:T(8,128)(2,1)S(1)}, u32[]{:S(2)}, u32[]{:S(2)}) collective-permute-start(bf16[768,512]{1,0:T(8,128)(2,1)S(1)} %pad_maximum_fusion.13), channel_id=1, source_target_pairs={{8,0},{16,8},{24,16},{28,24},{20,28},{12,20},{4,12},{0,4},{9,1},{1... | collective-permute-start | bytes 2359304 | tf_op jit(solution)/shard_map/ppermute | solution.py:79
  156.4 28.7 %collective-permute-start.20 = (bf16[256,512]{0,1:T(8,128)(2,1)S(1)}, bf16[256,512]{0,1:T(8,128)(2,1)S(1)}, u32[]{:S(2)}, u32[]{:S(2)}) collective-permute-start(bf16[256,512]{0,1:T(8,128)(2,1)S(1)} %collective-permute-done.15), channel_id=1, source_target_pairs={{0,8},{8,16},{16,24},{24,28},{28,20},{20,12},{12,4},{4,0},{1,9},{9... | collective-permute-start | bytes 786440 | tf_op jit(solution)/shard_map/ppermute | solution.py:78
  156.7 29.4 %collective-permute-start.21 = (bf16[256,512]{0,1:T(8,128)(2,1)S(1)}, bf16[256,512]{0,1:T(8,128)(2,1)S(1)}, u32[]{:S(2)}, u32[]{:S(2)}) collective-permute-start(bf16[256,512]{0,1:T(8,128)(2,1)S(1)} %collective-permute-done.16), channel_id=1, source_target_pairs={{8,0},{16,8},{24,16},{28,24},{20,28},{12,20},{4,12},{0,4},{9,1},{1... | collective-permute-start | bytes 786440 | tf_op jit(solution)/shard_map/ppermute | solution.py:79
  186.1 36.5 %collective-permute-start.22 = (bf16[768,512]{1,0:T(8,128)(2,1)S(1)}, bf16[768,512]{1,0:T(8,128)(2,1)S(1)}, u32[]{:S(2)}, u32[]{:S(2)}) collective-permute-start(bf16[768,512]{1,0:T(8,128)(2,1)S(1)} %collective-permute-done.18), channel_id=1, source_target_pairs={{0,8},{8,16},{16,24},{24,28},{28,20},{20,12},{12,4},{4,0},{1,9},{9... | collective-permute-start | bytes 2359304 | tf_op jit(solution)/shard_map/ppermute | solution.py:78
  187.7 35.6 %collective-permute-start.23 = (bf16[768,512]{1,0:T(8,128)(2,1)S(1)}, bf16[768,512]{1,0:T(8,128)(2,1)S(1)}, u32[]{:S(2)}, u32[]{:S(2)}) collective-permute-start(bf16[768,512]{1,0:T(8,128)(2,1)S(1)} %collective-permute-done.19), channel_id=1, source_target_pairs={{8,0},{16,8},{24,16},{28,24},{20,28},{12,20},{4,12},{0,4},{9,1},{1... | collective-permute-start | bytes 2359304 | tf_op jit(solution)/shard_map/ppermute | solution.py:79
  188.9 33.6 %collective-permute-start.26 = (bf16[256,1024]{1,0:T(8,128)(2,1)S(1)}, bf16[256,1024]{1,0:T(8,128)(2,1)S(1)}, u32[]{:S(2)}, u32[]{:S(2)}) collective-permute-start(bf16[256,1024]{1,0:T(8,128)(2,1)S(1)} %copy-done.64), channel_id=1, source_target_pairs={{0,4},{4,0},{8,12},{12,8},{16,20},{20,16},{24,28},{28,24},{1,5},{5... | collective-permute-start | bytes 1572872 | tf_op jit(solution)/shard_map/ppermute | solution.py:156
  191.2 31.3 %collective-permute-start.24 = (bf16[256,512]{0,1:T(8,128)(2,1)S(1)}, bf16[256,512]{0,1:T(8,128)(2,1)S(1)}, u32[]{:S(2)}, u32[]{:S(2)}) collective-permute-start(bf16[256,512]{0,1:T(8,128)(2,1)S(1)} %collective-permute-done.20), channel_id=1, source_target_pairs={{0,8},{8,16},{16,24},{24,28},{28,20},{20,12},{12,4},{4,0},{1,9},{9... | collective-permute-start | bytes 786440 | tf_op jit(solution)/shard_map/ppermute | solution.py:78
  191.9 30.6 %collective-permute-start.25 = (bf16[256,512]{0,1:T(8,128)(2,1)S(1)}, bf16[256,512]{0,1:T(8,128)(2,1)S(1)}, u32[]{:S(2)}, u32[]{:S(2)}) collective-permute-start(bf16[256,512]{0,1:T(8,128)(2,1)S(1)} %collective-permute-done.21), channel_id=1, source_target_pairs={{8,0},{16,8},{24,16},{28,24},{20,28},{12,20},{4,12},{0,4},{9,1},{1... | collective-permute-start | bytes 786440 | tf_op jit(solution)/shard_map/ppermute | solution.py:79
  223.3 39.3 %collective-permute-start.27 = (bf16[768,512]{1,0:T(8,128)(2,1)S(1)}, bf16[768,512]{1,0:T(8,128)(2,1)S(1)}, u32[]{:S(2)}, u32[]{:S(2)}) collective-permute-start(bf16[768,512]{1,0:T(8,128)(2,1)S(1)} %collective-permute-done.22), channel_id=1, source_target_pairs={{0,8},{8,16},{16,24},{24,28},{28,20},{20,12},{12,4},{4,0},{1,9},{9... | collective-permute-start | bytes 2359304 | tf_op jit(solution)/shard_map/ppermute | solution.py:78
  223.3 39.3 %collective-permute-start.28 = (bf16[768,512]{1,0:T(8,128)(2,1)S(1)}, bf16[768,512]{1,0:T(8,128)(2,1)S(1)}, u32[]{:S(2)}, u32[]{:S(2)}) collective-permute-start(bf16[768,512]{1,0:T(8,128)(2,1)S(1)} %collective-permute-done.23), channel_id=1, source_target_pairs={{8,0},{16,8},{24,16},{28,24},{20,28},{12,20},{4,12},{0,4},{9,1},{1... | collective-permute-start | bytes 2359304 | tf_op jit(solution)/shard_map/ppermute | solution.py:79
  225.5 37.1 %collective-permute-start.29 = (bf16[128,512]{0,1:T(8,128)(2,1)S(1)}, bf16[128,512]{0,1:T(8,128)(2,1)S(1)}, u32[]{:S(2)}, u32[]{:S(2)}) collective-permute-start(bf16[128,512]{0,1:T(8,128)(2,1)S(1)} %slice.308), channel_id=1, source_target_pairs={{0,8},{8,16},{16,24},{24,28},{28,20},{20,12},{12,4},{4,0},{1,9},{9... | collective-permute-start | bytes 393224 | tf_op jit(solution)/shard_map/ppermute | solution.py:78
  225.6 37.0 %collective-permute-start.30 = (bf16[128,512]{0,1:T(8,128)(2,1)S(1)}, bf16[128,512]{0,1:T(8,128)(2,1)S(1)}, u32[]{:S(2)}, u32[]{:S(2)}) collective-permute-start(bf16[128,512]{0,1:T(8,128)(2,1)S(1)} %slice.309), channel_id=1, source_target_pairs={{8,0},{16,8},{24,16},{28,24},{20,28},{12,20},{4,12},{0,4},{9,1},{1... | collective-permute-start | bytes 393224 | tf_op jit(solution)/shard_map/ppermute | solution.py:79
  243.0 28.1 %collective-permute-start.35 = (bf16[192,1024]{1,0:T(8,128)(2,1)S(1)}, bf16[192,1024]{1,0:T(8,128)(2,1)S(1)}, u32[]{:S(2)}, u32[]{:S(2)}) collective-permute-start(bf16[192,1024]{1,0:T(8,128)(2,1)S(1)} %slice.313), channel_id=1, source_target_pairs={{0,4},{4,0},{8,12},{12,8},{16,20},{20,16},{24,28},{28,24},{1,5},{5... | collective-permute-start | bytes 1179656 | tf_op jit(solution)/shard_map/ppermute | solution.py:156
  287.4 171.9 %all-gather.8.cloned.1.call-start = ((), (), s32[]{:S(2)}) async-start(), calls=%async_computation.6 | async-start | bytes 5242880 | tf_op jit(solution)/shard_map/all_gather | solution.py:263
  358.8 344.2 %reduce-scatter.11.cloned.1.call-start = ((), (), s32[]{:S(2)}) async-start(), calls=%async_computation.10 | async-start | bytes 5242880 | tf_op jit(solution)/shard_map/reduce_scatter | solution.py:267
  403.6 383.4 %reduce-scatter.7.cloned.1.call-start = ((), (), s32[]{:S(2)}) async-start(), calls=%async_computation.8 | async-start | bytes 5242880 | tf_op jit(solution)/shard_map/reduce_scatter | solution.py:267
  528.8 262.1 %reduce-scatter.9.cloned.1.call-start = ((), (), s32[]{:S(2)}) async-start(), calls=%async_computation.9 | async-start | bytes 5242880 | tf_op jit(solution)/shard_map/reduce_scatter | solution.py:267
  582.8 280.4 %reduce-scatter.5.cloned.1.call-start = ((), (), s32[]{:S(2)}) async-start(), calls=%async_computation.7 | async-start | bytes 2359296 | tf_op jit(solution)/shard_map/reduce_scatter | solution.py:723
  636.3 58.3 %collective-permute-start.61 = (bf16[768,512]{1,0:T(8,128)(2,1)}, bf16[768,512]{1,0:T(8,128)(2,1)}, u32[]{:S(2)}, u32[]{:S(2)}) collective-permute-start(bf16[768,512]{1,0:T(8,128)(2,1)} %pad_maximum_fusion.18), channel_id=1, source_target_pairs={{8,0},{16,8},{24,16},{28,24},{20,28},{12,20},{4,12},{0,4},{9,1},{1... | collective-permute-start | bytes 2359304 | tf_op jit(solution)/shard_map/ppermute | solution.py:136
  637.5 57.1 %collective-permute-start.60 = (bf16[768,512]{1,0:T(8,128)(2,1)}, bf16[768,512]{1,0:T(8,128)(2,1)}, u32[]{:S(2)}, u32[]{:S(2)}) collective-permute-start(bf16[768,512]{1,0:T(8,128)(2,1)} %pad_maximum_fusion.17), channel_id=1, source_target_pairs={{0,8},{8,16},{16,24},{24,28},{28,20},{20,12},{12,4},{4,0},{1,9},{9... | collective-permute-start | bytes 2359304 | tf_op jit(solution)/shard_map/ppermute | solution.py:135
  698.0 32.2 %collective-permute-start.64 = (bf16[768,512]{1,0:T(8,128)(2,1)}, bf16[768,512]{1,0:T(8,128)(2,1)}, u32[]{:S(2)}, u32[]{:S(2)}) collective-permute-start(bf16[768,512]{1,0:T(8,128)(2,1)} %get-tuple-element.336), channel_id=1, source_target_pairs={{0,8},{8,16},{16,24},{24,28},{28,20},{20,12},{12,4},{4,0},{1,9},{9... | collective-permute-start | bytes 2359304 | tf_op jit(solution)/shard_map/ppermute | solution.py:135
  701.7 30.4 %collective-permute-start.65 = (bf16[768,512]{1,0:T(8,128)(2,1)}, bf16[768,512]{1,0:T(8,128)(2,1)}, u32[]{:S(2)}, u32[]{:S(2)}) collective-permute-start(bf16[768,512]{1,0:T(8,128)(2,1)} %get-tuple-element.335), channel_id=1, source_target_pairs={{8,0},{16,8},{24,16},{28,24},{20,28},{12,20},{4,12},{0,4},{9,1},{1... | collective-permute-start | bytes 2359304 | tf_op jit(solution)/shard_map/ppermute | solution.py:136
  705.0 33.2 %collective-permute-start.85 = (bf16[256,1024]{1,0:T(8,128)(2,1)}, bf16[256,1024]{1,0:T(8,128)(2,1)}, u32[]{:S(2)}, u32[]{:S(2)}) collective-permute-start(bf16[256,1024]{1,0:T(8,128)(2,1)} %broadcast_select_fusion), channel_id=1, source_target_pairs={{0,4},{4,0},{8,12},{12,8},{16,20},{20,16},{24,28},{28,24},{1,5},{5... | collective-permute-start | bytes 1572872 | tf_op jit(solution)/shard_map/ppermute | solution.py:156
  774.9 44.2 %collective-permute-start.68 = (bf16[128,1024]{1,0:T(8,128)(2,1)}, bf16[128,1024]{1,0:T(8,128)(2,1)}, u32[]{:S(2)}, u32[]{:S(2)}) collective-permute-start(bf16[128,1024]{1,0:T(8,128)(2,1)} %get-tuple-element.352), channel_id=1, source_target_pairs={{0,8},{8,16},{16,24},{24,28},{28,20},{20,12},{12,4},{4,0},{1,9},{9... | collective-permute-start | bytes 786440 | tf_op jit(solution)/shard_map/ppermute | solution.py:135
  776.0 43.1 %collective-permute-start.69 = (bf16[128,1024]{1,0:T(8,128)(2,1)S(1)}, bf16[128,1024]{1,0:T(8,128)(2,1)}, u32[]{:S(2)}, u32[]{:S(2)}) collective-permute-start(bf16[128,1024]{1,0:T(8,128)(2,1)S(1)} %get-tuple-element.353), channel_id=1, source_target_pairs={{8,0},{16,8},{24,16},{28,24},{20,28},{12,20},{4,12},{0,4},{9,1},{1... | collective-permute-start | bytes 786440 | tf_op jit(solution)/shard_map/ppermute | solution.py:136
  786.5 32.6 %collective-permute-start.70 = (bf16[2,192,2048]{2,1,0:T(8,128)(2,1)}, bf16[2,192,2048]{2,1,0:T(8,128)(2,1)}, u32[]{:S(2)}, u32[]{:S(2)}) collective-permute-start(bf16[2,192,2048]{2,1,0:T(8,128)(2,1)} %get-tuple-element.357), channel_id=1, source_target_pairs={{0,1},{1,0},{2,3},{3,2},{4,5},{5,4},{6,7},{7,6},{8,9},{9,8},{10,11... | collective-permute-start | bytes 4718600 | tf_op jit(solution)/shard_map/ppermute | solution.py:156
  (155 other events, 2722.1 us)
Sparse Core Ops, SparseCore 0:
  62.1 110.9 all-gather.3
  287.5 90.3 all-gather.5
  380.0 79.2 all-gather.7
  461.5 75.2 reduce-scatter.10
  539.1 79.0 reduce-scatter.6
  620.3 106.9 reduce-scatter.8
  738.4 75.6 reduce-scatter.4

commit v4 on v3

--- a/solution.py
+++ b/solution.py
@@ -248,8 +248,9 @@
     return jnp.where((blk & PAIR_BIT) != 0, 1, 0)
 
 
-def halves(shard, axis):
-    side = pair_side(lax.axis_index("blk"))
+def halves(shard, axis, side=None):
+    if side is None:
+        side = pair_side(lax.axis_index("blk"))
     low, high = jnp.split(shard, 2, axis=axis)
     return jnp.where(side == 0, low, high), jnp.where(side == 0, high, low)
 
@@ -544,17 +545,26 @@
 
     score_scale = 1.0 / math.sqrt(width)
 
-    qkv = RingGather(jnp.concatenate([query_weight, key_matrix, value_matrix], axis=1))
-    qkv.go()
-    gate_mine, gate_other = halves(gate_weight, 1)
+    projections = lax.all_gather(
+        jnp.concatenate([query_weight, key_matrix, value_matrix, out_weight.T], axis=1),
+        "blk",
+        axis=0,
+        tiled=True,
+    )
+    tokens_y = flip(tokens, "head", 2)
+    side = pair_side(blk)
+    gate_mine, gate_other = halves(gate_weight, 1, side)
     gate_got = flip(gate_other, "blk", PAIR_BIT)
-    tokens_y = flip(tokens, "head", 2)
     gains = gain_hop(jnp.stack([attn_gain, mlp_gain]), 1)
-    gains, gate_got, segment_ids, positions = join([qkv], gains, gate_got, segment_ids, positions)
-
-    qkv.go()
-    gate_full = group_gather(place_half(gate_mine, gate_got))
     gains = gain_hop(gains, 2)
+    gains = gain_hop(gains, 4)
+    for bit in (8, 16, 32):
+        gains = gain_hop(gains, bit)
+    tokens_y, gains, gate_got, gate_mine, segment_ids, positions = barrier(
+        tokens_y, gains, gate_got, gate_mine, segment_ids, positions
+    )
+    gate_half = place_half(gate_mine, gate_got)
+    tokens_parts = head_rest(tokens, tokens_y)
     segs = slots(segment_ids.reshape(blocks, heads, own_rows), head)
     poss = slots(positions.reshape(blocks, heads, own_rows), head)
     index = slots(jnp.arange(blocks * rows, dtype=jnp.int32).reshape(blocks, heads, own_rows), head)
@@ -569,36 +579,33 @@
     every = (ids < blk) & (seg_first == seg_last[blk])
     kind = jnp.where(every, 1, jnp.where(some, 2, 0)).astype(jnp.int32)
     index = index.reshape(blocks, 1, rows)
-    up_mine, up_other = halves(up_weight, 1)
-    tokens_y, gains, low, own_pos, up_other = join([qkv], tokens_y, gains, low, own_pos, up_other)
-
-    qkv.go()
+    up_mine, up_other = halves(up_weight, 1, side)
     up_got = flip(up_other, "blk", PAIR_BIT)
-    tokens_parts = head_rest(tokens, tokens_y)
-    gains = gain_hop(gains, 4)
-    for bit in (8, 16, 32):
-        gains = gain_hop(gains, bit)
     tokens_all = head_all(*tokens_parts)
     source_all = tokens_all.astype(F32)
     inverse_all = norm_scale(source_all)
-    table = rotary_table(own_pos, width)
-    inverse_all, gains, up_got, cosine, sine = join([qkv], inverse_all, gains, up_got, *table)
-    table = (cosine, sine)
-    qkv.rest()
-
-    qkv.go()
-    up_full = group_gather(place_half(up_mine, up_got))
     gains = gains.astype(F32)
     gain_one, gain_two = gains[0], gains[1]
     normed_all = (source_all * inverse_all * gain_one).astype(BF)
     source = source_all[:own_rows]
     inverse_one = inverse_all[:own_rows]
+    table = rotary_table(own_pos, width)
+    normed_all, low, up_mine, up_got, gate_half, cosine, sine = barrier(
+        normed_all, low, up_mine, up_got, gate_half, *table
+    )
+    table = (cosine, sine)
+    up_half = place_half(up_mine, up_got)
+    down_mine, down_other = halves(down_weight, 0, side)
+    down_mine, down_other = down_mine.T, down_other.T
+    down_got = flip(down_other, "blk", PAIR_BIT)
     cot_y = flip(cotangent, "head", 2)
-    normed_all, out_in = join([qkv], normed_all, out_weight.T)
-
-    qkv_full = qkv.full()
-    out = RingGather(out_in)
-    out.go()
+    normed_all, projections, up_half, down_mine, down_got, cot_y = barrier(
+        normed_all, projections, up_half, down_mine, down_got, cot_y
+    )
+    qkv_full = projections[:, : query_cols + 2 * width]
+    out_full = projections[:, query_cols + 2 * width :]
+    gate_full = group_gather(gate_half)
+
     pair_linear = simple_product(normed_all, qkv_full[:, query_cols:])
     pair = jnp.concatenate(
         [
@@ -607,27 +614,21 @@
         ],
         axis=1,
     )
-    pair, cot_y, normed_low = join([out], pair, cot_y, normed_all)
+    pair, cot_y, normed_low, up_half = barrier(pair, cot_y, normed_all, up_half)
+    up_full = group_gather(up_half)
     pairs = RingGather(pair)
     pairs.go()
-    out.go()
     queries = (
         apply_rotary(simple_product(normed_low, qkv_full[:, :query_cols]), table, 1.0).astype(BF)
         * score_scale
     )
-    down_mine, down_other = halves(down_weight, 0)
-    down_mine, down_other = down_mine.T, down_other.T
-    queries, down_mine, down_other = join([pairs, out], queries, down_mine, down_other)
+    queries = join([pairs], queries)
     pairs.go()
-    out.go()
-    down_got = flip(down_other, "blk", PAIR_BIT)
-    down_got = join([pairs, out], down_got)
+    join([pairs])
     pairs.go()
-    out.rest()
-    out.go()
     down_full = group_gather(place_half(down_mine, down_got))
     cot_x = flip(cotangent, "blk", PAIR_BIT)
-    cot_x = join([pairs, out], cot_x)
+    cot_x, gate_full = join([pairs], cot_x, gate_full)
     pairs.rest()
     pairs.go()
     cot_far = wide_far(cot_y, cot_x)
@@ -638,11 +639,11 @@
         kind, queries, pairs_full, low[:, None], high[:, None], index, repeats, width
     )
     attn_low = attn_full.astype(BF)
-    kept, near = head_near(times_rows(attn_low, out.full()))
+    kept, near = head_near(times_rows(attn_low, out_full))
     kept, near = barrier(kept, near)
     kept, far = head_far(kept, near)
     cotangent_all = wide_rest(cotangent, cot_y, cot_x, cot_far)
-    kept, far, cotangent_all = barrier(kept, far, cotangent_all)
+    kept, far, cotangent_all, up_full = barrier(kept, far, cotangent_all, up_full)
     residual = source + kept + far.astype(F32)
 
     inverse_two = norm_scale(residual)
@@ -650,7 +651,9 @@
     near_y, near_x = barrier(*wide_near(normed_two))
     far_y, far_x = wide_far(near_y, near_x)
     trio = jnp.concatenate([normed_two, near_y, near_x], axis=0)
-    far_y, far_x, trio, beside = barrier(far_y, far_x, trio, flip(trio, "head", 1))
+    far_y, far_x, trio, beside, down_full = barrier(
+        far_y, far_x, trio, flip(trio, "head", 1), down_full
+    )
     far = jnp.concatenate([far_y, far_x], axis=1)
     normed_two_all = jnp.concatenate([trio, beside, far, flip(far, "head", 1)], axis=0)
     gate_lin = simple_product(normed_two_all, gate_full)
@@ -688,7 +691,7 @@
     mlp_gain_part = jnp.sum(after(normed_two_grad, branch_grad) * residual * inverse_two, axis=0)
     branch_y, mlp_gain_part, layer_part = barrier(branch_y, mlp_gain_part, layer_part)
     branch_all = head_all(*head_rest(branch_grad, branch_y))
-    attn_grad = simple_product(branch_all, out.full()).astype(BF)
+    attn_grad = simple_product(branch_all, out_full).astype(BF)
     attn_grad, branch_all, layer_part = barrier(attn_grad, branch_all, layer_part)
 
     row_delta = jnp.stack(
@@ -721,19 +724,25 @@
     layer.go_far()
     out_part = outer_sum(branch_all, after(attn_low, *sent)).astype(BF)
     out_sum = lax.psum_scatter(out_part, "blk", scatter_dimension=0, tiled=True)
-    out_part = join([pair_sum, layer], out_part)
+    down_mine, down_other = send_half(down_sum)
+    out_part, down_mine, down_other = join([pair_sum, layer], out_part, down_mine, down_other)
     sent = pair_sum.go()
     layer.go_near()
     query_lin_grad = apply_rotary(
         after(query_rot_grad, *sent) * score_scale, table, -1.0
     ).astype(BF)
-    query_lin_grad = join([pair_sum, layer], query_lin_grad)
+    down_grad = narrow_half(after(down_mine, *sent), down_other).T
+    gate_mine, gate_other = send_half(gate_sum)
+    query_lin_grad, down_grad, gate_mine, gate_other = join(
+        [pair_sum, layer], query_lin_grad, down_grad, gate_mine, gate_other
+    )
     sent = pair_sum.go()
     layer_out = (residual + layer.total()).astype(BF)
-    layer_out = join([pair_sum], layer_out)
+    gate_grad = narrow_half(after(gate_mine, *sent), gate_other)
+    layer_out, gate_grad = join([pair_sum], layer_out, gate_grad)
     pair_sum.rest()
     pair_sum.go()
-    join([pair_sum])
+    up_mine, up_other = join([pair_sum], *send_half(up_sum))
     pair_total = pair_sum.total()
     pair_lin_grad = jnp.concatenate(
         [apply_rotary(pair_total[:, :width], table, -1.0), pair_total[:, width:]], axis=1
@@ -751,22 +760,20 @@
     qkv_sum.go()
     kept, far = head_far(kept, near)
     gain_grads = gain_grads + flip(gain_grads, "head", 2)
-    kept, far, gain_grads = join([qkv_sum], kept, far, gain_grads)
+    kept, far, gain_grads, out_sum = join([qkv_sum], kept, far, gain_grads, out_sum)
     qkv_sum.go()
     bit = blocks // 2
     gain_grads = gain_back(gain_grads, bit)
     normed_grad = kept + far.astype(F32)
     tokens_grad = residual_grad + norm_back(source, gain_one, inverse_one, normed_grad)
-    gain_grads, tokens_grad = join([qkv_sum], gain_grads, tokens_grad)
+    out_grad = out_sum.astype(F32).T
+    gain_grads, tokens_grad, out_grad = join([qkv_sum], gain_grads, tokens_grad, out_grad)
     qkv_sum.rest()
     qkv_sum.go()
     while bit > 1:
         bit //= 2
         gain_grads = gain_back(gain_grads, bit)
-    down_grad = narrow_half(*send_half(down_sum)).T
-    gate_grad = narrow_half(*send_half(gate_sum))
-    up_grad = narrow_half(*send_half(up_sum))
-    out_grad = out_sum.astype(F32).T
+    up_grad = narrow_half(up_mine, up_other)
     join([qkv_sum])
     qkv_grad = qkv_sum.total()
     return (

time: 897 us -> 871 us (0.971)
  starting transfers between devices: 112 us -> 76.4 us
  other arithmetic: 102 us -> 120 us
    ppermute x20 -> x12, waiting for transfers between devices: 126 us -> 67.3 us  [go(): self.left = lax.ppermute(left, 'blk', self.routes[0])]
    all_gather x0 -> x1, waiting for transfers between devices: none -> 49.2 us  [local(): lax.all_gather(jnp.concatenate([query_weight, key_matrix, value_matrix, o...]
    ppermute x20 -> x12, starting transfers between devices: 38.8 us -> 19.3 us  [go(): self.left = lax.ppermute(left, 'blk', self.routes[0])]
    all_gather x3, waiting for transfers between devices: 55.4 us -> 42.7 us  [group_gather(): lax.all_gather(rows, 'blk', axis=0, tiled=True, axis_index_groups=plane_g...]
    ppermute x46, waiting for transfers between devices: 145 us -> 157 us  [flip(): lax.ppermute(value, axis, [(i, i ^ bit) for i in range(lax.axis_size(axis...]
    ppermute x46, starting transfers between devices: 51 us -> 41.2 us  [flip(): lax.ppermute(value, axis, [(i, i ^ bit) for i in range(lax.axis_size(axis...]
    unnamed x201 -> x180, local copies, waits for them, and re-layouts: 30.3 us -> 22.8 us
    ppermute x20 -> x12, waiting for transfers between devices: 97.3 us -> 104 us  [go(): self.right = lax.ppermute(right, 'blk', self.routes[1])]
  transfers between devices with their start and end apart: 93 -> 78, of which waited for: 45 -> 35; matrix products, arithmetic and copies ran while one was open for 33% -> 31% of each run, Pallas kernels for 2% -> 2%
where the time goes in v4:
time: 871 us; the launch traced here: 860 us
  waiting for transfers between devices  425 us (49%)
  matrix products  122 us (14%)
  other arithmetic  120 us (14%)
  local copies, waits for them, and re-layouts  81.4 us (9%)
  starting transfers between devices  76.4 us (9%)
  Pallas kernels  19.3 us (2%)
  between operations  16 us (2%)
    ppermute x46, waiting for transfers between devices, flip(): lax.ppermute(value, axis, [(i, i ^ bit) for i in range(lax.axis_size(axis...  157 us
    ppermute x12, waiting for transfers between devices, go(): self.right = lax.ppermute(right, 'blk', self.routes[1])  104 us
    ppermute x12, waiting for transfers between devices, go(): self.left = lax.ppermute(left, 'blk', self.routes[0])  67.3 us
    all_gather x1, waiting for transfers between devices, local(): lax.all_gather(jnp.concatenate([query_weight, key_matrix, value_matrix, o...  49.2 us
    dot_general x6, matrix products, simple_product(): return jnp.dot(matrix_a, matrix_b, preferred_element_type=F32)  45.9 us
    all_gather x3, waiting for transfers between devices, group_gather(): lax.all_gather(rows, 'blk', axis=0, tiled=True, axis_index_groups=plane_g...  42.7 us
    ppermute x46, starting transfers between devices, flip(): lax.ppermute(value, axis, [(i, i ^ bit) for i in range(lax.axis_size(axis...  41.2 us
    dot_general x5, matrix products, outer_sum(): lax.dot_general(matrix_a, matrix_b, (((0,), (0,)), ((), ())), preferred_e...  38.8 us
  transfers between devices with their start and end apart: 78, of which 35 were waited for; matrix products, arithmetic and copies ran while one was open for 31% of the time, Pallas kernels for 2%

profile of v4, /device:TPU:0, one launch (start us, length us, event | category | flops | bytes accessed | tf_op | source)
XLA Modules:
  0.0 860.1 jit_solution(4623609461921209199)
XLA Ops:
  47.9 6.3 multiply_convert_fusion.3
  63.2 17.5 %collective-permute-done.7 = bf16[256,1024]{1,0:T(8,128)(2,1)} collective-permute-done((bf16[256,1024]{1,0:T(8,128)(2,1)}, bf16[256,1024]{1,0:T(8,128)(2,1)}, u32[]{:S(2)}, u32[]{:S(2)}) %collective-permute-start.7) | collective-permute-done | bytes 524320 | tf_op jit(solution)/shard_map/ppermute | solution.py:156
  80.7 49.2 %all-gather.5.cloned.1.call-done = bf16[2048,1536]{0,1:T(8,128)(2,1)} async-done(((bf16[256,1536]{0,1:T(8,128)(2,1)}), bf16[2048,1536]{0,1:T(8,128)(2,1)}) %all-gather.5.cloned.1.call-update) | async-done | bytes 6291472 | tf_op jit(solution)/shard_map/all_gather | solution.py:548
  143.3 44.1 %collective-permute-done.10 = bf16[768,512]{1,0:T(8,128)(2,1)} collective-permute-done((bf16[768,512]{1,0:T(8,128)(2,1)S(1)}, bf16[768,512]{1,0:T(8,128)(2,1)}, u32[]{:S(2)}, u32[]{:S(2)}) %collective-permute-start.10) | collective-permute-done | bytes 786464 | tf_op jit(solution)/shard_map/ppermute | solution.py:79
  192.7 26.8 %collective-permute-done.11 = bf16[768,512]{1,0:T(8,128)(2,1)} collective-permute-done((bf16[768,512]{1,0:T(8,128)(2,1)}, bf16[768,512]{1,0:T(8,128)(2,1)}, u32[]{:S(2)}, u32[]{:S(2)}) %collective-permute-start.11) | collective-permute-done | bytes 786464 | tf_op jit(solution)/shard_map/ppermute | solution.py:78
  219.5 20.2 %collective-permute-done.12 = bf16[768,512]{1,0:T(8,128)(2,1)} collective-permute-done((bf16[768,512]{1,0:T(8,128)(2,1)}, bf16[768,512]{1,0:T(8,128)(2,1)}, u32[]{:S(2)}, u32[]{:S(2)}) %collective-permute-start.12) | collective-permute-done | bytes 786464 | tf_op jit(solution)/shard_map/ppermute | solution.py:79
  273.2 6.7 collective-permute-done.16
  280.0 14.3 %collective-permute-done.17 = bf16[384,512]{1,0:T(8,128)(2,1)S(1)} collective-permute-done((bf16[384,512]{1,0:T(8,128)(2,1)S(1)}, bf16[384,512]{1,0:T(8,128)(2,1)S(1)}, u32[]{:S(2)}, u32[]{:S(2)}) %collective-permute-start.17) | collective-permute-done | bytes 393248 | tf_op jit(solution)/shard_map/ppermute | solution.py:79
  295.9 9.2 %attend.1 = (f32[768,512]{1,0:T(8,128)S(1)}, f32[2,768,1]{2,1,0:T(8,128)S(1)}) custom-call(s32[8]{0:T(128)S(1)} %and_select_fusion.1.refs_0_, bf16[768,512]{1,0:T(8,128)(2,1)S(1)} %maximum_multiply_fusion.refs_1_, bf16[6144,512]{1,0:T(8,128)(2,1)} %constant_dynamic-update-slice_fusion.8.refs_2_, s32[768,1]{1,0:T(8,128)S(1)} %broadcast_in_dim.40.refs_3_, ...), custom_call_target="tpu_custom_call" | custom-call | flops 12079595520 | bytes 12582912 | tf_op jit(solution)/shard_map/attend/pallas_call | solution.py:408
  332.2 13.1 %collective-permute-done.21 = bf16[192,2048]{1,0:T(8,128)(2,1)} collective-permute-done((bf16[192,2048]{1,0:T(8,128)(2,1)S(1)}, bf16[192,2048]{1,0:T(8,128)(2,1)}, u32[]{:S(2)}, u32[]{:S(2)}) %collective-permute-start.21) | collective-permute-done | bytes 786464 | tf_op jit(solution)/shard_map/ppermute | solution.py:156
  348.4 18.2 %collective-permute-done.24 = bf16[192,2048]{1,0:T(8,128)(2,1)S(1)} collective-permute-done((bf16[192,2048]{1,0:T(8,128)(2,1)S(1)}, bf16[192,2048]{1,0:T(8,128)(2,1)S(1)}, u32[]{:S(2)}, u32[]{:S(2)}) %collective-permute-start.24) | collective-permute-done | bytes 786464 | tf_op jit(solution)/shard_map/ppermute | solution.py:156
  371.9 42.7 %all-gather.11.cloned.1.call-done = bf16[2048,1024]{1,0:T(8,128)(2,1)} async-done(((bf16[512,1024]{1,0:T(8,128)(2,1)}), bf16[2048,1024]{1,0:T(8,128)(2,1)}) %all-gather.11.cloned.1.call-update) | async-done | bytes 4194320 | tf_op jit(solution)/shard_map/all_gather | solution.py:264
  418.1 11.8 %pad_maximum_fusion = bf16[1536,2048]{1,0:T(8,128)(2,1)S(1)} fusion(bf16[192,2048]{1,0:T(8,128)(2,1)S(1)} %collective-permute-done.29, bf16[192,2048]{1,0:T(8,128)(2,1)S(1)} %constant_dynamic-update-slice_fusion.6, bf16[576,2048]{1,0:T(8,128)(2,1)} %collective-permute-done.28, bf16[576,2048]{1,0:T(8,128)(2,1)} %pad_maximum_fusion.4), kind=kLoop, calls=%fused_computation.3 | loop fusion | flops 25165824 | bytes 12582912 | tf_op jit(solution)/shard_map/concatenate | solution.py:658
  430.0 6.8 fusion.43
  436.8 9.5 %multiply_convert_fusion.2 = (bf16[1536,1024]{1,0:T(8,128)(2,1)}, f32[1536,1024]{1,0:T(8,128)}) fusion(f32[1536,1024]{1,0:T(8,128)S(1)} %fusion.43, bf16[1536,2048]{1,0:T(8,128)(2,1)S(1)} %pad_maximum_fusion, bf16[2048,1024]{1,0:T(8,128)(2,1)S(1)} %copy-done.66), kind=kOutput, calls=%fused_computation.7 | convolution fusion | flops 6451888128 | bytes 26214400 | tf_op jit(solution)/shard_map/dot_general | solution.py:232
  446.4 10.5 %convolution_convert_fusion.3 = bf16[2048,1024]{1,0:T(8,128)(2,1)} fusion(bf16[1536,2048]{1,0:T(8,128)(2,1)S(1)} %bitcast.86, bf16[1536,1024]{1,0:T(8,128)(2,1)} %get-tuple-element.210), kind=kOutput, calls=%fused_computation.18 | convolution fusion | flops 6444548096 | bytes 13631488 | tf_op jit(solution)/shard_map/dot_general | solution.py:236
  457.0 17.0 %multiply_convert_fusion.1 = (bf16[1536,1024]{1,0:T(8,128)(2,1)}, bf16[1536,1024]{1,0:T(8,128)(2,1)S(1)}) fusion(f32[1536,1024]{1,0:T(8,128)} %copy-done.71, f32[1536,1024]{1,0:T(8,128)} %get-tuple-element.424, bf16[1536,2048]{1,0:T(8,128)(2,1)} %constant_dynamic-update-slice_fusion, bf16[2048,1024]{1,0:T(8,128)(2,1)} %all-gather.11.cloned.1.call-done), kind=kOutput, calls=%fused_computation.6 | convolution fusion | flops 6462898176 | bytes 29360128 | tf_op jit(solution)/shard_map/dot_general | solution.py:232
  474.0 9.2 %fusion.44 = f32[1536,2048]{1,0:T(8,128)} fusion(bf16[1536,1024]{1,0:T(8,128)(2,1)S(1)} %get-tuple-element.205, bf16[2048,1024]{1,0:T(8,128)(2,1)S(1)} %copy-done.67), kind=kOutput, calls=%fused_computation.232 | convolution fusion | flops 6442450944 | bytes 19922944 | tf_op jit(solution)/shard_map/dot_general | solution.py:242
  483.2 12.6 %add_convert_fusion = bf16[1536,2048]{1,0:T(8,128)(2,1)} fusion(f32[1536,2048]{1,0:T(8,128)} %fusion.44, bf16[1536,1024]{1,0:T(8,128)(2,1)} %get-tuple-element.200, bf16[2048,1024]{1,0:T(8,128)(2,1)S(1)} %copy-done.65), kind=kOutput, calls=%fused_computation.1 | convolution fusion | flops 6448742400 | bytes 26214400 | tf_op jit(solution)/shard_map/dot_general | solution.py:242
  509.3 8.5 convolution_convert_fusion.2
  527.8 11.3 %convolution_convert_fusion.1 = bf16[2048,1024]{1,0:T(8,128)(2,1)} fusion(bf16[1536,2048]{1,0:T(8,128)(2,1)} %copy-done.29, bf16[1536,1024]{1,0:T(8,128)(2,1)} %copy-done.72), kind=kOutput, calls=%fused_computation.16 | convolution fusion | flops 6444548096 | bytes 13631488 | tf_op jit(solution)/shard_map/dot_general | solution.py:236
  551.7 7.1 convolution_convert_fusion
  559.1 9.2 %collective-permute-done.36 = bf16[192,2048]{1,0:T(8,128)(2,1)S(1)} collective-permute-done((bf16[192,2048]{1,0:T(8,128)(2,1)S(1)}, bf16[192,2048]{1,0:T(8,128)(2,1)S(1)}, u32[]{:S(2)}, u32[]{:S(2)}) %collective-permute-start.36) | collective-permute-done | bytes 786464 | tf_op jit(solution)/shard_map/ppermute | solution.py:156
  587.8 10.1 %attend_back.1 = (f32[768,512]{1,0:T(8,128)S(1)}, bf16[6144,512]{1,0:T(8,128)(2,1)S(1)}) custom-call(s32[8]{0:T(128)S(1)} %copy-done.7, bf16[768,512]{1,0:T(8,128)(2,1)S(1)} %copy-done.5, bf16[6144,512]{1,0:T(8,128)(2,1)} %constant_dynamic-update-slice_fusion.8.refs_2_, bf16[768,512]{1,0:T(8,128)(2,1)S(1)} %fusion.14.refs_3_, ...), custom_call_target="tpu_custom_call" | custom-call | flops 12079595520 | bytes 12582912 | tf_op jit(solution)/shard_map/attend_back/pallas_call | solution.py:487
  625.5 9.1 %collective-permute-done.44 = bf16[256,1024]{1,0:T(8,128)(2,1)} collective-permute-done((bf16[256,1024]{1,0:T(8,128)(2,1)}, bf16[256,1024]{1,0:T(8,128)(2,1)}, u32[]{:S(2)}, u32[]{:S(2)}) %collective-permute-start.44) | collective-permute-done | bytes 524320 | tf_op jit(solution)/shard_map/ppermute | solution.py:156
  652.7 24.9 %collective-permute-done.48 = bf16[192,2048]{1,0:T(8,128)(2,1)} collective-permute-done((bf16[192,2048]{1,0:T(8,128)(2,1)}, bf16[192,2048]{1,0:T(8,128)(2,1)}, u32[]{:S(2)}, u32[]{:S(2)}) %collective-permute-start.48) | collective-permute-done | bytes 786464 | tf_op jit(solution)/shard_map/ppermute | solution.py:156
  677.6 13.0 %collective-permute-done.46 = bf16[768,512]{1,0:T(8,128)(2,1)} collective-permute-done((bf16[768,512]{1,0:T(8,128)(2,1)}, bf16[768,512]{1,0:T(8,128)(2,1)}, u32[]{:S(2)}, u32[]{:S(2)}) %collective-permute-start.46) | collective-permute-done | bytes 786464 | tf_op jit(solution)/shard_map/ppermute | solution.py:136
  692.9 7.3 collective-permute-start.50
  705.2 18.6 %collective-permute-done.50 = bf16[768,512]{1,0:T(8,128)(2,1)S(1)} collective-permute-done((bf16[768,512]{1,0:T(8,128)(2,1)S(1)}, bf16[768,512]{1,0:T(8,128)(2,1)S(1)}, u32[]{:S(2)}, u32[]{:S(2)}) %collective-permute-start.50) | collective-permute-done | bytes 786464 | tf_op jit(solution)/shard_map/ppermute | solution.py:135
  733.6 31.8 %collective-permute-done.54 = bf16[256,1024]{1,0:T(8,128)(2,1)} collective-permute-done((bf16[256,1024]{1,0:T(8,128)(2,1)S(1)}, bf16[256,1024]{1,0:T(8,128)(2,1)}, u32[]{:S(2)}, u32[]{:S(2)}) %collective-permute-start.54) | collective-permute-done | bytes 524320 | tf_op jit(solution)/shard_map/ppermute | solution.py:156
  807.3 8.4 collective-permute-done.60
  827.6 6.3 collective-permute-done.63
  (508 shorter events, 332.5 us)
Async XLA Ops:
  7.2 122.6 %all-gather.5.cloned.1.call-start = ((), (), s32[]{:S(2)}) async-start(), calls=%async_computation.4 | async-start | bytes 7077888 | tf_op jit(solution)/shard_map/all_gather | solution.py:548
  12.4 244.9 %all-gather.7.cloned.1.call-start = ((), (), s32[]{:S(2)}) async-start(), calls=%async_computation.5 | async-start | bytes 5242880 | tf_op jit(solution)/shard_map/all_gather | solution.py:264
  20.7 33.5 %collective-permute-start.6 = (bf16[256,1024]{1,0:T(8,128)(2,1)}, bf16[256,1024]{1,0:T(8,128)(2,1)}, u32[]{:S(2)}, u32[]{:S(2)}) collective-permute-start(bf16[256,1024]{1,0:T(8,128)(2,1)} %get-tuple-element.405), channel_id=1, source_target_pairs={{0,4},{4,0},{8,12},{12,8},{16,20},{20,16},{24,28},{28,24},{1,5},{5... | collective-permute-start | bytes 1572872 | tf_op jit(solution)/shard_map/ppermute | solution.py:156
  54.2 291.0 %all-gather.9.cloned.1.call-start = ((), (), s32[]{:S(2)}) async-start(), calls=%async_computation.6 | async-start | bytes 5242880 | tf_op jit(solution)/shard_map/all_gather | solution.py:264
  54.3 26.4 %collective-permute-start.8 = (bf16[192,2048]{1,0:T(8,128)(2,1)}, bf16[192,2048]{1,0:T(8,128)(2,1)S(1)}, u32[]{:S(2)}, u32[]{:S(2)}) collective-permute-start(bf16[192,2048]{1,0:T(8,128)(2,1)} %param.25), channel_id=1, source_target_pairs={{0,2},{1,3},{2,0},{3,1},{4,6},{5,7},{6,4},{7,5},{8,10},{9,11},{10,... | collective-permute-start | bytes 2359304 | tf_op jit(solution)/shard_map/ppermute | solution.py:156
  134.6 280.0 %all-gather.11.cloned.1.call-start = ((), (), s32[]{:S(2)}) async-start(), calls=%async_computation.7 | async-start | bytes 5242880 | tf_op jit(solution)/shard_map/all_gather | solution.py:264
  135.4 121.9 %collective-permute-start.15 = (bf16[192,2048]{1,0:T(8,128)(2,1)S(1)}, bf16[192,2048]{1,0:T(8,128)(2,1)}, u32[]{:S(2)}, u32[]{:S(2)}) collective-permute-start(bf16[192,2048]{1,0:T(8,128)(2,1)S(1)} %copy-done.27), channel_id=1, source_target_pairs={{0,4},{4,0},{8,12},{12,8},{16,20},{20,16},{24,28},{28,24},{1,5},{5... | collective-permute-start | bytes 2359304 | tf_op jit(solution)/shard_map/ppermute | solution.py:156
  135.9 51.5 %collective-permute-start.10 = (bf16[768,512]{1,0:T(8,128)(2,1)S(1)}, bf16[768,512]{1,0:T(8,128)(2,1)}, u32[]{:S(2)}, u32[]{:S(2)}) collective-permute-start(bf16[768,512]{1,0:T(8,128)(2,1)S(1)} %pad_maximum_fusion.14), channel_id=1, source_target_pairs={{8,0},{16,8},{24,16},{28,24},{20,28},{12,20},{4,12},{0,4},{9,1},{1... | collective-permute-start | bytes 2359304 | tf_op jit(solution)/shard_map/ppermute | solution.py:79
  137.4 50.0 %collective-permute-start.9 = (bf16[768,512]{1,0:T(8,128)(2,1)S(1)}, bf16[768,512]{1,0:T(8,128)(2,1)}, u32[]{:S(2)}, u32[]{:S(2)}) collective-permute-start(bf16[768,512]{1,0:T(8,128)(2,1)S(1)} %pad_maximum_fusion.14), channel_id=1, source_target_pairs={{0,8},{8,16},{16,24},{24,28},{28,20},{20,12},{12,4},{4,0},{1,9},{9... | collective-permute-start | bytes 2359304 | tf_op jit(solution)/shard_map/ppermute | solution.py:78
  187.4 32.1 %collective-permute-start.11 = (bf16[768,512]{1,0:T(8,128)(2,1)}, bf16[768,512]{1,0:T(8,128)(2,1)}, u32[]{:S(2)}, u32[]{:S(2)}) collective-permute-start(bf16[768,512]{1,0:T(8,128)(2,1)} %collective-permute-done.9), channel_id=1, source_target_pairs={{0,8},{8,16},{16,24},{24,28},{28,20},{20,12},{12,4},{4,0},{1,9},{9... | collective-permute-start | bytes 2359304 | tf_op jit(solution)/shard_map/ppermute | solution.py:78
  187.4 52.3 %collective-permute-start.12 = (bf16[768,512]{1,0:T(8,128)(2,1)}, bf16[768,512]{1,0:T(8,128)(2,1)}, u32[]{:S(2)}, u32[]{:S(2)}) collective-permute-start(bf16[768,512]{1,0:T(8,128)(2,1)} %collective-permute-done.10), channel_id=1, source_target_pairs={{8,0},{16,8},{24,16},{28,24},{20,28},{12,20},{4,12},{0,4},{9,1},{1... | collective-permute-start | bytes 2359304 | tf_op jit(solution)/shard_map/ppermute | solution.py:79
  244.8 28.5 %collective-permute-start.19 = (bf16[192,1024]{1,0:T(8,128)(2,1)}, bf16[192,1024]{1,0:T(8,128)(2,1)}, u32[]{:S(2)}, u32[]{:S(2)}) collective-permute-start(bf16[192,1024]{1,0:T(8,128)(2,1)} %slice.308), channel_id=1, source_target_pairs={{0,4},{4,0},{8,12},{12,8},{16,20},{20,16},{24,28},{28,24},{1,5},{5... | collective-permute-start | bytes 1179656 | tf_op jit(solution)/shard_map/ppermute | solution.py:156
  265.8 28.5 %collective-permute-start.17 = (bf16[384,512]{1,0:T(8,128)(2,1)S(1)}, bf16[384,512]{1,0:T(8,128)(2,1)S(1)}, u32[]{:S(2)}, u32[]{:S(2)}) collective-permute-start(bf16[384,512]{1,0:T(8,128)(2,1)S(1)} %slice.306), channel_id=1, source_target_pairs={{8,0},{16,8},{24,16},{28,24},{20,28},{12,20},{4,12},{0,4},{9,1},{1... | collective-permute-start | bytes 1179656 | tf_op jit(solution)/shard_map/ppermute | solution.py:79
  266.9 27.4 %collective-permute-start.18 = (bf16[192,1024]{1,0:T(8,128)(2,1)S(1)}, bf16[192,1024]{1,0:T(8,128)(2,1)S(1)}, u32[]{:S(2)}, u32[]{:S(2)}) collective-permute-start(bf16[192,1024]{1,0:T(8,128)(2,1)S(1)} %slice.307), channel_id=1, source_target_pairs={{0,2},{1,3},{2,0},{3,1},{4,6},{5,7},{6,4},{7,5},{8,10},{9,11},{10,... | collective-permute-start | bytes 1179656 | tf_op jit(solution)/shard_map/ppermute | solution.py:156
  317.0 296.9 %reduce-scatter.5.cloned.1.call-start = ((), (), s32[]{:S(2)}) async-start(), calls=%async_computation.8 | async-start | bytes 5242880 | tf_op jit(solution)/shard_map/reduce_scatter | solution.py:268
  368.9 45.7 %collective-permute-start.28 = (bf16[576,2048]{1,0:T(8,128)(2,1)}, bf16[576,2048]{1,0:T(8,128)(2,1)}, u32[]{:S(2)}, u32[]{:S(2)}) collective-permute-start(bf16[576,2048]{1,0:T(8,128)(2,1)} %pad_maximum_fusion.4), channel_id=1, source_target_pairs={{0,1},{1,0},{2,3},{3,2},{4,5},{5,4},{6,7},{7,6},{8,9},{9,8},{10,11... | collective-permute-start | bytes 7077896 | tf_op jit(solution)/shard_map/ppermute | solution.py:156
  370.5 44.2 %collective-permute-start.26 = (bf16[192,1024]{1,0:T(8,128)(2,1)}, bf16[192,1024]{1,0:T(8,128)(2,1)S(1)}, u32[]{:S(2)}, u32[]{:S(2)}) collective-permute-start(bf16[192,1024]{1,0:T(8,128)(2,1)} %slice.315), channel_id=1, source_target_pairs={{0,2},{1,3},{2,0},{3,1},{4,6},{5,7},{6,4},{7,5},{8,10},{9,11},{10,... | collective-permute-start | bytes 1179656 | tf_op jit(solution)/shard_map/ppermute | solution.py:156
  371.7 43.0 %collective-permute-start.27 = (bf16[192,1024]{1,0:T(8,128)(2,1)}, bf16[192,1024]{1,0:T(8,128)(2,1)}, u32[]{:S(2)}, u32[]{:S(2)}) collective-permute-start(bf16[192,1024]{1,0:T(8,128)(2,1)} %slice.316), channel_id=1, source_target_pairs={{0,4},{4,0},{8,12},{12,8},{16,20},{20,16},{24,28},{28,24},{1,5},{5... | collective-permute-start | bytes 1179656 | tf_op jit(solution)/shard_map/ppermute | solution.py:156
  456.9 190.8 %reduce-scatter.7.cloned.1.call-start = ((), (), s32[]{:S(2)}) async-start(), calls=%async_computation.9 | async-start | bytes 5242880 | tf_op jit(solution)/shard_map/reduce_scatter | solution.py:268
  527.8 204.2 %reduce-scatter.9.cloned.1.call-start = ((), (), s32[]{:S(2)}) async-start(), calls=%async_computation.10 | async-start | bytes 5242880 | tf_op jit(solution)/shard_map/reduce_scatter | solution.py:268
  585.1 222.2 %reduce-scatter.11.cloned.1.call-start = ((), (), s32[]{:S(2)}) async-start(), calls=%async_computation.11 | async-start | bytes 2359296 | tf_op jit(solution)/shard_map/reduce_scatter | solution.py:726
  599.5 23.0 %collective-permute-start.42 = (bf16[192,1024]{1,0:T(8,128)(2,1)}, bf16[192,1024]{1,0:T(8,128)(2,1)}, u32[]{:S(2)}, u32[]{:S(2)}) collective-permute-start(bf16[192,1024]{1,0:T(8,128)(2,1)} %get-tuple-element.410), channel_id=1, source_target_pairs={{0,2},{1,3},{2,0},{3,1},{4,6},{5,7},{6,4},{7,5},{8,10},{9,11},{10,... | collective-permute-start | bytes 1179656 | tf_op jit(solution)/shard_map/ppermute | solution.py:156
  637.1 53.5 %collective-permute-start.46 = (bf16[768,512]{1,0:T(8,128)(2,1)}, bf16[768,512]{1,0:T(8,128)(2,1)}, u32[]{:S(2)}, u32[]{:S(2)}) collective-permute-start(bf16[768,512]{1,0:T(8,128)(2,1)} %pad_maximum_fusion.19), channel_id=1, source_target_pairs={{8,0},{16,8},{24,16},{28,24},{20,28},{12,20},{4,12},{0,4},{9,1},{1... | collective-permute-start | bytes 2359304 | tf_op jit(solution)/shard_map/ppermute | solution.py:136
  639.8 50.8 %collective-permute-start.45 = (bf16[768,512]{1,0:T(8,128)(2,1)}, bf16[768,512]{1,0:T(8,128)(2,1)}, u32[]{:S(2)}, u32[]{:S(2)}) collective-permute-start(bf16[768,512]{1,0:T(8,128)(2,1)} %pad_maximum_fusion.18), channel_id=1, source_target_pairs={{0,8},{8,16},{16,24},{24,28},{28,20},{20,12},{12,4},{4,0},{1,9},{9... | collective-permute-start | bytes 2359304 | tf_op jit(solution)/shard_map/ppermute | solution.py:135
  643.8 33.8 %collective-permute-start.48 = (bf16[192,2048]{1,0:T(8,128)(2,1)}, bf16[192,2048]{1,0:T(8,128)(2,1)}, u32[]{:S(2)}, u32[]{:S(2)}) collective-permute-start(bf16[192,2048]{1,0:T(8,128)(2,1)} %pad_maximum_fusion.21), channel_id=1, source_target_pairs={{0,4},{4,0},{8,12},{12,8},{16,20},{20,16},{24,28},{28,24},{1,5},{5... | collective-permute-start | bytes 2359304 | tf_op jit(solution)/shard_map/ppermute | solution.py:156
  645.7 31.9 %collective-permute-start.47 = (bf16[192,2048]{1,0:T(8,128)(2,1)}, bf16[192,2048]{1,0:T(8,128)(2,1)}, u32[]{:S(2)}, u32[]{:S(2)}) collective-permute-start(bf16[192,2048]{1,0:T(8,128)(2,1)} %pad_maximum_fusion.20), channel_id=1, source_target_pairs={{0,2},{1,3},{2,0},{3,1},{4,6},{5,7},{6,4},{7,5},{8,10},{9,11},{10,... | collective-permute-start | bytes 2359304 | tf_op jit(solution)/shard_map/ppermute | solution.py:156
  649.0 41.7 %collective-permute-start.49 = (bf16[256,1024]{1,0:T(8,128)(2,1)S(1)}, bf16[256,1024]{1,0:T(8,128)(2,1)S(1)}, u32[]{:S(2)}, u32[]{:S(2)}) collective-permute-start(bf16[256,1024]{1,0:T(8,128)(2,1)S(1)} %get-tuple-element.389), channel_id=1, source_target_pairs={{0,4},{4,0},{8,12},{12,8},{16,20},{20,16},{24,28},{28,24},{1,5},{5... | collective-permute-start | bytes 1572872 | tf_op jit(solution)/shard_map/ppermute | solution.py:156
  692.9 30.8 %collective-permute-start.50 = (bf16[768,512]{1,0:T(8,128)(2,1)S(1)}, bf16[768,512]{1,0:T(8,128)(2,1)S(1)}, u32[]{:S(2)}, u32[]{:S(2)}) collective-permute-start(bf16[768,512]{1,0:T(8,128)(2,1)S(1)} %get-tuple-element.336), channel_id=1, source_target_pairs={{0,8},{8,16},{16,24},{24,28},{28,20},{20,12},{12,4},{4,0},{1,9},{9... | collective-permute-start | bytes 2359304 | tf_op jit(solution)/shard_map/ppermute | solution.py:135
  700.2 25.7 %collective-permute-start.51 = (bf16[768,512]{1,0:T(8,128)(2,1)S(1)}, bf16[768,512]{1,0:T(8,128)(2,1)S(1)}, u32[]{:S(2)}, u32[]{:S(2)}) collective-permute-start(bf16[768,512]{1,0:T(8,128)(2,1)S(1)} %get-tuple-element.335), channel_id=1, source_target_pairs={{8,0},{16,8},{24,16},{28,24},{20,28},{12,20},{4,12},{0,4},{9,1},{1... | collective-permute-start | bytes 2359304 | tf_op jit(solution)/shard_map/ppermute | solution.py:136
  728.6 36.7 %collective-permute-start.52 = (bf16[768,512]{1,0:T(8,128)(2,1)}, bf16[768,512]{1,0:T(8,128)(2,1)}, u32[]{:S(2)}, u32[]{:S(2)}) collective-permute-start(bf16[768,512]{1,0:T(8,128)(2,1)} %get-tuple-element.334), channel_id=1, source_target_pairs={{0,8},{8,16},{16,24},{24,28},{28,20},{20,12},{12,4},{4,0},{1,9},{9... | collective-permute-start | bytes 2359304 | tf_op jit(solution)/shard_map/ppermute | solution.py:135
  731.9 33.5 %collective-permute-start.53 = (bf16[768,512]{1,0:T(8,128)(2,1)S(1)}, bf16[768,512]{1,0:T(8,128)(2,1)}, u32[]{:S(2)}, u32[]{:S(2)}) collective-permute-start(bf16[768,512]{1,0:T(8,128)(2,1)S(1)} %get-tuple-element.333), channel_id=1, source_target_pairs={{8,0},{16,8},{24,16},{28,24},{20,28},{12,20},{4,12},{0,4},{9,1},{1... | collective-permute-start | bytes 2359304 | tf_op jit(solution)/shard_map/ppermute | solution.py:136
  733.2 32.2 %collective-permute-start.54 = (bf16[256,1024]{1,0:T(8,128)(2,1)S(1)}, bf16[256,1024]{1,0:T(8,128)(2,1)}, u32[]{:S(2)}, u32[]{:S(2)}) collective-permute-start(bf16[256,1024]{1,0:T(8,128)(2,1)S(1)} %get-tuple-element.385), channel_id=1, source_target_pairs={{0,4},{4,0},{8,12},{12,8},{16,20},{20,16},{24,28},{28,24},{1,5},{5... | collective-permute-start | bytes 1572872 | tf_op jit(solution)/shard_map/ppermute | solution.py:156
  (129 other events, 1945.5 us)
Sparse Core Ops, SparseCore 0:
  12.5 117.2 all-gather.4
  132.0 108.2 all-gather.6
  242.4 91.0 all-gather.8
  335.5 79.1 all-gather.10
  457.0 75.2 reduce-scatter.4
  534.6 77.2 reduce-scatter.6
  614.2 103.1 reduce-scatter.8
  733.7 73.5 reduce-scatter.10

commit v5 on v4

--- a/solution.py
+++ b/solution.py
@@ -614,8 +614,9 @@
         ],
         axis=1,
     )
-    pair, cot_y, normed_low, up_half = barrier(pair, cot_y, normed_all, up_half)
-    up_full = group_gather(up_half)
+    up_down_half = jnp.concatenate([up_half, place_half(down_mine, down_got)], axis=1)
+    pair, cot_y, normed_low, up_down_half = barrier(pair, cot_y, normed_all, up_down_half)
+    up_down_full = group_gather(up_down_half)
     pairs = RingGather(pair)
     pairs.go()
     queries = (
@@ -626,7 +627,6 @@
     pairs.go()
     join([pairs])
     pairs.go()
-    down_full = group_gather(place_half(down_mine, down_got))
     cot_x = flip(cotangent, "blk", PAIR_BIT)
     cot_x, gate_full = join([pairs], cot_x, gate_full)
     pairs.rest()
@@ -643,7 +643,7 @@
     kept, near = barrier(kept, near)
     kept, far = head_far(kept, near)
     cotangent_all = wide_rest(cotangent, cot_y, cot_x, cot_far)
-    kept, far, cotangent_all, up_full = barrier(kept, far, cotangent_all, up_full)
+    kept, far, cotangent_all = barrier(kept, far, cotangent_all)
     residual = source + kept + far.astype(F32)
 
     inverse_two = norm_scale(residual)
@@ -651,13 +651,14 @@
     near_y, near_x = barrier(*wide_near(normed_two))
     far_y, far_x = wide_far(near_y, near_x)
     trio = jnp.concatenate([normed_two, near_y, near_x], axis=0)
-    far_y, far_x, trio, beside, down_full = barrier(
-        far_y, far_x, trio, flip(trio, "head", 1), down_full
-    )
+    far_y, far_x, trio, beside = barrier(far_y, far_x, trio, flip(trio, "head", 1))
     far = jnp.concatenate([far_y, far_x], axis=1)
     normed_two_all = jnp.concatenate([trio, beside, far, flip(far, "head", 1)], axis=0)
     gate_lin = simple_product(normed_two_all, gate_full)
-    up_lin = simple_product(after(normed_two_all, gate_lin), up_full)
+    gate_lin, normed_two_all, up_down_full = barrier(gate_lin, normed_two_all, up_down_full)
+    half = up_down_full.shape[1] // 2
+    up_full, down_full = up_down_full[:, :half], up_down_full[:, half:]
+    up_lin = simple_product(normed_two_all, up_full)
     sigmoid_gate = jax.nn.sigmoid(gate_lin)
     silu_gate = gate_lin * sigmoid_gate
     hidden = (silu_gate * up_lin).astype(BF)

time: 871 us -> 862 us (0.990)
  waiting for transfers between devices: 425 us -> 402 us
  matrix products: 122 us -> 133 us
  starting transfers between devices: 76.4 us -> 86.2 us
    all_gather x3 -> x2, waiting for transfers between devices: 42.7 us -> 0.01 us  [group_gather(): lax.all_gather(rows, 'blk', axis=0, tiled=True, axis_index_groups=plane_g...]
    ppermute x12, waiting for transfers between devices: 104 us -> 120 us  [go(): self.right = lax.ppermute(right, 'blk', self.routes[1])]
    ppermute x12, starting transfers between devices: 19.3 us -> 28.3 us  [go(): self.left = lax.ppermute(left, 'blk', self.routes[0])]
    unnamed x180 -> x168, local copies, waits for them, and re-layouts: 22.8 us -> 21.9 us
  transfers between devices with their start and end apart: 78 -> 77, of which waited for: 35 -> 35; matrix products, arithmetic and copies ran while one was open for 31% -> 33% of each run, Pallas kernels for 2% -> 2%
where the time goes in v5:
time: 862 us; the launch traced here: 851 us
  waiting for transfers between devices  402 us (47%)
  matrix products  133 us (15%)
  other arithmetic  120 us (14%)
  starting transfers between devices  86.2 us (10%)
  local copies, waits for them, and re-layouts  74.7 us (9%)
  Pallas kernels  19.3 us (2%)
  between operations  16.1 us (2%)
    ppermute x46, waiting for transfers between devices, flip(): lax.ppermute(value, axis, [(i, i ^ bit) for i in range(lax.axis_size(axis...  159 us
    ppermute x12, waiting for transfers between devices, go(): self.right = lax.ppermute(right, 'blk', self.routes[1])  120 us
    ppermute x12, waiting for transfers between devices, go(): self.left = lax.ppermute(left, 'blk', self.routes[0])  70.3 us
    dot_general x6, matrix products, simple_product(): return jnp.dot(matrix_a, matrix_b, preferred_element_type=F32)  50.5 us
    all_gather x1, waiting for transfers between devices, local(): lax.all_gather(jnp.concatenate([query_weight, key_matrix, value_matrix, o...  48.4 us
    ppermute x46, starting transfers between devices, flip(): lax.ppermute(value, axis, [(i, i ^ bit) for i in range(lax.axis_size(axis...  45.8 us
    dot_general x5, matrix products, times_rows(): lax.dot_general(matrix_a, matrix_b, (((1,), (1,)), ((), ())), preferred_e...  42.6 us
    dot_general x5, matrix products, outer_sum(): lax.dot_general(matrix_a, matrix_b, (((0,), (0,)), ((), ())), preferred_e...  39.5 us
  transfers between devices with their start and end apart: 77, of which 35 were waited for; matrix products, arithmetic and copies ran while one was open for 33% of the time, Pallas kernels for 2%

profile of v5, /device:TPU:0, one launch (start us, length us, event | category | flops | bytes accessed | tf_op | source)
XLA Modules:
  0.0 851.0 jit_solution(10235145399307512483)
XLA Ops:
  47.9 6.3 multiply_convert_fusion.3
  63.1 19.0 %collective-permute-done.7 = bf16[256,1024]{1,0:T(8,128)(2,1)} collective-permute-done((bf16[256,1024]{1,0:T(8,128)(2,1)S(1)}, bf16[256,1024]{1,0:T(8,128)(2,1)}, u32[]{:S(2)}, u32[]{:S(2)}) %collective-permute-start.7) | collective-permute-done | bytes 524320 | tf_op jit(solution)/shard_map/ppermute | solution.py:156
  82.1 48.4 %all-gather.4.cloned.1.call-done = bf16[2048,1536]{0,1:T(8,128)(2,1)} async-done(((bf16[256,1536]{0,1:T(8,128)(2,1)}), bf16[2048,1536]{0,1:T(8,128)(2,1)}) %all-gather.4.cloned.1.call-update) | async-done | bytes 6291472 | tf_op jit(solution)/shard_map/all_gather | solution.py:548
  145.9 48.1 %collective-permute-done.10 = bf16[768,512]{1,0:T(8,128)(2,1)} collective-permute-done((bf16[768,512]{1,0:T(8,128)(2,1)}, bf16[768,512]{1,0:T(8,128)(2,1)}, u32[]{:S(2)}, u32[]{:S(2)}) %collective-permute-start.10) | collective-permute-done | bytes 786464 | tf_op jit(solution)/shard_map/ppermute | solution.py:79
  198.2 29.5 %collective-permute-done.11 = bf16[768,512]{1,0:T(8,128)(2,1)} collective-permute-done((bf16[768,512]{1,0:T(8,128)(2,1)}, bf16[768,512]{1,0:T(8,128)(2,1)}, u32[]{:S(2)}, u32[]{:S(2)}) %collective-permute-start.11) | collective-permute-done | bytes 786464 | tf_op jit(solution)/shard_map/ppermute | solution.py:78
  227.8 14.5 %collective-permute-done.12 = bf16[768,512]{1,0:T(8,128)(2,1)} collective-permute-done((bf16[768,512]{1,0:T(8,128)(2,1)}, bf16[768,512]{1,0:T(8,128)(2,1)}, u32[]{:S(2)}, u32[]{:S(2)}) %collective-permute-start.12) | collective-permute-done | bytes 786464 | tf_op jit(solution)/shard_map/ppermute | solution.py:79
  287.1 12.3 %collective-permute-done.17 = bf16[384,512]{1,0:T(8,128)(2,1)S(1)} collective-permute-done((bf16[384,512]{1,0:T(8,128)(2,1)S(1)}, bf16[384,512]{1,0:T(8,128)(2,1)S(1)}, u32[]{:S(2)}, u32[]{:S(2)}) %collective-permute-start.17) | collective-permute-done | bytes 393248 | tf_op jit(solution)/shard_map/ppermute | solution.py:79
  301.0 9.2 %attend.1 = (f32[768,512]{1,0:T(8,128)S(1)}, f32[2,768,1]{2,1,0:T(8,128)S(1)}) custom-call(s32[8]{0:T(128)S(1)} %and_select_fusion.1.refs_0_, bf16[768,512]{1,0:T(8,128)(2,1)S(1)} %maximum_multiply_fusion.refs_1_, bf16[6144,512]{1,0:T(8,128)(2,1)} %constant_dynamic-update-slice_fusion.8.refs_2_, s32[768,1]{1,0:T(8,128)S(1)} %broadcast_in_dim.40.refs_3_, ...), custom_call_target="tpu_custom_call" | custom-call | flops 12079595520 | bytes 12582912 | tf_op jit(solution)/shard_map/attend/pallas_call | solution.py:408
  326.1 16.9 %collective-permute-done.21 = bf16[192,2048]{1,0:T(8,128)(2,1)S(1)} collective-permute-done((bf16[192,2048]{1,0:T(8,128)(2,1)S(1)}, bf16[192,2048]{1,0:T(8,128)(2,1)S(1)}, u32[]{:S(2)}, u32[]{:S(2)}) %collective-permute-start.21) | collective-permute-done | bytes 786464 | tf_op jit(solution)/shard_map/ppermute | solution.py:156
  346.2 16.6 %collective-permute-done.24 = bf16[192,2048]{1,0:T(8,128)(2,1)S(1)} collective-permute-done((bf16[192,2048]{1,0:T(8,128)(2,1)S(1)}, bf16[192,2048]{1,0:T(8,128)(2,1)S(1)}, u32[]{:S(2)}, u32[]{:S(2)}) %collective-permute-start.24) | collective-permute-done | bytes 786464 | tf_op jit(solution)/shard_map/ppermute | solution.py:156
  367.3 8.5 collective-permute-done.26
  379.2 20.1 %pad_maximum_fusion = bf16[1536,2048]{1,0:T(8,128)(2,1)S(1)} fusion(bf16[192,2048]{1,0:T(8,128)(2,1)S(1)} %collective-permute-done.29, bf16[192,2048]{1,0:T(8,128)(2,1)S(1)} %constant_dynamic-update-slice_fusion.6, bf16[576,2048]{1,0:T(8,128)(2,1)S(1)} %collective-permute-done.28, bf16[576,2048]{1,0:T(8,128)(2,1)S(1)} %pad_maximum_fusion.4), kind=kLoop, calls=%fused_computation.3 | loop fusion | flops 25165824 | bytes 12582912 | tf_op jit(solution)/shard_map/concatenate | solution.py:656
  401.9 8.5 fusion.50
  410.4 12.9 %multiply_convert_fusion.2 = (bf16[1536,1024]{1,0:T(8,128)(2,1)S(1)}, f32[1536,1024]{1,0:T(8,128)}) fusion(f32[1536,1024]{1,0:T(8,128)} %fusion.50, bf16[1536,2048]{1,0:T(8,128)(2,1)} %copy-done.31, bf16[2048,2048]{1,0:T(8,128)(2,1)} %all-gather.8.cloned.1.call-done), kind=kOutput, calls=%fused_computation.7 | convolution fusion | flops 6451888128 | bytes 26214400 | tf_op jit(solution)/shard_map/dot_general | solution.py:232
  425.0 11.2 %convolution_convert_fusion.3 = bf16[2048,1024]{1,0:T(8,128)(2,1)} fusion(bf16[1536,2048]{1,0:T(8,128)(2,1)} %copy-done.55, bf16[1536,1024]{1,0:T(8,128)(2,1)S(1)} %get-tuple-element.210), kind=kOutput, calls=%fused_computation.18 | convolution fusion | flops 6444548096 | bytes 13631488 | tf_op jit(solution)/shard_map/dot_general | solution.py:236
  436.3 16.9 %multiply_convert_fusion.1 = (bf16[1536,1024]{1,0:T(8,128)(2,1)}, bf16[1536,1024]{1,0:T(8,128)(2,1)S(1)}) fusion(f32[1536,1024]{1,0:T(8,128)} %fusion.50, f32[1536,1024]{1,0:T(8,128)} %get-tuple-element.424, bf16[1536,2048]{1,0:T(8,128)(2,1)} %copy-done.55, bf16[2048,2048]{1,0:T(8,128)(2,1)} %all-gather.8.cloned.1.call-done), kind=kOutput, calls=%fused_computation.6 | convolution fusion | flops 6462898176 | bytes 29360128 | tf_op jit(solution)/shard_map/dot_general | solution.py:232
  453.1 12.6 %fusion.6 = f32[1536,2048]{1,0:T(8,128)} fusion(bf16[1536,1024]{1,0:T(8,128)(2,1)S(1)} %get-tuple-element.205, bf16[2048,2048]{1,0:T(8,128)(2,1)} %all-gather.8.cloned.1.call-done), kind=kOutput, calls=%fused_computation.23 | convolution fusion | flops 6442450944 | bytes 19922944 | tf_op jit(solution)/shard_map/dot_general | solution.py:242
  465.7 12.6 %add_convert_fusion = bf16[1536,2048]{1,0:T(8,128)(2,1)} fusion(f32[1536,2048]{1,0:T(8,128)} %fusion.6, bf16[1536,1024]{1,0:T(8,128)(2,1)} %get-tuple-element.200, bf16[2048,1024]{1,0:T(8,128)(2,1)S(1)} %copy-done.64), kind=kOutput, calls=%fused_computation.1 | convolution fusion | flops 6448742400 | bytes 26214400 | tf_op jit(solution)/shard_map/dot_general | solution.py:242
  491.0 8.7 %convolution_convert_fusion.2 = bf16[2048,1024]{1,0:T(8,128)(2,1)} fusion(bf16[1536,2048]{1,0:T(8,128)(2,1)S(1)} %bitcast.69, bf16[1536,1024]{1,0:T(8,128)(2,1)S(1)} %copy-done.68), kind=kOutput, calls=%fused_computation.17 | convolution fusion | flops 6444548096 | bytes 13631488 | tf_op jit(solution)/shard_map/dot_general | solution.py:236
  508.6 11.2 %convolution_convert_fusion.1 = bf16[2048,1024]{1,0:T(8,128)(2,1)} fusion(bf16[1536,2048]{1,0:T(8,128)(2,1)} %copy-done.31, bf16[1536,1024]{1,0:T(8,128)(2,1)} %copy-done.67), kind=kOutput, calls=%fused_computation.16 | convolution fusion | flops 6444548096 | bytes 13631488 | tf_op jit(solution)/shard_map/dot_general | solution.py:236
  531.7 9.5 %convolution_convert_fusion = bf16[1536,2048]{1,0:T(8,128)(2,1)S(1)} fusion(bf16[1536,1024]{1,0:T(8,128)(2,1)S(1)} %copy-done.70, bf16[2048,2048]{1,0:T(8,128)(2,1)} %all-gather.8.cloned.1.call-done), kind=kOutput, calls=%fused_computation.2 | convolution fusion | flops 6445596672 | bytes 13631488 | tf_op jit(solution)/shard_map/dot_general | solution.py:242
  541.5 6.8 collective-permute-done.36
  567.8 10.1 %attend_back.1 = (f32[768,512]{1,0:T(8,128)S(1)}, bf16[6144,512]{1,0:T(8,128)(2,1)S(1)}) custom-call(s32[8]{0:T(128)S(1)} %copy-done.7, bf16[768,512]{1,0:T(8,128)(2,1)S(1)} %copy-done.5, bf16[6144,512]{1,0:T(8,128)(2,1)} %constant_dynamic-update-slice_fusion.8.refs_2_, bf16[768,512]{1,0:T(8,128)(2,1)S(1)} %fusion.21.refs_3_, ...), custom_call_target="tpu_custom_call" | custom-call | flops 12079595520 | bytes 12582912 | tf_op jit(solution)/shard_map/attend_back/pallas_call | solution.py:487
  587.1 10.0 %collective-permute-start.40 = (bf16[384,512]{1,0:T(8,128)(2,1)}, bf16[384,512]{1,0:T(8,128)(2,1)}, u32[]{:S(2)}, u32[]{:S(2)}) collective-permute-start(bf16[384,512]{1,0:T(8,128)(2,1)} %get-tuple-element.338), channel_id=1, source_target_pairs={{0,8},{8,16},{16,24},{24,28},{28,20},{20,12},{12,4},{4,0},{1,9},{9... | collective-permute-start | bytes 1179656 | tf_op jit(solution)/shard_map/ppermute | solution.py:135
  611.2 13.4 %collective-permute-done.41 = bf16[384,512]{1,0:T(8,128)(2,1)} collective-permute-done((bf16[384,512]{1,0:T(8,128)(2,1)}, bf16[384,512]{1,0:T(8,128)(2,1)}, u32[]{:S(2)}, u32[]{:S(2)}) %collective-permute-start.41) | collective-permute-done | bytes 393248 | tf_op jit(solution)/shard_map/ppermute | solution.py:136
  628.1 6.6 collective-permute-start.45
  645.5 25.2 %collective-permute-done.48 = bf16[192,2048]{1,0:T(8,128)(2,1)} collective-permute-done((bf16[192,2048]{1,0:T(8,128)(2,1)}, bf16[192,2048]{1,0:T(8,128)(2,1)}, u32[]{:S(2)}, u32[]{:S(2)}) %collective-permute-start.48) | collective-permute-done | bytes 786464 | tf_op jit(solution)/shard_map/ppermute | solution.py:156
  670.6 15.0 %collective-permute-done.46 = bf16[768,512]{1,0:T(8,128)(2,1)} collective-permute-done((bf16[768,512]{1,0:T(8,128)(2,1)}, bf16[768,512]{1,0:T(8,128)(2,1)}, u32[]{:S(2)}, u32[]{:S(2)}) %collective-permute-start.46) | collective-permute-done | bytes 786464 | tf_op jit(solution)/shard_map/ppermute | solution.py:136
  695.3 20.4 %collective-permute-done.50 = bf16[768,512]{1,0:T(8,128)(2,1)S(1)} collective-permute-done((bf16[768,512]{1,0:T(8,128)(2,1)S(1)}, bf16[768,512]{1,0:T(8,128)(2,1)S(1)}, u32[]{:S(2)}, u32[]{:S(2)}) %collective-permute-start.50) | collective-permute-done | bytes 786464 | tf_op jit(solution)/shard_map/ppermute | solution.py:135
  725.8 32.5 %collective-permute-done.54 = bf16[256,1024]{1,0:T(8,128)(2,1)} collective-permute-done((bf16[256,1024]{1,0:T(8,128)(2,1)S(1)}, bf16[256,1024]{1,0:T(8,128)(2,1)}, u32[]{:S(2)}, u32[]{:S(2)}) %collective-permute-start.54) | collective-permute-done | bytes 524320 | tf_op jit(solution)/shard_map/ppermute | solution.py:156
  798.6 8.4 collective-permute-done.60
  818.9 6.0 collective-permute-done.63
  (492 shorter events, 327.1 us)
Async XLA Ops:
  7.2 123.3 %all-gather.4.cloned.1.call-start = ((), (), s32[]{:S(2)}) async-start(), calls=%async_computation.4 | async-start | bytes 7077888 | tf_op jit(solution)/shard_map/all_gather | solution.py:548
  12.4 245.6 %all-gather.6.cloned.1.call-start = ((), (), s32[]{:S(2)}) async-start(), calls=%async_computation.5 | async-start | bytes 5242880 | tf_op jit(solution)/shard_map/all_gather | solution.py:264
  20.7 33.5 %collective-permute-start.6 = (bf16[256,1024]{1,0:T(8,128)(2,1)}, bf16[256,1024]{1,0:T(8,128)(2,1)}, u32[]{:S(2)}, u32[]{:S(2)}) collective-permute-start(bf16[256,1024]{1,0:T(8,128)(2,1)} %get-tuple-element.405), channel_id=1, source_target_pairs={{0,4},{4,0},{8,12},{12,8},{16,20},{20,16},{24,28},{28,24},{1,5},{5... | collective-permute-start | bytes 1572872 | tf_op jit(solution)/shard_map/ppermute | solution.py:156
  54.2 356.2 %all-gather.8.cloned.1.call-start = ((), (), s32[]{:S(2)}) async-start(), calls=%async_computation.6 | async-start | bytes 10485760 | tf_op jit(solution)/shard_map/all_gather | solution.py:264
  54.3 27.8 %collective-permute-start.8 = (bf16[192,2048]{1,0:T(8,128)(2,1)}, bf16[192,2048]{1,0:T(8,128)(2,1)S(1)}, u32[]{:S(2)}, u32[]{:S(2)}) collective-permute-start(bf16[192,2048]{1,0:T(8,128)(2,1)} %param.25), channel_id=1, source_target_pairs={{0,2},{1,3},{2,0},{3,1},{4,6},{5,7},{6,4},{7,5},{8,10},{9,11},{10,... | collective-permute-start | bytes 2359304 | tf_op jit(solution)/shard_map/ppermute | solution.py:156
  138.8 55.2 %collective-permute-start.10 = (bf16[768,512]{1,0:T(8,128)(2,1)}, bf16[768,512]{1,0:T(8,128)(2,1)}, u32[]{:S(2)}, u32[]{:S(2)}) collective-permute-start(bf16[768,512]{1,0:T(8,128)(2,1)} %pad_maximum_fusion.13), channel_id=1, source_target_pairs={{8,0},{16,8},{24,16},{28,24},{20,28},{12,20},{4,12},{0,4},{9,1},{1... | collective-permute-start | bytes 2359304 | tf_op jit(solution)/shard_map/ppermute | solution.py:79
  139.3 54.7 %collective-permute-start.9 = (bf16[768,512]{1,0:T(8,128)(2,1)}, bf16[768,512]{1,0:T(8,128)(2,1)}, u32[]{:S(2)}, u32[]{:S(2)}) collective-permute-start(bf16[768,512]{1,0:T(8,128)(2,1)} %pad_maximum_fusion.13), channel_id=1, source_target_pairs={{0,8},{8,16},{16,24},{24,28},{28,20},{20,12},{12,4},{4,0},{1,9},{9... | collective-permute-start | bytes 2359304 | tf_op jit(solution)/shard_map/ppermute | solution.py:78
  194.0 33.8 %collective-permute-start.11 = (bf16[768,512]{1,0:T(8,128)(2,1)}, bf16[768,512]{1,0:T(8,128)(2,1)}, u32[]{:S(2)}, u32[]{:S(2)}) collective-permute-start(bf16[768,512]{1,0:T(8,128)(2,1)} %collective-permute-done.9), channel_id=1, source_target_pairs={{0,8},{8,16},{16,24},{24,28},{28,20},{20,12},{12,4},{4,0},{1,9},{9... | collective-permute-start | bytes 2359304 | tf_op jit(solution)/shard_map/ppermute | solution.py:78
  194.0 48.3 %collective-permute-start.12 = (bf16[768,512]{1,0:T(8,128)(2,1)}, bf16[768,512]{1,0:T(8,128)(2,1)}, u32[]{:S(2)}, u32[]{:S(2)}) collective-permute-start(bf16[768,512]{1,0:T(8,128)(2,1)} %collective-permute-done.10), channel_id=1, source_target_pairs={{8,0},{16,8},{24,16},{28,24},{20,28},{12,20},{4,12},{0,4},{9,1},{1... | collective-permute-start | bytes 2359304 | tf_op jit(solution)/shard_map/ppermute | solution.py:79
  196.0 62.0 %collective-permute-start.15 = (bf16[192,2048]{1,0:T(8,128)(2,1)S(1)}, bf16[192,2048]{1,0:T(8,128)(2,1)}, u32[]{:S(2)}, u32[]{:S(2)}) collective-permute-start(bf16[192,2048]{1,0:T(8,128)(2,1)S(1)} %copy-done.28), channel_id=1, source_target_pairs={{0,4},{4,0},{8,12},{12,8},{16,20},{20,16},{24,28},{28,24},{1,5},{5... | collective-permute-start | bytes 2359304 | tf_op jit(solution)/shard_map/ppermute | solution.py:156
  242.9 24.4 %collective-permute-start.14 = (bf16[768,512]{1,0:T(8,128)(2,1)}, bf16[768,512]{1,0:T(8,128)(2,1)}, u32[]{:S(2)}, u32[]{:S(2)}) collective-permute-start(bf16[768,512]{1,0:T(8,128)(2,1)} %collective-permute-done.12), channel_id=1, source_target_pairs={{8,0},{16,8},{24,16},{28,24},{20,28},{12,20},{4,12},{0,4},{9,1},{1... | collective-permute-start | bytes 2359304 | tf_op jit(solution)/shard_map/ppermute | solution.py:79
  246.6 35.3 %collective-permute-start.19 = (bf16[192,1024]{1,0:T(8,128)(2,1)}, bf16[192,1024]{1,0:T(8,128)(2,1)}, u32[]{:S(2)}, u32[]{:S(2)}) collective-permute-start(bf16[192,1024]{1,0:T(8,128)(2,1)} %slice.314), channel_id=1, source_target_pairs={{0,4},{4,0},{8,12},{12,8},{16,20},{20,16},{24,28},{28,24},{1,5},{5... | collective-permute-start | bytes 1179656 | tf_op jit(solution)/shard_map/ppermute | solution.py:156
  247.5 355.2 %reduce-scatter.5.cloned.1.call-start = ((), (), s32[]{:S(2)}) async-start(), calls=%async_computation.7 | async-start | bytes 5242880 | tf_op jit(solution)/shard_map/reduce_scatter | solution.py:268
  273.8 25.6 %collective-permute-start.17 = (bf16[384,512]{1,0:T(8,128)(2,1)S(1)}, bf16[384,512]{1,0:T(8,128)(2,1)S(1)}, u32[]{:S(2)}, u32[]{:S(2)}) collective-permute-start(bf16[384,512]{1,0:T(8,128)(2,1)S(1)} %slice.312), channel_id=1, source_target_pairs={{8,0},{16,8},{24,16},{28,24},{20,28},{12,20},{4,12},{0,4},{9,1},{1... | collective-permute-start | bytes 1179656 | tf_op jit(solution)/shard_map/ppermute | solution.py:79
  274.9 24.5 %collective-permute-start.18 = (bf16[192,1024]{1,0:T(8,128)(2,1)S(1)}, bf16[192,1024]{1,0:T(8,128)(2,1)S(1)}, u32[]{:S(2)}, u32[]{:S(2)}) collective-permute-start(bf16[192,1024]{1,0:T(8,128)(2,1)S(1)} %slice.313), channel_id=1, source_target_pairs={{0,2},{1,3},{2,0},{3,1},{4,6},{5,7},{6,4},{7,5},{8,10},{9,11},{10,... | collective-permute-start | bytes 1179656 | tf_op jit(solution)/shard_map/ppermute | solution.py:156
  436.2 204.0 %reduce-scatter.7.cloned.1.call-start = ((), (), s32[]{:S(2)}) async-start(), calls=%async_computation.8 | async-start | bytes 5242880 | tf_op jit(solution)/shard_map/reduce_scatter | solution.py:268
  508.6 215.8 %reduce-scatter.9.cloned.1.call-start = ((), (), s32[]{:S(2)}) async-start(), calls=%async_computation.9 | async-start | bytes 5242880 | tf_op jit(solution)/shard_map/reduce_scatter | solution.py:268
  565.1 233.5 %reduce-scatter.11.cloned.1.call-start = ((), (), s32[]{:S(2)}) async-start(), calls=%async_computation.10 | async-start | bytes 2359296 | tf_op jit(solution)/shard_map/reduce_scatter | solution.py:727
  579.4 31.7 %collective-permute-start.42 = (bf16[192,1024]{1,0:T(8,128)(2,1)}, bf16[192,1024]{1,0:T(8,128)(2,1)}, u32[]{:S(2)}, u32[]{:S(2)}) collective-permute-start(bf16[192,1024]{1,0:T(8,128)(2,1)} %get-tuple-element.410), channel_id=1, source_target_pairs={{0,2},{1,3},{2,0},{3,1},{4,6},{5,7},{6,4},{7,5},{8,10},{9,11},{10,... | collective-permute-start | bytes 1179656 | tf_op jit(solution)/shard_map/ppermute | solution.py:156
  580.7 30.5 %collective-permute-start.43 = (bf16[192,1024]{1,0:T(8,128)(2,1)}, bf16[192,1024]{1,0:T(8,128)(2,1)}, u32[]{:S(2)}, u32[]{:S(2)}) collective-permute-start(bf16[192,1024]{1,0:T(8,128)(2,1)} %get-tuple-element.409), channel_id=1, source_target_pairs={{0,4},{4,0},{8,12},{12,8},{16,20},{20,16},{24,28},{28,24},{1,5},{5... | collective-permute-start | bytes 1179656 | tf_op jit(solution)/shard_map/ppermute | solution.py:156
  587.1 24.1 %collective-permute-start.40 = (bf16[384,512]{1,0:T(8,128)(2,1)}, bf16[384,512]{1,0:T(8,128)(2,1)}, u32[]{:S(2)}, u32[]{:S(2)}) collective-permute-start(bf16[384,512]{1,0:T(8,128)(2,1)} %get-tuple-element.338), channel_id=1, source_target_pairs={{0,8},{8,16},{16,24},{24,28},{28,20},{20,12},{12,4},{4,0},{1,9},{9... | collective-permute-start | bytes 1179656 | tf_op jit(solution)/shard_map/ppermute | solution.py:135
  597.0 27.5 %collective-permute-start.41 = (bf16[384,512]{1,0:T(8,128)(2,1)}, bf16[384,512]{1,0:T(8,128)(2,1)}, u32[]{:S(2)}, u32[]{:S(2)}) collective-permute-start(bf16[384,512]{1,0:T(8,128)(2,1)} %get-tuple-element.339), channel_id=1, source_target_pairs={{8,0},{16,8},{24,16},{28,24},{20,28},{12,20},{4,12},{0,4},{9,1},{1... | collective-permute-start | bytes 1179656 | tf_op jit(solution)/shard_map/ppermute | solution.py:136
  627.1 58.5 %collective-permute-start.46 = (bf16[768,512]{1,0:T(8,128)(2,1)}, bf16[768,512]{1,0:T(8,128)(2,1)}, u32[]{:S(2)}, u32[]{:S(2)}) collective-permute-start(bf16[768,512]{1,0:T(8,128)(2,1)} %pad_maximum_fusion.18), channel_id=1, source_target_pairs={{8,0},{16,8},{24,16},{28,24},{20,28},{12,20},{4,12},{0,4},{9,1},{1... | collective-permute-start | bytes 2359304 | tf_op jit(solution)/shard_map/ppermute | solution.py:136
  628.1 57.5 %collective-permute-start.45 = (bf16[768,512]{1,0:T(8,128)(2,1)}, bf16[768,512]{1,0:T(8,128)(2,1)}, u32[]{:S(2)}, u32[]{:S(2)}) collective-permute-start(bf16[768,512]{1,0:T(8,128)(2,1)} %pad_maximum_fusion.17), channel_id=1, source_target_pairs={{0,8},{8,16},{16,24},{24,28},{28,20},{20,12},{12,4},{4,0},{1,9},{9... | collective-permute-start | bytes 2359304 | tf_op jit(solution)/shard_map/ppermute | solution.py:135
  637.5 33.1 %collective-permute-start.48 = (bf16[192,2048]{1,0:T(8,128)(2,1)}, bf16[192,2048]{1,0:T(8,128)(2,1)}, u32[]{:S(2)}, u32[]{:S(2)}) collective-permute-start(bf16[192,2048]{1,0:T(8,128)(2,1)} %pad_maximum_fusion.20), channel_id=1, source_target_pairs={{0,4},{4,0},{8,12},{12,8},{16,20},{20,16},{24,28},{28,24},{1,5},{5... | collective-permute-start | bytes 2359304 | tf_op jit(solution)/shard_map/ppermute | solution.py:156
  638.8 31.8 %collective-permute-start.47 = (bf16[192,2048]{1,0:T(8,128)(2,1)}, bf16[192,2048]{1,0:T(8,128)(2,1)}, u32[]{:S(2)}, u32[]{:S(2)}) collective-permute-start(bf16[192,2048]{1,0:T(8,128)(2,1)} %pad_maximum_fusion.19), channel_id=1, source_target_pairs={{0,2},{1,3},{2,0},{3,1},{4,6},{5,7},{6,4},{7,5},{8,10},{9,11},{10,... | collective-permute-start | bytes 2359304 | tf_op jit(solution)/shard_map/ppermute | solution.py:156
  641.5 44.1 %collective-permute-start.49 = (bf16[256,1024]{1,0:T(8,128)(2,1)S(1)}, bf16[256,1024]{1,0:T(8,128)(2,1)S(1)}, u32[]{:S(2)}, u32[]{:S(2)}) collective-permute-start(bf16[256,1024]{1,0:T(8,128)(2,1)S(1)} %get-tuple-element.389), channel_id=1, source_target_pairs={{0,4},{4,0},{8,12},{12,8},{16,20},{20,16},{24,28},{28,24},{1,5},{5... | collective-permute-start | bytes 1572872 | tf_op jit(solution)/shard_map/ppermute | solution.py:156
  687.9 27.8 %collective-permute-start.50 = (bf16[768,512]{1,0:T(8,128)(2,1)S(1)}, bf16[768,512]{1,0:T(8,128)(2,1)S(1)}, u32[]{:S(2)}, u32[]{:S(2)}) collective-permute-start(bf16[768,512]{1,0:T(8,128)(2,1)S(1)} %get-tuple-element.336), channel_id=1, source_target_pairs={{0,8},{8,16},{16,24},{24,28},{28,20},{20,12},{12,4},{4,0},{1,9},{9... | collective-permute-start | bytes 2359304 | tf_op jit(solution)/shard_map/ppermute | solution.py:135
  689.5 30.2 %collective-permute-start.51 = (bf16[768,512]{1,0:T(8,128)(2,1)S(1)}, bf16[768,512]{1,0:T(8,128)(2,1)S(1)}, u32[]{:S(2)}, u32[]{:S(2)}) collective-permute-start(bf16[768,512]{1,0:T(8,128)(2,1)S(1)} %get-tuple-element.335), channel_id=1, source_target_pairs={{8,0},{16,8},{24,16},{28,24},{20,28},{12,20},{4,12},{0,4},{9,1},{1... | collective-permute-start | bytes 2359304 | tf_op jit(solution)/shard_map/ppermute | solution.py:136
  722.3 36.0 %collective-permute-start.52 = (bf16[768,512]{1,0:T(8,128)(2,1)}, bf16[768,512]{1,0:T(8,128)(2,1)}, u32[]{:S(2)}, u32[]{:S(2)}) collective-permute-start(bf16[768,512]{1,0:T(8,128)(2,1)} %get-tuple-element.334), channel_id=1, source_target_pairs={{0,8},{8,16},{16,24},{24,28},{28,20},{20,12},{12,4},{4,0},{1,9},{9... | collective-permute-start | bytes 2359304 | tf_op jit(solution)/shard_map/ppermute | solution.py:135
  724.1 34.2 %collective-permute-start.53 = (bf16[768,512]{1,0:T(8,128)(2,1)S(1)}, bf16[768,512]{1,0:T(8,128)(2,1)}, u32[]{:S(2)}, u32[]{:S(2)}) collective-permute-start(bf16[768,512]{1,0:T(8,128)(2,1)S(1)} %get-tuple-element.333), channel_id=1, source_target_pairs={{8,0},{16,8},{24,16},{28,24},{20,28},{12,20},{4,12},{0,4},{9,1},{1... | collective-permute-start | bytes 2359304 | tf_op jit(solution)/shard_map/ppermute | solution.py:136
  725.6 32.7 %collective-permute-start.54 = (bf16[256,1024]{1,0:T(8,128)(2,1)S(1)}, bf16[256,1024]{1,0:T(8,128)(2,1)}, u32[]{:S(2)}, u32[]{:S(2)}) collective-permute-start(bf16[256,1024]{1,0:T(8,128)(2,1)S(1)} %get-tuple-element.385), channel_id=1, source_target_pairs={{0,4},{4,0},{8,12},{12,8},{16,20},{20,16},{24,28},{28,24},{1,5},{5... | collective-permute-start | bytes 1572872 | tf_op jit(solution)/shard_map/ppermute | solution.py:156
  (122 other events, 1898.3 us)
Sparse Core Ops, SparseCore 0:
  12.5 117.9 all-gather.3
  132.7 107.8 all-gather.5
  247.6 158.9 all-gather.7
  436.3 86.2 reduce-scatter.4
  524.9 77.2 reduce-scatter.6
  604.3 105.9 reduce-scatter.8
  725.9 72.5 reduce-scatter.10

commit v6 on v5

--- a/solution.py
+++ b/solution.py
@@ -651,9 +651,12 @@
     near_y, near_x = barrier(*wide_near(normed_two))
     far_y, far_x = wide_far(near_y, near_x)
     trio = jnp.concatenate([normed_two, near_y, near_x], axis=0)
-    far_y, far_x, trio, beside = barrier(far_y, far_x, trio, flip(trio, "head", 1))
+    early = jnp.concatenate([trio, flip(trio, "head", 1), trio[: 2 * own_rows]], axis=0)
+    far_y, far_x, early = barrier(far_y, far_x, early)
     far = jnp.concatenate([far_y, far_x], axis=1)
-    normed_two_all = jnp.concatenate([trio, beside, far, flip(far, "head", 1)], axis=0)
+    normed_two_all = lax.dynamic_update_slice_in_dim(
+        early, jnp.concatenate([far, flip(far, "head", 1)], axis=0), 6 * own_rows, 0
+    )
     gate_lin = simple_product(normed_two_all, gate_full)
     gate_lin, normed_two_all, up_down_full = barrier(gate_lin, normed_two_all, up_down_full)
     half = up_down_full.shape[1] // 2

time: 862 us -> 899 us (1.043)
  waiting for transfers between devices: 402 us -> 452 us
  other arithmetic: 120 us -> 103 us
    all_gather x2, waiting for transfers between devices: 0.01 us -> 82.4 us  [group_gather(): lax.all_gather(rows, 'blk', axis=0, tiled=True, axis_index_groups=plane_g...]
    concatenate x1 -> x0, other arithmetic: 20.1 us -> none  [local(): jnp.concatenate([trio, beside, far, flip(far, 'head', 1)], axis=0)]
    ppermute x12, waiting for transfers between devices: 120 us -> 106 us  [go(): self.right = lax.ppermute(right, 'blk', self.routes[1])]
    ppermute x12, waiting for transfers between devices: 70.3 us -> 56.7 us  [go(): self.left = lax.ppermute(left, 'blk', self.routes[0])]
    unnamed x168 -> x178, local copies, waits for them, and re-layouts: 21.9 us -> 22 us
  transfers between devices with their start and end apart: 77 -> 77, of which waited for: 35 -> 37; matrix products, arithmetic and copies ran while one was open for 33% -> 29% of each run, Pallas kernels for 2% -> 1%
where the time goes in v6:
time: 899 us; the launch traced here: 892 us
  waiting for transfers between devices  452 us (50%)
  matrix products  134 us (15%)
  other arithmetic  103 us (11%)
  starting transfers between devices  93.8 us (10%)
  local copies, waits for them, and re-layouts  73.9 us (8%)
  Pallas kernels  19.3 us (2%)
  between operations  16.1 us (2%)
    ppermute x46, waiting for transfers between devices, flip(): lax.ppermute(value, axis, [(i, i ^ bit) for i in range(lax.axis_size(axis...  153 us
    ppermute x12, waiting for transfers between devices, go(): self.right = lax.ppermute(right, 'blk', self.routes[1])  106 us
    all_gather x2, waiting for transfers between devices, group_gather(): lax.all_gather(rows, 'blk', axis=0, tiled=True, axis_index_groups=plane_g...  82.4 us
    ppermute x12, waiting for transfers between devices, go(): self.left = lax.ppermute(left, 'blk', self.routes[0])  56.7 us
    dot_general x6, matrix products, simple_product(): return jnp.dot(matrix_a, matrix_b, preferred_element_type=F32)  51.4 us
    all_gather x1, waiting for transfers between devices, local(): lax.all_gather(jnp.concatenate([query_weight, key_matrix, value_matrix, o...  48.4 us
    ppermute x46, starting transfers between devices, flip(): lax.ppermute(value, axis, [(i, i ^ bit) for i in range(lax.axis_size(axis...  45.6 us
    dot_general x5, matrix products, outer_sum(): lax.dot_general(matrix_a, matrix_b, (((0,), (0,)), ((), ())), preferred_e...  42.1 us
  transfers between devices with their start and end apart: 77, of which 37 were waited for; matrix products, arithmetic and copies ran while one was open for 29% of the time, Pallas kernels for 1%

profile of v6, /device:TPU:0, one launch (start us, length us, event | category | flops | bytes accessed | tf_op | source)
XLA Modules:
  0.0 891.7 jit_solution(17962974177055390966)
XLA Ops:
  47.9 6.3 multiply_convert_fusion.3
  63.1 19.0 %collective-permute-done.7 = bf16[256,1024]{1,0:T(8,128)(2,1)} collective-permute-done((bf16[256,1024]{1,0:T(8,128)(2,1)S(1)}, bf16[256,1024]{1,0:T(8,128)(2,1)}, u32[]{:S(2)}, u32[]{:S(2)}) %collective-permute-start.7) | collective-permute-done | bytes 524320 | tf_op jit(solution)/shard_map/ppermute | solution.py:156
  82.1 48.4 %all-gather.4.cloned.1.call-done = bf16[2048,1536]{0,1:T(8,128)(2,1)} async-done(((bf16[256,1536]{0,1:T(8,128)(2,1)}), bf16[2048,1536]{0,1:T(8,128)(2,1)}) %all-gather.4.cloned.1.call-update) | async-done | bytes 6291472 | tf_op jit(solution)/shard_map/all_gather | solution.py:548
  145.8 48.2 %collective-permute-done.10 = bf16[768,512]{1,0:T(8,128)(2,1)} collective-permute-done((bf16[768,512]{1,0:T(8,128)(2,1)}, bf16[768,512]{1,0:T(8,128)(2,1)}, u32[]{:S(2)}, u32[]{:S(2)}) %collective-permute-start.10) | collective-permute-done | bytes 786464 | tf_op jit(solution)/shard_map/ppermute | solution.py:79
  198.2 29.5 %collective-permute-done.11 = bf16[768,512]{1,0:T(8,128)(2,1)} collective-permute-done((bf16[768,512]{1,0:T(8,128)(2,1)}, bf16[768,512]{1,0:T(8,128)(2,1)}, u32[]{:S(2)}, u32[]{:S(2)}) %collective-permute-start.11) | collective-permute-done | bytes 786464 | tf_op jit(solution)/shard_map/ppermute | solution.py:78
  227.8 14.6 %collective-permute-done.12 = bf16[768,512]{1,0:T(8,128)(2,1)} collective-permute-done((bf16[768,512]{1,0:T(8,128)(2,1)}, bf16[768,512]{1,0:T(8,128)(2,1)}, u32[]{:S(2)}, u32[]{:S(2)}) %collective-permute-start.12) | collective-permute-done | bytes 786464 | tf_op jit(solution)/shard_map/ppermute | solution.py:79
  279.9 9.2 %attend.1 = (f32[768,512]{1,0:T(8,128)S(1)}, f32[2,768,1]{2,1,0:T(8,128)S(1)}) custom-call(s32[8]{0:T(128)S(1)} %and_select_fusion.1.refs_0_, bf16[768,512]{1,0:T(8,128)(2,1)S(1)} %maximum_multiply_fusion.refs_1_, bf16[6144,512]{1,0:T(8,128)(2,1)} %constant_dynamic-update-slice_fusion.14.refs_2_, s32[768,1]{1,0:T(8,128)S(1)} %broadcast_in_dim.40.refs_3_, ...), custom_call_target="tpu_custom_call" | custom-call | flops 12079595520 | bytes 12582912 | tf_op jit(solution)/shard_map/attend/pallas_call | solution.py:408
  310.3 17.7 %collective-permute-done.21 = bf16[192,2048]{1,0:T(8,128)(2,1)S(1)} collective-permute-done((bf16[192,2048]{1,0:T(8,128)(2,1)S(1)}, bf16[192,2048]{1,0:T(8,128)(2,1)S(1)}, u32[]{:S(2)}, u32[]{:S(2)}) %collective-permute-start.21) | collective-permute-done | bytes 786464 | tf_op jit(solution)/shard_map/ppermute | solution.py:156
  333.8 13.8 %collective-permute-done.24 = bf16[192,2048]{1,0:T(8,128)(2,1)S(1)} collective-permute-done((bf16[192,2048]{1,0:T(8,128)(2,1)S(1)}, bf16[192,2048]{1,0:T(8,128)(2,1)S(1)}, u32[]{:S(2)}, u32[]{:S(2)}) %collective-permute-start.24) | collective-permute-done | bytes 786464 | tf_op jit(solution)/shard_map/ppermute | solution.py:156
  355.9 6.8 collective-permute-done.26
  369.2 8.5 fusion.50
  377.7 82.4 %all-gather.8.cloned.1.call-done = bf16[2048,2048]{1,0:T(8,128)(2,1)} async-done(((bf16[512,2048]{1,0:T(8,128)(2,1)}), bf16[2048,2048]{1,0:T(8,128)(2,1)}) %all-gather.8.cloned.1.call-update) | async-done | bytes 8388624 | tf_op jit(solution)/shard_map/all_gather | solution.py:264
  460.1 13.0 %multiply_convert_fusion.2 = (bf16[1536,1024]{1,0:T(8,128)(2,1)S(1)}, f32[1536,1024]{1,0:T(8,128)}) fusion(f32[1536,1024]{1,0:T(8,128)} %fusion.50, bf16[1536,2048]{1,0:T(8,128)(2,1)} %copy-done.61, bf16[2048,2048]{1,0:T(8,128)(2,1)} %all-gather.8.cloned.1.call-done), kind=kOutput, calls=%fused_computation.6 | convolution fusion | flops 6451888128 | bytes 26214400 | tf_op jit(solution)/shard_map/dot_general | solution.py:232
  474.7 11.2 %convolution_convert_fusion.3 = bf16[2048,1024]{1,0:T(8,128)(2,1)} fusion(bf16[1536,2048]{1,0:T(8,128)(2,1)} %copy-done.59, bf16[1536,1024]{1,0:T(8,128)(2,1)S(1)} %get-tuple-element.208), kind=kOutput, calls=%fused_computation.17 | convolution fusion | flops 6444548096 | bytes 13631488 | tf_op jit(solution)/shard_map/dot_general | solution.py:236
  486.0 17.8 %multiply_convert_fusion.1 = (bf16[1536,1024]{1,0:T(8,128)(2,1)}, bf16[1536,1024]{1,0:T(8,128)(2,1)S(1)}) fusion(f32[1536,1024]{1,0:T(8,128)} %fusion.50, f32[1536,1024]{1,0:T(8,128)} %get-tuple-element.424, bf16[1536,2048]{1,0:T(8,128)(2,1)} %copy-done.59, bf16[2048,2048]{1,0:T(8,128)(2,1)} %all-gather.8.cloned.1.call-done), kind=kOutput, calls=%fused_computation.5 | convolution fusion | flops 6462898176 | bytes 29360128 | tf_op jit(solution)/shard_map/dot_general | solution.py:232
  503.8 12.5 %fusion.6 = f32[1536,2048]{1,0:T(8,128)} fusion(bf16[1536,1024]{1,0:T(8,128)(2,1)S(1)} %get-tuple-element.203, bf16[2048,2048]{1,0:T(8,128)(2,1)} %all-gather.8.cloned.1.call-done), kind=kOutput, calls=%fused_computation.22 | convolution fusion | flops 6442450944 | bytes 19922944 | tf_op jit(solution)/shard_map/dot_general | solution.py:242
  516.3 10.7 %add_convert_fusion = bf16[1536,2048]{1,0:T(8,128)(2,1)S(1)} fusion(f32[1536,2048]{1,0:T(8,128)} %fusion.6, bf16[1536,1024]{1,0:T(8,128)(2,1)} %get-tuple-element.198, bf16[2048,1024]{1,0:T(8,128)(2,1)S(1)} %copy-done.69), kind=kOutput, calls=%fused_computation.1 | convolution fusion | flops 6448742400 | bytes 26214400 | tf_op jit(solution)/shard_map/dot_general | solution.py:242
  537.5 11.4 %convolution_convert_fusion.2 = bf16[2048,1024]{1,0:T(8,128)(2,1)} fusion(bf16[1536,2048]{1,0:T(8,128)(2,1)} %copy-done.61, bf16[1536,1024]{1,0:T(8,128)(2,1)S(1)} %copy-done.73), kind=kOutput, calls=%fused_computation.16 | convolution fusion | flops 6444548096 | bytes 13631488 | tf_op jit(solution)/shard_map/dot_general | solution.py:236
  557.1 11.2 %convolution_convert_fusion.1 = bf16[2048,1024]{1,0:T(8,128)(2,1)} fusion(bf16[1536,2048]{1,0:T(8,128)(2,1)} %copy-done.61, bf16[1536,1024]{1,0:T(8,128)(2,1)} %copy-done.72), kind=kOutput, calls=%fused_computation.15 | convolution fusion | flops 6444548096 | bytes 13631488 | tf_op jit(solution)/shard_map/dot_general | solution.py:236
  580.3 9.3 %convolution_convert_fusion = bf16[1536,2048]{1,0:T(8,128)(2,1)S(1)} fusion(bf16[1536,1024]{1,0:T(8,128)(2,1)S(1)} %copy-done.75, bf16[2048,2048]{1,0:T(8,128)(2,1)} %all-gather.8.cloned.1.call-done), kind=kOutput, calls=%fused_computation.2 | convolution fusion | flops 6445596672 | bytes 13631488 | tf_op jit(solution)/shard_map/dot_general | solution.py:242
  589.9 7.5 collective-permute-done.36
  616.9 10.1 %attend_back.1 = (f32[768,512]{1,0:T(8,128)S(1)}, bf16[6144,512]{1,0:T(8,128)(2,1)S(1)}) custom-call(s32[8]{0:T(128)S(1)} %copy-done.7, bf16[768,512]{1,0:T(8,128)(2,1)S(1)} %copy-done.5, bf16[6144,512]{1,0:T(8,128)(2,1)} %constant_dynamic-update-slice_fusion.14.refs_2_, bf16[768,512]{1,0:T(8,128)(2,1)S(1)} %fusion.21.refs_3_, ...), custom_call_target="tpu_custom_call" | custom-call | flops 12079595520 | bytes 12582912 | tf_op jit(solution)/shard_map/attend_back/pallas_call | solution.py:487
  668.9 13.5 %collective-permute-start.45 = (bf16[768,512]{1,0:T(8,128)(2,1)}, bf16[768,512]{1,0:T(8,128)(2,1)}, u32[]{:S(2)}, u32[]{:S(2)}) collective-permute-start(bf16[768,512]{1,0:T(8,128)(2,1)} %pad_maximum_fusion.16), channel_id=1, source_target_pairs={{0,8},{8,16},{16,24},{24,28},{28,20},{20,12},{12,4},{4,0},{1,9},{9... | collective-permute-start | bytes 2359304 | tf_op jit(solution)/shard_map/ppermute | solution.py:135
  694.1 12.6 %collective-permute-done.48 = bf16[192,2048]{1,0:T(8,128)(2,1)} collective-permute-done((bf16[192,2048]{1,0:T(8,128)(2,1)}, bf16[192,2048]{1,0:T(8,128)(2,1)}, u32[]{:S(2)}, u32[]{:S(2)}) %collective-permute-start.48) | collective-permute-done | bytes 786464 | tf_op jit(solution)/shard_map/ppermute | solution.py:156
  706.7 23.2 %collective-permute-done.46 = bf16[768,512]{1,0:T(8,128)(2,1)} collective-permute-done((bf16[768,512]{1,0:T(8,128)(2,1)}, bf16[768,512]{1,0:T(8,128)(2,1)}, u32[]{:S(2)}, u32[]{:S(2)}) %collective-permute-start.46) | collective-permute-done | bytes 786464 | tf_op jit(solution)/shard_map/ppermute | solution.py:136
  732.2 8.4 collective-permute-start.50
  745.6 6.4 collective-permute-done.50
  752.0 6.2 collective-permute-done.51
  767.0 30.4 %collective-permute-done.54 = bf16[256,1024]{1,0:T(8,128)(2,1)} collective-permute-done((bf16[256,1024]{1,0:T(8,128)(2,1)S(1)}, bf16[256,1024]{1,0:T(8,128)(2,1)}, u32[]{:S(2)}, u32[]{:S(2)}) %collective-permute-start.54) | collective-permute-done | bytes 524320 | tf_op jit(solution)/shard_map/ppermute | solution.py:156
  839.6 7.8 collective-permute-done.60
  858.4 7.3 collective-permute-done.63
  874.8 6.4 collective-permute-done.67
  (502 shorter events, 334.5 us)
Async XLA Ops:
  7.2 123.3 %all-gather.4.cloned.1.call-start = ((), (), s32[]{:S(2)}) async-start(), calls=%async_computation.4 | async-start | bytes 7077888 | tf_op jit(solution)/shard_map/all_gather | solution.py:548
  12.4 245.3 %all-gather.6.cloned.1.call-start = ((), (), s32[]{:S(2)}) async-start(), calls=%async_computation.5 | async-start | bytes 5242880 | tf_op jit(solution)/shard_map/all_gather | solution.py:264
  16.4 20.3 %collective-permute-start.4 = (bf16[256,1024]{1,0:T(8,128)(2,1)}, bf16[256,1024]{1,0:T(8,128)(2,1)S(1)}, u32[]{:S(2)}, u32[]{:S(2)}) collective-permute-start(bf16[256,1024]{1,0:T(8,128)(2,1)} %get-tuple-element.408), channel_id=1, source_target_pairs={{0,4},{4,0},{8,12},{12,8},{16,20},{20,16},{24,28},{28,24},{1,5},{5... | collective-permute-start | bytes 1572872 | tf_op jit(solution)/shard_map/ppermute | solution.py:156
  16.4 20.2 %collective-permute-start = (bf16[192,2048]{1,0:T(8,128)(2,1)S(1)}, bf16[192,2048]{1,0:T(8,128)(2,1)S(1)}, u32[]{:S(2)}, u32[]{:S(2)}) collective-permute-start(bf16[192,2048]{1,0:T(8,128)(2,1)S(1)} %copy-done.12), channel_id=1, source_target_pairs={{0,2},{1,3},{2,0},{3,1},{4,6},{5,7},{6,4},{7,5},{8,10},{9,11},{10,... | collective-permute-start | bytes 2359304 | tf_op jit(solution)/shard_map/ppermute | solution.py:156
  20.7 33.5 %collective-permute-start.6 = (bf16[256,1024]{1,0:T(8,128)(2,1)}, bf16[256,1024]{1,0:T(8,128)(2,1)}, u32[]{:S(2)}, u32[]{:S(2)}) collective-permute-start(bf16[256,1024]{1,0:T(8,128)(2,1)} %get-tuple-element.405), channel_id=1, source_target_pairs={{0,4},{4,0},{8,12},{12,8},{16,20},{20,16},{24,28},{28,24},{1,5},{5... | collective-permute-start | bytes 1572872 | tf_op jit(solution)/shard_map/ppermute | solution.py:156
  54.2 405.9 %all-gather.8.cloned.1.call-start = ((), (), s32[]{:S(2)}) async-start(), calls=%async_computation.6 | async-start | bytes 10485760 | tf_op jit(solution)/shard_map/all_gather | solution.py:264
  54.3 27.8 %collective-permute-start.8 = (bf16[192,2048]{1,0:T(8,128)(2,1)}, bf16[192,2048]{1,0:T(8,128)(2,1)S(1)}, u32[]{:S(2)}, u32[]{:S(2)}) collective-permute-start(bf16[192,2048]{1,0:T(8,128)(2,1)} %param.25), channel_id=1, source_target_pairs={{0,2},{1,3},{2,0},{3,1},{4,6},{5,7},{6,4},{7,5},{8,10},{9,11},{10,... | collective-permute-start | bytes 2359304 | tf_op jit(solution)/shard_map/ppermute | solution.py:156
  61.3 20.7 %collective-permute-start.7 = (bf16[256,1024]{1,0:T(8,128)(2,1)S(1)}, bf16[256,1024]{1,0:T(8,128)(2,1)}, u32[]{:S(2)}, u32[]{:S(2)}) collective-permute-start(bf16[256,1024]{1,0:T(8,128)(2,1)S(1)} %get-tuple-element.397), channel_id=1, source_target_pairs={{0,4},{4,0},{8,12},{12,8},{16,20},{20,16},{24,28},{28,24},{1,5},{5... | collective-permute-start | bytes 1572872 | tf_op jit(solution)/shard_map/ppermute | solution.py:156
  138.8 55.2 %collective-permute-start.10 = (bf16[768,512]{1,0:T(8,128)(2,1)}, bf16[768,512]{1,0:T(8,128)(2,1)}, u32[]{:S(2)}, u32[]{:S(2)}) collective-permute-start(bf16[768,512]{1,0:T(8,128)(2,1)} %pad_maximum_fusion.12), channel_id=1, source_target_pairs={{8,0},{16,8},{24,16},{28,24},{20,28},{12,20},{4,12},{0,4},{9,1},{1... | collective-permute-start | bytes 2359304 | tf_op jit(solution)/shard_map/ppermute | solution.py:79
  139.3 54.7 %collective-permute-start.9 = (bf16[768,512]{1,0:T(8,128)(2,1)}, bf16[768,512]{1,0:T(8,128)(2,1)}, u32[]{:S(2)}, u32[]{:S(2)}) collective-permute-start(bf16[768,512]{1,0:T(8,128)(2,1)} %pad_maximum_fusion.12), channel_id=1, source_target_pairs={{0,8},{8,16},{16,24},{24,28},{28,20},{20,12},{12,4},{4,0},{1,9},{9... | collective-permute-start | bytes 2359304 | tf_op jit(solution)/shard_map/ppermute | solution.py:78
  194.0 33.8 %collective-permute-start.11 = (bf16[768,512]{1,0:T(8,128)(2,1)}, bf16[768,512]{1,0:T(8,128)(2,1)}, u32[]{:S(2)}, u32[]{:S(2)}) collective-permute-start(bf16[768,512]{1,0:T(8,128)(2,1)} %collective-permute-done.9), channel_id=1, source_target_pairs={{0,8},{8,16},{16,24},{24,28},{28,20},{20,12},{12,4},{4,0},{1,9},{9... | collective-permute-start | bytes 2359304 | tf_op jit(solution)/shard_map/ppermute | solution.py:78
  194.0 48.3 %collective-permute-start.12 = (bf16[768,512]{1,0:T(8,128)(2,1)}, bf16[768,512]{1,0:T(8,128)(2,1)}, u32[]{:S(2)}, u32[]{:S(2)}) collective-permute-start(bf16[768,512]{1,0:T(8,128)(2,1)} %collective-permute-done.10), channel_id=1, source_target_pairs={{8,0},{16,8},{24,16},{28,24},{20,28},{12,20},{4,12},{0,4},{9,1},{1... | collective-permute-start | bytes 2359304 | tf_op jit(solution)/shard_map/ppermute | solution.py:79
  196.0 61.7 %collective-permute-start.15 = (bf16[192,2048]{1,0:T(8,128)(2,1)S(1)}, bf16[192,2048]{1,0:T(8,128)(2,1)}, u32[]{:S(2)}, u32[]{:S(2)}) collective-permute-start(bf16[192,2048]{1,0:T(8,128)(2,1)S(1)} %copy-done.27), channel_id=1, source_target_pairs={{0,4},{4,0},{8,12},{12,8},{16,20},{20,16},{24,28},{28,24},{1,5},{5... | collective-permute-start | bytes 2359304 | tf_op jit(solution)/shard_map/ppermute | solution.py:156
  242.3 20.8 %collective-permute-start.13 = (bf16[768,512]{1,0:T(8,128)(2,1)}, bf16[768,512]{1,0:T(8,128)(2,1)}, u32[]{:S(2)}, u32[]{:S(2)}) collective-permute-start(bf16[768,512]{1,0:T(8,128)(2,1)} %collective-permute-done.11), channel_id=1, source_target_pairs={{0,8},{8,16},{16,24},{24,28},{28,20},{20,12},{12,4},{4,0},{1,9},{9... | collective-permute-start | bytes 2359304 | tf_op jit(solution)/shard_map/ppermute | solution.py:78
  242.9 20.2 %collective-permute-start.14 = (bf16[768,512]{1,0:T(8,128)(2,1)}, bf16[768,512]{1,0:T(8,128)(2,1)}, u32[]{:S(2)}, u32[]{:S(2)}) collective-permute-start(bf16[768,512]{1,0:T(8,128)(2,1)} %collective-permute-done.12), channel_id=1, source_target_pairs={{8,0},{16,8},{24,16},{28,24},{20,28},{12,20},{4,12},{0,4},{9,1},{1... | collective-permute-start | bytes 2359304 | tf_op jit(solution)/shard_map/ppermute | solution.py:79
  246.6 28.6 %collective-permute-start.19 = (bf16[192,1024]{1,0:T(8,128)(2,1)}, bf16[192,1024]{1,0:T(8,128)(2,1)}, u32[]{:S(2)}, u32[]{:S(2)}) collective-permute-start(bf16[192,1024]{1,0:T(8,128)(2,1)} %slice.316), channel_id=1, source_target_pairs={{0,4},{4,0},{8,12},{12,8},{16,20},{20,16},{24,28},{28,24},{1,5},{5... | collective-permute-start | bytes 1179656 | tf_op jit(solution)/shard_map/ppermute | solution.py:156
  296.5 346.6 %reduce-scatter.5.cloned.1.call-start = ((), (), s32[]{:S(2)}) async-start(), calls=%async_computation.7 | async-start | bytes 5242880 | tf_op jit(solution)/shard_map/reduce_scatter | solution.py:268
  329.0 21.6 %collective-permute-start.25 = (bf16[192,2048]{1,0:T(8,128)(2,1)S(1)}, bf16[192,2048]{1,0:T(8,128)(2,1)S(1)}, u32[]{:S(2)}, u32[]{:S(2)}) collective-permute-start(bf16[192,2048]{1,0:T(8,128)(2,1)S(1)} %get-tuple-element.322), channel_id=1, source_target_pairs={{0,4},{4,0},{8,12},{12,8},{16,20},{20,16},{24,28},{28,24},{1,5},{5... | collective-permute-start | bytes 2359304 | tf_op jit(solution)/shard_map/ppermute | solution.py:156
  486.0 202.0 %reduce-scatter.7.cloned.1.call-start = ((), (), s32[]{:S(2)}) async-start(), calls=%async_computation.8 | async-start | bytes 5242880 | tf_op jit(solution)/shard_map/reduce_scatter | solution.py:268
  557.1 208.5 %reduce-scatter.9.cloned.1.call-start = ((), (), s32[]{:S(2)}) async-start(), calls=%async_computation.9 | async-start | bytes 5242880 | tf_op jit(solution)/shard_map/reduce_scatter | solution.py:268
  614.2 225.3 %reduce-scatter.11.cloned.1.call-start = ((), (), s32[]{:S(2)}) async-start(), calls=%async_computation.10 | async-start | bytes 2359296 | tf_op jit(solution)/shard_map/reduce_scatter | solution.py:730
  628.7 22.9 %collective-permute-start.42 = (bf16[192,1024]{1,0:T(8,128)(2,1)}, bf16[192,1024]{1,0:T(8,128)(2,1)}, u32[]{:S(2)}, u32[]{:S(2)}) collective-permute-start(bf16[192,1024]{1,0:T(8,128)(2,1)} %get-tuple-element.410), channel_id=1, source_target_pairs={{0,2},{1,3},{2,0},{3,1},{4,6},{5,7},{6,4},{7,5},{8,10},{9,11},{10,... | collective-permute-start | bytes 1179656 | tf_op jit(solution)/shard_map/ppermute | solution.py:156
  629.3 22.2 %collective-permute-start.43 = (bf16[192,1024]{1,0:T(8,128)(2,1)}, bf16[192,1024]{1,0:T(8,128)(2,1)}, u32[]{:S(2)}, u32[]{:S(2)}) collective-permute-start(bf16[192,1024]{1,0:T(8,128)(2,1)} %get-tuple-element.409), channel_id=1, source_target_pairs={{0,4},{4,0},{8,12},{12,8},{16,20},{20,16},{24,28},{28,24},{1,5},{5... | collective-permute-start | bytes 1179656 | tf_op jit(solution)/shard_map/ppermute | solution.py:156
  636.5 21.9 %collective-permute-start.41 = (bf16[384,512]{1,0:T(8,128)(2,1)}, bf16[384,512]{1,0:T(8,128)(2,1)}, u32[]{:S(2)}, u32[]{:S(2)}) collective-permute-start(bf16[384,512]{1,0:T(8,128)(2,1)} %get-tuple-element.339), channel_id=1, source_target_pairs={{8,0},{16,8},{24,16},{28,24},{20,28},{12,20},{4,12},{0,4},{9,1},{1... | collective-permute-start | bytes 1179656 | tf_op jit(solution)/shard_map/ppermute | solution.py:136
  666.2 63.7 %collective-permute-start.46 = (bf16[768,512]{1,0:T(8,128)(2,1)}, bf16[768,512]{1,0:T(8,128)(2,1)}, u32[]{:S(2)}, u32[]{:S(2)}) collective-permute-start(bf16[768,512]{1,0:T(8,128)(2,1)} %pad_maximum_fusion.17), channel_id=1, source_target_pairs={{8,0},{16,8},{24,16},{28,24},{20,28},{12,20},{4,12},{0,4},{9,1},{1... | collective-permute-start | bytes 2359304 | tf_op jit(solution)/shard_map/ppermute | solution.py:136
  668.9 61.0 %collective-permute-start.45 = (bf16[768,512]{1,0:T(8,128)(2,1)}, bf16[768,512]{1,0:T(8,128)(2,1)}, u32[]{:S(2)}, u32[]{:S(2)}) collective-permute-start(bf16[768,512]{1,0:T(8,128)(2,1)} %pad_maximum_fusion.16), channel_id=1, source_target_pairs={{0,8},{8,16},{16,24},{24,28},{28,20},{20,12},{12,4},{4,0},{1,9},{9... | collective-permute-start | bytes 2359304 | tf_op jit(solution)/shard_map/ppermute | solution.py:135
  685.3 21.4 %collective-permute-start.48 = (bf16[192,2048]{1,0:T(8,128)(2,1)}, bf16[192,2048]{1,0:T(8,128)(2,1)}, u32[]{:S(2)}, u32[]{:S(2)}) collective-permute-start(bf16[192,2048]{1,0:T(8,128)(2,1)} %pad_maximum_fusion.19), channel_id=1, source_target_pairs={{0,4},{4,0},{8,12},{12,8},{16,20},{20,16},{24,28},{28,24},{1,5},{5... | collective-permute-start | bytes 2359304 | tf_op jit(solution)/shard_map/ppermute | solution.py:156
  686.2 20.5 %collective-permute-start.47 = (bf16[192,2048]{1,0:T(8,128)(2,1)}, bf16[192,2048]{1,0:T(8,128)(2,1)}, u32[]{:S(2)}, u32[]{:S(2)}) collective-permute-start(bf16[192,2048]{1,0:T(8,128)(2,1)} %pad_maximum_fusion.18), channel_id=1, source_target_pairs={{0,2},{1,3},{2,0},{3,1},{4,6},{5,7},{6,4},{7,5},{8,10},{9,11},{10,... | collective-permute-start | bytes 2359304 | tf_op jit(solution)/shard_map/ppermute | solution.py:156
  689.2 40.7 %collective-permute-start.49 = (bf16[256,1024]{1,0:T(8,128)(2,1)S(1)}, bf16[256,1024]{1,0:T(8,128)(2,1)S(1)}, u32[]{:S(2)}, u32[]{:S(2)}) collective-permute-start(bf16[256,1024]{1,0:T(8,128)(2,1)S(1)} %get-tuple-element.389), channel_id=1, source_target_pairs={{0,4},{4,0},{8,12},{12,8},{16,20},{20,16},{24,28},{28,24},{1,5},{5... | collective-permute-start | bytes 1572872 | tf_op jit(solution)/shard_map/ppermute | solution.py:156
  760.9 36.6 %collective-permute-start.52 = (bf16[768,512]{1,0:T(8,128)(2,1)}, bf16[768,512]{1,0:T(8,128)(2,1)}, u32[]{:S(2)}, u32[]{:S(2)}) collective-permute-start(bf16[768,512]{1,0:T(8,128)(2,1)} %get-tuple-element.334), channel_id=1, source_target_pairs={{0,8},{8,16},{16,24},{24,28},{28,20},{20,12},{12,4},{4,0},{1,9},{9... | collective-permute-start | bytes 2359304 | tf_op jit(solution)/shard_map/ppermute | solution.py:135
  765.6 31.9 %collective-permute-start.53 = (bf16[768,512]{1,0:T(8,128)(2,1)S(1)}, bf16[768,512]{1,0:T(8,128)(2,1)}, u32[]{:S(2)}, u32[]{:S(2)}) collective-permute-start(bf16[768,512]{1,0:T(8,128)(2,1)S(1)} %get-tuple-element.333), channel_id=1, source_target_pairs={{8,0},{16,8},{24,16},{28,24},{20,28},{12,20},{4,12},{0,4},{9,1},{1... | collective-permute-start | bytes 2359304 | tf_op jit(solution)/shard_map/ppermute | solution.py:136
  766.9 30.6 %collective-permute-start.54 = (bf16[256,1024]{1,0:T(8,128)(2,1)S(1)}, bf16[256,1024]{1,0:T(8,128)(2,1)}, u32[]{:S(2)}, u32[]{:S(2)}) collective-permute-start(bf16[256,1024]{1,0:T(8,128)(2,1)S(1)} %get-tuple-element.385), channel_id=1, source_target_pairs={{0,4},{4,0},{8,12},{12,8},{16,20},{20,16},{24,28},{28,24},{1,5},{5... | collective-permute-start | bytes 1572872 | tf_op jit(solution)/shard_map/ppermute | solution.py:156
  (125 other events, 1873.3 us)
Sparse Core Ops, SparseCore 0:
  12.5 117.9 all-gather.3
  132.7 107.8 all-gather.5
  296.6 163.5 all-gather.7
  486.1 74.9 reduce-scatter.4
  563.4 77.2 reduce-scatter.6
  642.8 102.7 reduce-scatter.8
  767.2 72.3 reduce-scatter.10
